TPU v7x, 512 devices: a whole 4x4x16 slice. The times are simulated.
512 devices in a mesh: band: 32 (over y, x, core), slab: 16 (over z).
Axes of the slice: x: 4, y: 4, z: 16, core: 2. Of those that a mesh axis runs over, the one named last changes fastest.
Arguments:
- response: float32 [32, 2048, 256], P('band', 'slab'), may hold values from -70 to 70, as said below
- previous: float32 [32, 2048, 256], P('band', 'slab'), may hold values from -18 to 18, as said below
- earlier_beta: float32 [1], replicated, may hold values from 0.3 to 1
- band_gap: float32 [32], P('band'), may hold values from 0.5 to 2
- occupied: bfloat16 [32, 2048, 256], P('band', 'slab'), may hold values from -1 to 1, as said below
- occupied_real: bfloat16 [32, 2, 128, 16384], P('band', None, 'slab'), may hold values from -13 to 13, as said below
- xc_kernel: float32 [128, 16384], P('slab'), may hold values from -1.5 to -0.3
- stick_map: int32 [2048], replicated, may hold values from 0 to 16383, as said below
Outputs:
- next_vector: float32 [32, 2048, 256], P('band', 'slab')
- margins: float32 [2, 32, 32], P(None, None, 'band')
- coefficients: float32 [2], replicated
Inputs may be any that keep to these rules, and one draw needn't show every extreme that they name: response stays within the range. previous stays within the range. occupied stays within the range. occupied_real stays within the range. `stick_map`: distinct grid columns, those of the 2048 smallest in-plane frequencies (the sphere's cross-section, ties broken arbitrarily), in an arbitrary order.
All inputs are finite; a program needn't handle non-finite values.
Results may differ from a plain program's by a relative error of at most 0.00075.
Values may be sent and summed in bfloat16 or wider, within the bound.
No kernel may reach another device: no remote copies, remote signals or barrier semaphores. Data moves between devices by JAX's collectives and lax.ppermute only.
A program may use at most 64 MiB of HBM per device.

v0:
```python
import math

import jax
import jax.numpy as jnp
from jax import lax
from jax.sharding import PartitionSpec as P

PRECISE = lax.Precision.HIGHEST


def phase_table(points, sign_value):
    indices = jnp.arange(points, dtype=jnp.int32)
    products = indices[:, None] * indices[None, :] % points
    angles = products.astype(jnp.float32) * (2.0 * math.pi / points)
    cosine = jnp.cos(angles)
    sine_part = sign_value * jnp.sin(angles)
    return jnp.stack([jnp.stack([cosine, sine_part]), jnp.stack([-sine_part, cosine])])


def signed_freq(indices, points):
    return jnp.where(indices < points // 2, indices, indices - points).astype(jnp.float32)


def plane_transform(plane_grid, phases):
    plane_grid = jnp.einsum("bcpxy,cdyk->bdpxk", plane_grid, phases, precision=PRECISE)
    return jnp.einsum("bcpxy,cdxk->bdpky", plane_grid, phases, precision=PRECISE)


def plane_back(spectrum, inverse):
    halfway = jnp.einsum("cpxy,cdyk->dpxk", spectrum, inverse, precision=PRECISE)
    return jnp.einsum("cpxy,cxk->pky", halfway, inverse[:, 0], precision=PRECISE)


def per_device(
    response, previous, earlier_beta, band_gap, occupied, occupied_real, xc_kernel, stick_map
):
    bands, sticks_dev, row_width = response.shape
    grid_size = row_width // 2
    planes = occupied_real.shape[2]
    norm_root = float(grid_size) ** 1.5
    inverse = phase_table(grid_size, 1.0)
    forward = phase_table(grid_size, -1.0)
    coefficient = response.reshape(bands, sticks_dev, 2, grid_size)
    stick_field = jnp.einsum("bscg,cdgz->bdzs", coefficient, inverse, precision=PRECISE)
    exchanged = lax.all_to_all(stick_field, "slab", split_axis=2, concat_axis=3, tiled=True)
    plane_grid = (
        jnp.zeros((bands, 2, planes, grid_size * grid_size), jnp.float32)
        .at[:, :, :, stick_map]
        .set(exchanged)
    )
    field_values = plane_transform(
        plane_grid.reshape(bands, 2, planes, grid_size, grid_size), inverse
    )
    field_values = field_values.reshape(bands, 2, planes, grid_size * grid_size) / norm_root
    partial_sum = 2.0 * jnp.sum(occupied_real * field_values, axis=(0, 1))
    all_freq = signed_freq(jnp.arange(grid_size, dtype=jnp.int32), grid_size)
    density = lax.psum(partial_sum, "band")
    density_grid = density.reshape(planes, grid_size, grid_size)
    spectrum = jnp.einsum("pxy,dyk->dpxk", density_grid, forward[0], precision=PRECISE)
    spectrum = jnp.einsum("cpxy,cdxk->dpky", spectrum, forward, precision=PRECISE)
    columns = lax.all_to_all(spectrum, "slab", split_axis=2, concat_axis=1, tiled=True)
    columns = jnp.einsum("czxy,cdzk->dkxy", columns, forward, precision=PRECISE)
    x_rows = columns.shape[2]
    x_freq = signed_freq(
        lax.axis_index("slab") * x_rows + jnp.arange(x_rows, dtype=jnp.int32), grid_size
    )
    wave_sq = (
        all_freq[:, None, None] ** 2 + x_freq[None, :, None] ** 2 + all_freq[None, None, :] ** 2
    )
    kernel = jnp.where(
        wave_sq > 0.0, (0.2 * grid_size) ** 2 / (math.pi * jnp.maximum(wave_sq, 1.0)), 0.0
    )
    kernel = kernel / float(grid_size) ** 3
    columns = jnp.einsum("czxy,cdzk->dkxy", columns * kernel, inverse, precision=PRECISE)
    returned_planes = lax.all_to_all(columns, "slab", split_axis=1, concat_axis=2, tiled=True)
    hartree = plane_back(returned_planes, inverse).reshape(planes, grid_size * grid_size)
    potential = hartree + xc_kernel * density
    product = (potential * occupied_real).reshape(bands, 2, planes, grid_size, grid_size)
    transformed = plane_transform(product, forward).reshape(bands, 2, planes, grid_size * grid_size)
    chosen = jnp.take(transformed, stick_map, axis=3)
    gathered = lax.all_to_all(chosen, "slab", split_axis=3, concat_axis=2, tiled=True)
    applied = jnp.einsum("bczs,cdzk->bsdk", gathered, forward, precision=PRECISE)
    applied = applied.reshape(bands, sticks_dev, row_width) / norm_root
    flat_size = sticks_dev * row_width
    total_bands = occupied.shape[0] * lax.axis_size("band")
    rotated = jnp.concatenate([applied[:, :, grid_size:], -applied[:, :, :grid_size]], axis=2)
    probes = (
        jnp.concatenate([applied, rotated], axis=0)
        .astype(jnp.bfloat16)
        .reshape(2 * bands, flat_size)
    )
    block_rows = lax.all_gather(occupied, "band", axis=0, tiled=True)
    row_block = lax.dot_general(
        block_rows.reshape(block_rows.shape[0], flat_size),
        probes,
        (((1,), (1,)), ((), ())),
        preferred_element_type=jnp.float32,
    )
    margin_all = lax.psum(row_block, "slab")
    weights = margin_all.astype(jnp.bfloat16)
    block_rows = lax.all_gather(occupied, "band", axis=0, tiled=True)
    correction = lax.dot_general(
        weights,
        block_rows.reshape(block_rows.shape[0], flat_size),
        (((0,), (0,)), ((), ())),
        preferred_element_type=jnp.float32,
    )
    halves = correction.reshape(2, bands, sticks_dev, 2, grid_size)
    turned = jnp.stack([-halves[1, :, :, 1], halves[1, :, :, 0]], axis=2)
    removed = (halves[0] + turned).reshape(bands, sticks_dev, row_width)
    margins = margin_all.reshape(total_bands, 2, bands).transpose(1, 0, 2)
    pushed = band_gap[:, None, None] * response + applied - removed
    beta_old = earlier_beta[0]
    entries = float(response.size * lax.axis_size("band") * lax.axis_size("slab"))
    q_norm = jnp.sum(response * response)
    q_push = jnp.sum(response * pushed)
    q_norm_all, q_push_all = lax.psum((q_norm, q_push), ("band", "slab"))
    alpha_coef = q_push_all / q_norm_all
    residual = pushed - alpha_coef * response - beta_old * previous
    resid_sq = lax.psum(jnp.sum(residual * residual), ("band", "slab"))
    beta_coef = jnp.sqrt(resid_sq / entries + 1e-06)
    next_vector = residual / beta_coef
    return (next_vector, margins, jnp.stack([alpha_coef, beta_coef]))


def solution(mesh):
    placed = (
        P("band", "slab", None),
        P("band", "slab", None),
        P(),
        P("band"),
        P("band", "slab", None),
        P("band", None, "slab", None),
        P("slab", None),
        P(),
    )
    return jax.shard_map(
        per_device,
        mesh=mesh,
        in_specs=placed,
        out_specs=(P("band", "slab", None), P(None, None, "band"), P()),
        check_vma=False,
    )
```

profile of v0, /device:TPU:1, one launch (start us, length us, event | category | flops | bytes accessed | tf_op | source)
XLA Modules:
  0.0 834.6 jit_solution(16772197007140116305)
XLA Ops:
  10.2 15.7 %all-to-all-start = ((f32[1,2,128,128]{3,1,0,2:T(2,128)}), f32[1,2,128,128]{3,1,0,2:T(2,128)S(1)}, u32[]{:S(2)}, u32[]{:S(2)}) async-start(f32[1,2,128,128]{3,1,0,2:T(2,128)} %copy.76), calls=%async_computation | async-start | bytes 262144 | tf_op jit(solution)/shard_map/all_to_all | solution.py:45
  26.0 11.9 %all-to-all-done = f32[1,2,128,128]{3,1,0,2:T(2,128)S(1)} async-done(((f32[1,2,128,128]{3,1,0,2:T(2,128)}), f32[1,2,128,128]{3,1,0,2:T(2,128)S(1)}, u32[]{:S(2)}, u32[]{:S(2)}) %all-to-all-start) | async-done | bytes 131104 | tf_op jit(solution)/shard_map/all_to_all | solution.py:45
  38.9 6.0 broadcast.316
  44.9 186.8 %scatter_fusion = f32[2,8,16384]{1,0,2:T(2,128)} fusion(f32[2,8,16384]{1,0,2:T(2,128)} %broadcast.316, s32[2048]{0:T(1024)S(1)} %get-tuple-element.30, f32[2048,2,8]{2,1,0:T(2,128)S(1)} %bitcast.230), kind=kCustom, calls=%fused_computation.1 | custom fusion | bytes 401408 | tf_op jit(solution)/shard_map/scatter | solution.py:49
  231.7 13.1 %copy.78 = f32[2,8,128,128]{3,2,0,1:T(8,128)S(1)} copy(f32[2,8,128,128]{1,0,3,2:T(2,128)} %bitcast.223) | data formatting | bytes 2097152 | tf_op jit(solution)/shard_map/reshape.5
  244.9 1.1 convolution_bitcast_fusion.8
  245.9 1.0 fusion.6
  248.2 130.4 %all-reduce.3.cloned.1.call-done = f32[8,16384]{1,0:T(8,128)} async-done(((f32[8,16384]{1,0:T(8,128)}), f32[8,16384]{1,0:T(8,128)}) %all-reduce.3.cloned.1.call-update) | async-done | bytes 524304 | tf_op jit(solution)/shard_map/psum | solution.py:57
  378.6 2.1 convolution_bitcast_fusion.7
  380.6 1.0 convolution_bitcast_fusion.6
  381.7 1.6 copy.82
  383.3 12.0 %all-to-all-start.1 = ((f32[2,8,128,128]{3,1,0,2:T(8,128)}), f32[2,8,128,128]{3,1,0,2:T(8,128)S(1)}, u32[]{:S(2)}, u32[]{:S(2)}) async-start(f32[2,8,128,128]{3,1,0,2:T(8,128)} %copy.82), calls=%async_computation.1 | async-start | bytes 2097152 | tf_op jit(solution)/shard_map/all_to_all | solution.py:61
  395.6 44.2 %all-to-all-done.1 = f32[2,8,128,128]{3,1,0,2:T(8,128)S(1)} async-done(((f32[2,8,128,128]{3,1,0,2:T(8,128)}), f32[2,8,128,128]{3,1,0,2:T(8,128)S(1)}, u32[]{:S(2)}, u32[]{:S(2)}) %all-to-all-start.1) | async-done | bytes 1048608 | tf_op jit(solution)/shard_map/all_to_all | solution.py:61
  440.2 1.2 fusion.4
  442.4 1.6 copy.87
  444.0 13.5 %all-to-all-start.2 = ((f32[2,128,8,128]{3,2,0,1:T(8,128)}), f32[2,128,8,128]{3,2,0,1:T(8,128)S(1)}, u32[]{:S(2)}, u32[]{:S(2)}) async-start(f32[2,128,8,128]{3,2,0,1:T(8,128)} %copy.87), calls=%async_computation.2 | async-start | bytes 2097152 | tf_op jit(solution)/shard_map/all_to_all | solution.py:75
  458.3 44.5 %all-to-all-done.2 = f32[2,128,8,128]{3,2,0,1:T(8,128)S(1)} async-done(((f32[2,128,8,128]{3,2,0,1:T(8,128)}), f32[2,128,8,128]{3,2,0,1:T(8,128)S(1)}, u32[]{:S(2)}, u32[]{:S(2)}) %all-to-all-start.2) | async-done | bytes 1048608 | tf_op jit(solution)/shard_map/all_to_all | solution.py:75
  503.8 1.2 convolution_bitcast_fusion.9
  505.4 1.1 convolution_bitcast_fusion.2
  507.6 11.2 %copy.145 = f32[1,2,8,128,128]{2,1,4,3,0:T(2,128)} copy(f32[1,2,8,128,128]{4,3,2,1,0:T(8,128)S(1)} %convolution_bitcast_fusion.1) | data formatting | bytes 2097152 | tf_op jit(solution)/shard_map/reshape | solution.py:79
  518.9 20.1 %gather_fusion = f32[2048,2,8]{2,1,0:T(2,128)} fusion(f32[2,8,16384]{1,0,2:T(2,128)} %bitcast.224, s32[2048]{0:T(1024)S(1)} %get-tuple-element.29), kind=kCustom, calls=%fused_computation | custom fusion | bytes 270336 | tf_op jit(solution)/shard_map/jit(_take)/gather | solution.py:80
  539.0 10.0 %fusion.74 = f32[2048,1,2,8]{3,2,1,0:T(2,128)S(1)} fusion(f32[2048,2,8]{2,1,0:T(2,128)} %gather_fusion, pred[2048]{0:T(1024)(128)(4,1)S(1)} %compare_and_fusion), kind=kLoop, calls=%fused_computation.124 | loop fusion | flops 32768 | bytes 264192
  549.0 4.0 reshape.387
  553.0 12.8 %all-to-all-start.3 = ((f32[16,1,2048]{2,1,0:T(1,128)}), f32[16,1,2048]{2,1,0:T(1,128)S(1)}, u32[]{:S(2)}, u32[]{:S(2)}) async-start(f32[16,1,2048]{2,1,0:T(1,128)} %reshape.387), calls=%async_computation.3 | async-start | bytes 262144 | tf_op jit(solution)/shard_map/all_to_all | solution.py:81
  567.1 2.8 copy.150
  569.9 7.9 all-to-all-done.3
  579.3 4.5 reshape.388
  583.8 2.6 copy.98
  586.9 3.1 fusion.9
  590.0 22.7 %psum.36 = f32[32,2]{0,1:T(2,128)S(1)} all-reduce(f32[32,2]{0,1:T(2,128)S(1)} %fusion.9), channel_id=1, replica_groups=mesh['band'=32,'slab'=16] {'slab'}, use_global_device_ids=true, to_apply=%region_3.4 | all-reduce | flops 64 | bytes 512 | tf_op jit(solution)/shard_map/psum | solution.py:99
  615.0 109.3 %all-reduce = (f32[]{:T(128)}, f32[]{:T(128)}) all-reduce(f32[]{:T(128)} %get-tuple-element.16, f32[]{:T(128)} %get-tuple-element.15), channel_id=1, replica_groups=mesh['band'=32,'slab'=16] {'band','slab'}, use_global_device_ids=true, to_apply=%region_5.6 | all-reduce | flops 2 | bytes 16 | tf_op jit(solution)/shard_map/psum | solution.py:117
  726.2 99.6 %psum.39 = f32[]{:T(128)} all-reduce(f32[]{:T(128)} %get-tuple-element.19), channel_id=1, replica_groups=mesh['band'=32,'slab'=16] {'band','slab'}, use_global_device_ids=true, to_apply=%region_9.10 | all-reduce | flops 1 | bytes 8 | tf_op jit(solution)/shard_map/psum | solution.py:120
  (61 shorter events, 16.1 us)
Async XLA Ops:
  7.2 18.8 %copy-start.5 = (s32[2048]{0:T(1024)S(1)}, s32[2048]{0:T(1024)}, u32[]{:S(2)}) copy-start(s32[2048]{0:T(1024)} %param.15) | copy-start | bytes 24580
  10.2 27.8 %all-to-all-start = ((f32[1,2,128,128]{3,1,0,2:T(2,128)}), f32[1,2,128,128]{3,1,0,2:T(2,128)S(1)}, u32[]{:S(2)}, u32[]{:S(2)}) async-start(f32[1,2,128,128]{3,1,0,2:T(2,128)} %copy.76), calls=%async_computation | async-start | bytes 262144 | tf_op jit(solution)/shard_map/all_to_all | solution.py:45
  25.9 352.7 %all-reduce.3.cloned.1.call-start = ((), (), s32[]{:S(2)}) async-start(), calls=%async_computation.4 | async-start | bytes 1048576 | tf_op jit(solution)/shard_map/psum | solution.py:57
  245.9 1.3 copy-start.1
  383.3 56.6 %all-to-all-start.1 = ((f32[2,8,128,128]{3,1,0,2:T(8,128)}), f32[2,8,128,128]{3,1,0,2:T(8,128)S(1)}, u32[]{:S(2)}, u32[]{:S(2)}) async-start(f32[2,8,128,128]{3,1,0,2:T(8,128)} %copy.82), calls=%async_computation.1 | async-start | bytes 2097152 | tf_op jit(solution)/shard_map/all_to_all | solution.py:61
  444.0 58.7 %all-to-all-start.2 = ((f32[2,128,8,128]{3,2,0,1:T(8,128)}), f32[2,128,8,128]{3,2,0,1:T(8,128)S(1)}, u32[]{:S(2)}, u32[]{:S(2)}) async-start(f32[2,128,8,128]{3,2,0,1:T(8,128)} %copy.87), calls=%async_computation.2 | async-start | bytes 2097152 | tf_op jit(solution)/shard_map/all_to_all | solution.py:75
  457.5 109.6 %all-gather.2.cloned.1.call-start = ((), (), s32[]{:S(2)}) async-start(), calls=%async_computation.5 | async-start | bytes 2162688 | tf_op jit(solution)/shard_map/all_gather | solution.py:92
  502.7 2.3 copy-start
  502.7 2.3 copy-start.3
  553.0 24.8 %all-to-all-start.3 = ((f32[16,1,2048]{2,1,0:T(1,128)}), f32[16,1,2048]{2,1,0:T(1,128)S(1)}, u32[]{:S(2)}, u32[]{:S(2)}) async-start(f32[16,1,2048]{2,1,0:T(1,128)} %reshape.387), calls=%async_computation.3 | async-start | bytes 262144 | tf_op jit(solution)/shard_map/all_to_all | solution.py:81
  612.7 1.5 copy-start.6
  612.8 1.5 copy-start.2
  612.8 112.8 %copy-start.4 = (f32[1,128,256]{2,1,0:T(8,128)S(1)}, f32[1,128,256]{2,1,0:T(8,128)}, u32[]{:S(2)}) copy-start(f32[1,128,256]{2,1,0:T(8,128)} %param.9) | copy-start | bytes 393220
Sparse Core Ops, SparseCore 0:
  248.3 130.2 all-reduce.2
  461.9 59.3 all-gather.1
where the time goes:
time: 838 us; the launch traced here: 835 us
  local copies, waits for them, and re-layouts  259 us (31%)
  waiting for transfers between devices  240 us (29%)
  blocking collectives  232 us (28%)
  starting transfers between devices  54.1 us (6%)
  between operations  17.7 us (2%)
  other arithmetic  16.2 us (2%)
  matrix products  16.1 us (2%)
    scatter x1, local copies, waits for them, and re-layouts, per_device(): plane_grid = jnp.zeros((bands, 2, planes, grid_size * grid_size), jnp.flo...  187 us
    psum x1, waiting for transfers between devices, per_device(): density = lax.psum(partial_sum, 'band')  130 us
    psum x1, blocking collectives, per_device(): q_norm_all, q_push_all = lax.psum((q_norm, q_push), ('band', 'slab'))  109 us
    psum x1, blocking collectives, per_device(): resid_sq = lax.psum(jnp.sum(residual * residual), ('band', 'slab'))  99.6 us
    all_to_all x1, waiting for transfers between devices, per_device(): lax.all_to_all(columns, 'slab', split_axis=1, concat_axis=2, tiled=True)  44.5 us
    all_to_all x1, waiting for transfers between devices, per_device(): lax.all_to_all(spectrum, 'slab', split_axis=2, concat_axis=1, tiled=True)  44.2 us
    psum x1, blocking collectives, per_device(): margin_all = lax.psum(row_block, 'slab')  22.7 us
    gather x1, local copies, waits for them, and re-layouts, per_device(): chosen = jnp.take(transformed, stick_map, axis=3)  20.1 us
  transfers between devices with their start and end apart: 6, of which 5 were waited for; matrix products, arithmetic and copies ran while one was open for 6% of the time, Pallas kernels for 0%

commit v1 on v0

v1 whole, which is shorter than its diff:
```python
import math

import jax
import jax.numpy as jnp
import ml_dtypes
import numpy as np
from jax import lax
from jax.experimental import pallas as pl
from jax.experimental.pallas import tpu as pltpu
from jax.sharding import PartitionSpec as P

F32 = jnp.float32
BF16 = jnp.bfloat16
VMEM_LIMIT = 48 * 1024 * 1024

N = 128
SLABS = 16
PL = N // SLABS
BANDS = 32
AX = N // BANDS
STK = 128
STICKS = SLABS * STK
HALF = 64
NORM = float(N) ** -1.5


def pieces(table):
    high = table.astype(np.float32).astype(ml_dtypes.bfloat16)
    low = (table - high.astype(np.float64)).astype(np.float32).astype(ml_dtypes.bfloat16)
    return np.stack([high, low])


def angle(a, b):
    return 2.0 * np.pi * ((np.asarray(a)[:, None] * np.asarray(b)[None, :]) % N) / N


def tables():
    every = np.arange(N)
    short = np.arange(HALF)
    signed = np.where(short < HALF // 2, short, short - HALF)
    signed_x = signed.reshape(16, 4).T.reshape(-1)

    c, s = np.cos(angle(every, every)), np.sin(angle(every, every))
    by_slab = lambda m: m.reshape(SLABS, 1, PL, -1)
    z_inverse = np.concatenate(
        [
            np.concatenate([by_slab(c), by_slab(-s)], axis=3),
            np.concatenate([by_slab(s), by_slab(c)], axis=3),
        ],
        axis=1,
    ).reshape(2 * N, 2 * N)
    z_forward = np.concatenate(
        [
            np.concatenate([by_slab(c), by_slab(-s)], axis=3),
            np.concatenate([by_slab(s), by_slab(c)], axis=3),
        ],
        axis=1,
    ).reshape(2 * N, 2 * N)

    cy, sy = np.cos(angle(signed, every)), np.sin(angle(signed, every))
    y_inverse = np.zeros((4, HALF, 4, 2, N))
    for j in range(4):
        y_inverse[j, :, j, 0] = cy
        y_inverse[j, :, j, 1] = sy
    y_inverse = y_inverse.reshape(4 * HALF, 4 * 2 * N)
    y_forward = np.zeros((4, 2, N, 2, 4, HALF))
    for j in range(4):
        y_forward[j, 0, :, 0, j] = cy.T
        y_forward[j, 1, :, 0, j] = sy.T
        y_forward[j, 1, :, 1, j] = cy.T
        y_forward[j, 0, :, 1, j] = -sy.T
    y_forward = y_forward.reshape(4 * 2 * N, 2 * 4 * HALF)

    cx, sx = np.cos(angle(every, signed_x)), np.sin(angle(every, signed_x))
    x_inverse = 2.0 * NORM * np.block([[cx, -sx], [sx, cx]])
    x_forward = NORM * np.concatenate([cx.T, sx.T], axis=0)

    modes = np.zeros((N, N))
    modes[0] = 1.0 / math.sqrt(N)
    modes[1:64] = math.sqrt(2.0 / N) * np.cos(angle(np.arange(1, 64), every))
    modes[64] = np.cos(np.pi * every) / math.sqrt(N)
    modes[65:] = math.sqrt(2.0 / N) * np.sin(angle(np.arange(1, 64), every))
    return {
        "z_inverse": pieces(z_inverse),
        "z_forward": pieces(z_forward),
        "y_inverse": pieces(y_inverse),
        "y_forward": pieces(y_forward),
        "x_inverse": pieces(x_inverse),
        "x_forward": pieces(x_forward),
        "modes": pieces(modes),
        "modes_t": pieces(modes.T),
        "modes_t32": modes.T.astype(np.float32),
    }


TABLES = tables()


def split(value):
    high = value.astype(BF16)
    return high, (value - high.astype(F32)).astype(BF16)


def dot(a, b, contract=((1,), (0,))):
    return lax.dot_general(a, b, (contract, ((), ())), preferred_element_type=F32)


def dot3(a, b, contract=((1,), (0,))):
    return dot(a[0], b[0], contract) + (dot(a[1], b[0], contract) + dot(a[0], b[1], contract))


def call(body, out, *args, scratch=(), in_smem=()):
    specs = [
        pl.BlockSpec(memory_space=pltpu.SMEM if i in in_smem else pltpu.VMEM)
        for i in range(len(args))
    ]
    many = isinstance(out, (list, tuple))
    out_specs = [pl.BlockSpec(memory_space=pltpu.VMEM)] * len(out) if many else pl.BlockSpec(memory_space=pltpu.VMEM)
    return pl.pallas_call(
        body,
        out_shape=out,
        in_specs=specs,
        out_specs=out_specs,
        scratch_shapes=list(scratch),
        compiler_params=pltpu.CompilerParams(vmem_limit_bytes=VMEM_LIMIT),
    )(*args)


def shape(*dims, dtype=F32):
    return jax.ShapeDtypeStruct(dims, dtype)


def sticks_to_z(resp, table, out):
    out[...] = dot3((table[0], table[1]), split(resp[...]), ((1,), (1,))).reshape(SLABS, 2 * PL, STK)


def planes_to_modes(
    recv, q_mask, place, y_table, x_table, occ, modes, modes_t, out, r_high, r_low, d_high, d_low
):
    grid = jnp.zeros((256, 256), F32)
    for src in range(SLABS):
        lanes = slice(src * STK, (src + 1) * STK)
        high, low = split(recv[src])
        mask = q_mask[:, lanes]
        rows = [
            (part.astype(F32)[:, None, :] * mask[None]).reshape(256, STK).astype(BF16)
            for part in (high, low)
        ]
        chosen = place[lanes, :]
        grid += dot(jnp.concatenate(rows, axis=1), jnp.concatenate([chosen, chosen], axis=0))
    grid = split(grid)
    for j in range(4):
        cols = slice(j * 2 * N, (j + 1) * 2 * N)
        mixed = dot3(grid, (y_table[0, :, cols], y_table[1, :, cols]))
        real = mixed[:N, :N] - mixed[N:, N:]
        imag = mixed[:N, N:] + mixed[N:, :N]
        for c, part in enumerate((real, imag)):
            high, low = split(part)
            at = slice(c * HALF + j * 16, c * HALF + (j + 1) * 16)
            for p in range(PL):
                r_high[at, p * N : (p + 1) * N] = high[p * 16 : (p + 1) * 16]
                r_low[at, p * N : (p + 1) * N] = low[p * 16 : (p + 1) * 16]
    for p in range(PL):
        lanes = slice(p * N, (p + 1) * N)
        field = dot3((x_table[0], x_table[1]), (r_high[:, lanes], r_low[:, lanes]))
        density = occ[0, p].astype(F32) * field[:N] + occ[1, p].astype(F32) * field[N:]
        half = dot3(split(density), (modes_t[0], modes_t[1]))
        d_high[:, lanes], d_low[:, lanes] = split(half)
    for p in range(PL):
        lanes = slice(p * N, (p + 1) * N)
        out[pl.ds(p, N, stride=PL), :] = dot3(
            (modes[0], modes[1]), (d_high[:, lanes], d_low[:, lanes])
        )


def sum_bands(recv, to_slabs, to_bands):
    total = recv[0]
    for b in range(1, BANDS):
        total = total + recv[b]
    for i in range(SLABS):
        to_slabs[i] = total
    for i in range(BANDS):
        to_bands[i] = total


def solve_z(where, recv, modes, modes_t32, out):
    columns = [
        jnp.concatenate([recv[i, a * PL : (a + 1) * PL, :] for i in range(SLABS)], axis=0)
        for a in range(AX)
    ]
    spectrum = dot3((modes[0], modes[1]), split(jnp.concatenate(columns, axis=1)))
    freq = lambda i: jnp.where(i <= N // 2, i, i - N // 2)
    fz = freq(lax.broadcasted_iota(jnp.int32, (N, N), 0))
    fy = freq(lax.broadcasted_iota(jnp.int32, (N, N), 1))
    plane_sq = fz * fz + fy * fy
    weighted = []
    for a in range(AX):
        fx = freq(where[0] * AX + a)
        square = (plane_sq + fx * fx).astype(F32)
        kernel = jnp.where(
            square > 0.0, (0.2 * N) ** 2 / (math.pi * jnp.maximum(square, 1.0)), 0.0
        )
        weighted.append(spectrum[:, a * N : (a + 1) * N] * kernel)
    own = modes_t32[pl.ds(pl.multiple_of(where[1] * PL, PL), PL), :]
    result = dot3(split(own), split(jnp.concatenate(weighted, axis=1)))
    tile = jnp.concatenate([result[:, a * N : (a + 1) * N] for a in range(AX)], axis=0)
    for i in range(BANDS):
        out[i] = tile


def from_modes(recv, modes, modes_t, p):
    spectrum = recv[pl.ds(p, N, stride=PL), :]
    half = dot3((modes_t[0], modes_t[1]), split(spectrum))
    return dot3(split(half), (modes[0], modes[1]))


def density_part(recv, modes, modes_t, xc, out):
    for p in range(PL):
        out[p] = xc[p] * from_modes(recv, modes, modes_t, p)


def planes_to_sticks(
    recv, xc_part, occ, q_mask, pick, modes, modes_t, x_table, y_table, out, l_high, l_low, grid
):
    for p in range(PL):
        potential = from_modes(recv, modes, modes_t, p) + xc_part[p]
        product = jnp.concatenate(
            [potential * occ[0, p].astype(F32), potential * occ[1, p].astype(F32)], axis=1
        )
        mixed = dot3((x_table[0], x_table[1]), split(product))
        real = mixed[:HALF, :N] + mixed[HALF:, N:]
        imag = mixed[:HALF, N:] - mixed[HALF:, :N]
        for c, part in enumerate((real, imag)):
            high, low = split(part)
            for j in range(4):
                at = slice(j * 2 * N + c * N, j * 2 * N + (c + 1) * N)
                l_high[p * 16 : (p + 1) * 16, at] = high[j * 16 : (j + 1) * 16]
                l_low[p * 16 : (p + 1) * 16, at] = low[j * 16 : (j + 1) * 16]
    spectrum = dot3((l_high[...], l_low[...]), (y_table[0], y_table[1]))
    for part in range(2):
        for h in range(2):
            lanes = slice(part * 2 * N + h * N, part * 2 * N + (h + 1) * N)
            grid[h, part * N : (part + 1) * N, :] = spectrum[:, lanes]
    high, low = split(
        jnp.concatenate(
            [
                jnp.concatenate([grid[h, pl.ds(q, 16, stride=16), :] for h in range(2)], axis=1)
                for q in range(16)
            ],
            axis=0,
        )
    )
    for dst in range(SLABS):
        lanes = slice(dst * STK, (dst + 1) * STK)
        chosen = dot(high, pick[:, lanes]) + dot(low, pick[:, lanes])
        total = chosen[:16] * q_mask[0:1, lanes]
        for q in range(1, 16):
            total = total + chosen[q * 16 : (q + 1) * 16] * q_mask[q : q + 1, lanes]
        out[dst] = total


def apply_and_overlap(recv, table, occ_all, applied_out, part_out, sums):
    values = recv[...].reshape(2 * N, STK).T
    applied = dot3(split(values), (table[0], table[1]))
    applied_out[...] = applied
    rounded = applied.astype(BF16).astype(F32)
    turned = jnp.concatenate([rounded[:, N:], -rounded[:, :N]], axis=1)
    for w in range(BANDS):
        orbital = occ_all[w].astype(F32)
        for c, probe in enumerate((rounded, turned)):
            line = jnp.sum(orbital * probe, axis=0, keepdims=True)
            sums[c * BANDS + w : c * BANDS + w + 1, :] = line[:, :N] + line[:, N:]
    sums[2 * BANDS :, :] = jnp.zeros((N - 2 * BANDS, N), F32)
    row = jnp.sum(sums[...].T, axis=0, keepdims=True)
    for i in range(SLABS):
        part_out[i] = row


def total_sum(value):
    return jnp.sum(jnp.sum(value, axis=0, keepdims=True), axis=1, keepdims=True)


def lanes_of(values):
    lane = lax.broadcasted_iota(jnp.int32, (1, N), 1)
    row = jnp.zeros((1, N), F32)
    for i, value in enumerate(values):
        row = jnp.where(lane == i, value, row)
    return row


def push(recv, scalars, resp, prev, applied, occ_all, rest_out, margin_out, part_out):
    margin = recv[0]
    for i in range(1, SLABS):
        margin = margin + recv[i]
    margin_out[...] = margin
    weights = margin.astype(BF16).astype(F32)
    plain = jnp.zeros((STK, 2 * N), F32)
    turned = jnp.zeros((STK, 2 * N), F32)
    for w in range(BANDS):
        orbital = occ_all[w].astype(F32)
        plain = plain + weights[:, w : w + 1] * orbital
        turned = turned + weights[:, BANDS + w : BANDS + w + 1] * orbital
    removed = plain + jnp.concatenate([-turned[:, N:], turned[:, :N]], axis=1)
    response = resp[...]
    pushed = scalars[0] * response + applied[...] - removed
    rest = pushed - scalars[1] * prev[...]
    rest_out[...] = rest
    norm = total_sum(response * response)
    along = total_sum(response * pushed)
    slope = total_sum(response * rest) / jnp.where(norm > 0.0, norm, 1.0)
    left = rest - slope * response
    row = lanes_of([norm, along, slope, total_sum(left * left)])
    for i in range(SLABS):
        part_out[i] = row


def merge(recv, count):
    rows = jnp.concatenate([recv[i] for i in range(count)], axis=0)
    norms, alongs, slopes, least = (rows[:, i : i + 1] for i in range(4))
    add = lambda v: jnp.sum(v, axis=0, keepdims=True)
    norm = add(norms)
    slope = add(norms * slopes) / jnp.where(norm > 0.0, norm, 1.0)
    spread = slopes - slope
    return norm, add(alongs), slope, add(least + norms * spread * spread)


def merge_slabs(recv, part_out):
    row = lanes_of(merge(recv, SLABS))
    for i in range(BANDS):
        part_out[i] = row


def finish(recv, resp, rest, next_out, coef_out):
    norm, along, slope, least = merge(recv, BANDS)
    alpha = along / norm
    gap = slope - alpha
    resid_sq = least + norm * gap * gap
    beta = jnp.sqrt(resid_sq / float(2 * BANDS * STICKS * N) + 1e-06)
    next_out[...] = (rest[...] - alpha * resp[...]) / beta
    coef_out[...] = lanes_of([alpha, beta])


def swap(value, axis):
    return lax.all_to_all(value, axis, 0, 0, tiled=True)


def per_device(
    response, previous, earlier_beta, band_gap, occupied, occupied_real, xc_kernel, stick_map
):
    t = {name: jnp.asarray(value) for name, value in TABLES.items()}
    where = jnp.stack([lax.axis_index("band"), lax.axis_index("slab")]).astype(jnp.int32)
    resp = response.reshape(STK, 2 * N)
    prev = previous.reshape(STK, 2 * N)
    occ_all = lax.all_gather(occupied.reshape(1, STK, 2 * N), "band", axis=0, tiled=True)

    occ_planes = occupied_real.reshape(2, PL, N, N)
    xc_planes = xc_kernel.reshape(PL, N, N)
    gx = stick_map // N % HALF
    gy = stick_map % HALF
    q_mask = (gx[None, :] // 4 == jnp.arange(16, dtype=jnp.int32)[:, None]).astype(F32)
    column = gx % 4 * HALF + gy
    cells = jnp.arange(256, dtype=jnp.int32)
    pick = (column[None, :] == cells[:, None]).astype(BF16)
    place = (column[:, None] == cells[None, :]).astype(BF16)

    field = call(sticks_to_z, shape(SLABS, 2 * PL, STK), resp, t["z_inverse"])
    field = swap(field, "slab")
    bf_scratch = lambda *dims: pltpu.VMEM(dims, BF16)
    partial = call(
        planes_to_modes,
        shape(N * PL, N),
        field, q_mask, place, t["y_inverse"], t["x_inverse"], occ_planes, t["modes"], t["modes_t"],
        scratch=[bf_scratch(N, PL * N) for _ in range(4)],
    )
    partial = swap(partial.reshape(BANDS, AX * PL, N), "band")
    to_slabs, to_bands = call(
        sum_bands, [shape(SLABS, AX * PL, N), shape(BANDS, AX * PL, N)], partial
    )
    columns = swap(to_slabs, "slab")
    density = swap(to_bands, "band")
    xc_part = call(
        density_part, shape(PL, N, N), density.reshape(N * PL, N), t["modes"], t["modes_t"], xc_planes
    )
    hartree = call(
        solve_z, shape(BANDS, AX * PL, N), where, columns, t["modes"], t["modes_t32"], in_smem=(0,)
    )
    hartree = swap(hartree, "band")
    chosen = call(
        planes_to_sticks,
        shape(SLABS, 2 * PL, STK),
        hartree.reshape(N * PL, N), xc_part, occ_planes, q_mask, pick,
        t["modes"], t["modes_t"], t["x_forward"], t["y_forward"],
        scratch=[bf_scratch(N, 8 * N), bf_scratch(N, 8 * N), pltpu.VMEM((2, 2 * N, N), F32)],
    )
    gathered = swap(chosen, "slab")
    applied, overlaps = call(
        apply_and_overlap,
        [shape(STK, 2 * N), shape(SLABS, 1, N)],
        gathered, t["z_forward"], occ_all,
        scratch=[pltpu.VMEM((N, N), F32)],
    )
    overlaps = swap(overlaps, "slab")
    scalars = jnp.stack([band_gap[0], earlier_beta[0]])
    rest, margin, sums = call(
        push,
        [shape(STK, 2 * N), shape(1, N), shape(SLABS, 1, N)],
        overlaps, scalars, resp, prev, applied, occ_all,
        in_smem=(1,),
    )
    sums = swap(sums, "slab")
    sums = swap(call(merge_slabs, shape(BANDS, 1, N), sums), "band")
    next_vector, coefficients = call(
        finish, [shape(STK, 2 * N), shape(1, N)], sums, resp, rest
    )
    return (
        next_vector.reshape(1, STK, 2 * N),
        margin[0, : 2 * BANDS].reshape(2, BANDS, 1),
        coefficients[0, :2],
    )


def solution(mesh):
    placed = (
        P("band", "slab", None),
        P("band", "slab", None),
        P(),
        P("band"),
        P("band", "slab", None),
        P("band", None, "slab", None),
        P("slab", None),
        P(),
    )
    return jax.shard_map(
        per_device,
        mesh=mesh,
        in_specs=placed,
        out_specs=(P("band", "slab", None), P(None, None, "band"), P()),
        check_vma=False,
    )
```

time: 838 us -> 204 us (0.24)
  local copies, waits for them, and re-layouts: 259 us -> 7.49 us
  waiting for transfers between devices: 240 us -> 58.2 us
  blocking collectives: 232 us -> 54 us
  Pallas kernels: 0 us -> 19.1 us
  matrix products: 16.1 us -> 0 us
  other arithmetic: 16.2 us -> 1.44 us
    psum x3 -> x0, blocking collectives: 232 us -> none  [the longest x1 109 us: per_device(): q_norm_all, q_push_all = lax.psum((q_norm, q_push), ('band', 'slab'))]
    scatter x1 -> x0, local copies, waits for them, and re-layouts: 187 us -> none  [per_device(): plane_grid = jnp.zeros((bands, 2, planes, grid_size * grid_size), jnp.flo...]
    psum x1 -> x0, waiting for transfers between devices: 130 us -> none  [per_device(): density = lax.psum(partial_sum, 'band')]
    all_to_all x0 -> x3, blocking collectives: none -> 54 us  [swap(): return lax.all_to_all(value, axis, 0, 0, tiled=True)]
    all_to_all x4 -> x6, waiting for transfers between devices: 109 us -> 57.5 us  [swap(): return lax.all_to_all(value, axis, 0, 0, tiled=True)]
    gather x1 -> x0, local copies, waits for them, and re-layouts: 20.1 us -> none  [per_device(): chosen = jnp.take(transformed, stick_map, axis=3)]
    pallas_call x0 -> x10, Pallas kernels: none -> 19.1 us  [call(): pl.pallas_call(body, out_shape=out, in_specs=specs, out_specs=out_specs,...]
    dot_general x14 -> x0, matrix products: 16.1 us -> none  [the longest x1 3.08 us: per_device(): lax.dot_general(block_rows.reshape(block_rows.shape[0], flat_size), probe...]
  transfers between devices with their start and end apart: 6 -> 7, of which waited for: 5 -> 6; matrix products, arithmetic and copies ran while one was open for 6% -> 2% of each run, Pallas kernels for 0% -> 6%
where the time goes in v1:
time: 204 us; the launch traced here: 203 us
  waiting for transfers between devices  58.2 us (29%)
  blocking collectives  54 us (26%)
  starting transfers between devices  47.6 us (23%)
  Pallas kernels  19.1 us (9%)
  between operations  15.5 us (8%)
  local copies, waits for them, and re-layouts  7.49 us (4%)
    all_to_all x6, waiting for transfers between devices, swap(): return lax.all_to_all(value, axis, 0, 0, tiled=True)  57.5 us
    all_to_all x3, blocking collectives, swap(): return lax.all_to_all(value, axis, 0, 0, tiled=True)  54 us
    all_to_all x6, starting transfers between devices, swap(): return lax.all_to_all(value, axis, 0, 0, tiled=True)  47.5 us
    pallas_call x10, Pallas kernels, call(): pl.pallas_call(body, out_shape=out, in_specs=specs, out_specs=out_specs,...  19.1 us
    unnamed x32, local copies, waits for them, and re-layouts  6.31 us
  transfers between devices with their start and end apart: 7, of which 6 were waited for; matrix products, arithmetic and copies ran while one was open for 2% of the time, Pallas kernels for 6%

profile of v1, /device:TPU:1, one launch (start us, length us, event | category | flops | bytes accessed | tf_op | source)
XLA Modules:
  0.0 203.3 jit_solution(9936397737554326129)
XLA Ops:
  7.2 0.9 copy-done.3
  8.1 0.9 copy-done.7
  9.0 0.9 shard_map.184
  10.0 15.7 %all-to-all-start = ((f32[16,16,128]{2,1,0:T(8,128)}), f32[16,16,128]{2,1,0:T(8,128)S(1)}, u32[]{:S(2)}, u32[]{:S(2)}) async-start(f32[16,16,128]{2,1,0:T(8,128)} %shard_map.184), calls=%async_computation | async-start | bytes 262144 | tf_op jit(solution)/shard_map/all_to_all | solution.py:344
  25.8 0.7 all-gather.2.cloned.1.call-update
  26.4 0.7 fusion.6
  27.2 1.1 copy.27
  28.7 9.0 %all-to-all-done.recv = f32[16,16,128]{2,1,0:T(8,128)S(1)} async-done(((f32[16,16,128]{2,1,0:T(8,128)}), f32[16,16,128]{2,1,0:T(8,128)S(1)}, u32[]{:S(2)}, u32[]{:S(2)}) %all-to-all-start) | async-done | bytes 131104 | tf_op jit(solution)/shard_map/all_to_all | solution.py:344
  37.7 4.3 %shard_map.185 = f32[1024,128]{1,0:T(8,128)S(1)} custom-call(f32[16,16,128]{2,1,0:T(8,128)S(1)} %all-to-all-done.recv, f32[16,2048]{1,0:T(8,128)S(1)} %fusion.2.q_mask, bf16[2048,256]{1,0:T(8,128)(2,1)S(1)} %fusion.place, bf16[2,256,1024]{2,1,0:T(8,128)(2,1)S(1)} %copy-done.6, bf16[2,256,128]{2,1,0:T(8,128)(2,1)S(1)} %copy-done.11, ...), custom_call_target="tpu_custom_call" | custom-call | tf_op jit(solution)/shard_map/pallas_call | solution.py:119
  42.1 22.6 %all_to_all.45.recv = f32[32,32,128]{2,1,0:T(8,128)S(1)} all-to-all(f32[32,32,128]{2,1,0:T(8,128)S(1)} %bitcast.23), channel_id=1, replica_groups=mesh['band'=32,'slab'=16] {'band'}, dimensions={0} | all-to-all | bytes 1048576 | tf_op jit(solution)/shard_map/all_to_all | solution.py:344
  64.7 0.9 shard_map.186
  65.6 17.6 %all_to_all.46.recv = f32[16,32,128]{2,1,0:T(8,128)S(1)} all-to-all(f32[16,32,128]{2,1,0:T(8,128)S(1)} %get-tuple-element.12), channel_id=1, replica_groups=mesh['band'=32,'slab'=16] {'slab'}, dimensions={0} | all-to-all | bytes 524288 | tf_op jit(solution)/shard_map/all_to_all | solution.py:344
  83.2 8.7 %all-to-all-start.4 = ((f32[32,32,128]{2,1,0:T(8,128)}), f32[32,32,128]{2,1,0:T(8,128)S(1)}, u32[]{:S(2)}, u32[]{:S(2)}) async-start(f32[32,32,128]{2,1,0:T(8,128)} %get-tuple-element.13), calls=%async_computation.4 | async-start | bytes 1048576 | tf_op jit(solution)/shard_map/all_to_all | solution.py:344
  92.0 1.8 shard_map.187
  93.8 9.8 %all-to-all-done.4 = f32[32,32,128]{2,1,0:T(8,128)S(1)} async-done(((f32[32,32,128]{2,1,0:T(8,128)}), f32[32,32,128]{2,1,0:T(8,128)S(1)}, u32[]{:S(2)}, u32[]{:S(2)}) %all-to-all-start.4) | async-done | bytes 524320 | tf_op jit(solution)/shard_map/all_to_all | solution.py:344
  103.6 4.0 %all-to-all-start.3 = ((f32[32,32,128]{2,1,0:T(8,128)}), f32[32,32,128]{2,1,0:T(8,128)S(1)}, u32[]{:S(2)}, u32[]{:S(2)}) async-start(f32[32,32,128]{2,1,0:T(8,128)} %shard_map.187), calls=%async_computation.3 | async-start | bytes 1048576 | tf_op jit(solution)/shard_map/all_to_all | solution.py:344
  107.9 0.7 shard_map.188.xc_part
  108.6 10.6 %all-to-all-done.3 = f32[32,32,128]{2,1,0:T(8,128)S(1)} async-done(((f32[32,32,128]{2,1,0:T(8,128)}), f32[32,32,128]{2,1,0:T(8,128)S(1)}, u32[]{:S(2)}, u32[]{:S(2)}) %all-to-all-start.3) | async-done | bytes 524320 | tf_op jit(solution)/shard_map/all_to_all | solution.py:344
  119.2 1.6 copy-done.2
  120.8 4.6 %shard_map.189 = f32[16,16,128]{2,1,0:T(8,128)} custom-call(f32[1024,128]{1,0:T(8,128)S(1)} %bitcast.22, f32[8,128,128]{2,1,0:T(8,128)S(1)} %shard_map.188.xc_part, bf16[2,8,128,128]{3,2,1,0:T(8,128)(2,1)S(1)} %copy.27, f32[16,2048]{1,0:T(8,128)S(1)} %fusion.2.q_mask, bf16[256,2048]{1,0:T(8,128)(2,1)S(1)} %fusion.1.pick, bf16[2,128,128]{2,1,0:T(8,128)(2,1)S(1)} %copy-done.5, ...), custom_call_target="tpu_custom_call" | custom-call | tf_op jit(solution)/shard_map/pallas_call | solution.py:119
  125.4 5.8 %all-to-all-start.5 = ((f32[16,16,128]{2,1,0:T(8,128)}), f32[16,16,128]{2,1,0:T(8,128)S(1)}, u32[]{:S(2)}, u32[]{:S(2)}) async-start(f32[16,16,128]{2,1,0:T(8,128)} %shard_map.189), calls=%async_computation.5 | async-start | bytes 262144 | tf_op jit(solution)/shard_map/all_to_all | solution.py:344
  132.5 10.7 %all-to-all-done.5.recv = f32[16,16,128]{2,1,0:T(8,128)S(1)} async-done(((f32[16,16,128]{2,1,0:T(8,128)}), f32[16,16,128]{2,1,0:T(8,128)S(1)}, u32[]{:S(2)}, u32[]{:S(2)}) %all-to-all-start.5) | async-done | bytes 131104 | tf_op jit(solution)/shard_map/all_to_all | solution.py:344
  143.2 1.6 copy-done
  144.8 1.9 shard_map.190
  146.7 6.4 %all-to-all-start.6 = ((f32[16,1,128]{2,1,0:T(1,128)}), f32[16,1,128]{2,1,0:T(1,128)S(1)}, u32[]{:S(2)}, u32[]{:S(2)}) async-start(f32[16,1,128]{2,1,0:T(1,128)} %get-tuple-element.14), calls=%async_computation.6 | async-start | bytes 16384 | tf_op jit(solution)/shard_map/all_to_all | solution.py:344
  153.2 11.1 %all-to-all-done.6.recv = f32[16,1,128]{2,1,0:T(1,128)S(1)} async-done(((f32[16,1,128]{2,1,0:T(1,128)}), f32[16,1,128]{2,1,0:T(1,128)S(1)}, u32[]{:S(2)}, u32[]{:S(2)}) %all-to-all-start.6) | async-done | bytes 8224 | tf_op jit(solution)/shard_map/all_to_all | solution.py:344
  164.4 1.8 shard_map.191
  166.2 13.8 %all_to_all.47.recv = f32[16,1,128]{2,1,0:T(1,128)S(1)} all-to-all(f32[16,1,128]{2,1,0:T(1,128)S(1)} %get-tuple-element.16), channel_id=1, replica_groups=mesh['band'=32,'slab'=16] {'slab'}, dimensions={0} | all-to-all | bytes 16384 | tf_op jit(solution)/shard_map/all_to_all | solution.py:344
  180.0 1.0 shard_map.192
  181.0 6.9 %all-to-all-start.8 = ((f32[32,1,128]{2,1,0:T(1,128)}), f32[32,1,128]{2,1,0:T(1,128)S(1)}, u32[]{:S(2)}, u32[]{:S(2)}) async-start(f32[32,1,128]{2,1,0:T(1,128)} %shard_map.192), calls=%async_computation.8 | async-start | bytes 32768 | tf_op jit(solution)/shard_map/all_to_all | solution.py:344
  188.6 6.2 %all-to-all-done.8.recv = f32[32,1,128]{2,1,0:T(1,128)S(1)} async-done(((f32[32,1,128]{2,1,0:T(1,128)}), f32[32,1,128]{2,1,0:T(1,128)S(1)}, u32[]{:S(2)}, u32[]{:S(2)}) %all-to-all-start.8) | async-done | bytes 16416 | tf_op jit(solution)/shard_map/all_to_all | solution.py:344
  194.8 1.1 shard_map.193
  (37 shorter events, 2.1 us)
Async XLA Ops:
  7.2 0.9 copy-start.3
  8.1 0.9 copy-start.7
  9.0 28.7 %copy-start.5 = (bf16[2,128,128]{2,1,0:T(8,128)(2,1)S(1)}, bf16[2,128,128]{2,1,0:T(8,128)(2,1)}, u32[]{:S(2)}) copy-start(bf16[2,128,128]{2,1,0:T(8,128)(2,1)} %constant.88.clone.modes) | copy-start | bytes 196612
  9.0 28.7 %copy-start.6 = (bf16[2,256,1024]{2,1,0:T(8,128)(2,1)S(1)}, bf16[2,256,1024]{2,1,0:T(8,128)(2,1)}, u32[]{:S(2)}) copy-start(bf16[2,256,1024]{2,1,0:T(8,128)(2,1)} %constant.84.clone.y_table) | copy-start | bytes 3145732
  9.0 28.7 %copy-start.9 = (bf16[2,128,128]{2,1,0:T(8,128)(2,1)S(1)}, bf16[2,128,128]{2,1,0:T(8,128)(2,1)}, u32[]{:S(2)}) copy-start(bf16[2,128,128]{2,1,0:T(8,128)(2,1)} %constant.89.clone.modes_t) | copy-start | bytes 196612
  9.0 28.7 %copy-start.11 = (bf16[2,256,128]{2,1,0:T(8,128)(2,1)S(1)}, bf16[2,256,128]{2,1,0:T(8,128)(2,1)}, u32[]{:S(2)}) copy-start(bf16[2,256,128]{2,1,0:T(8,128)(2,1)} %constant.86.clone.x_table) | copy-start | bytes 393220
  10.0 27.8 %all-to-all-start = ((f32[16,16,128]{2,1,0:T(8,128)}), f32[16,16,128]{2,1,0:T(8,128)S(1)}, u32[]{:S(2)}, u32[]{:S(2)}) async-start(f32[16,16,128]{2,1,0:T(8,128)} %shard_map.184), calls=%async_computation | async-start | bytes 262144 | tf_op jit(solution)/shard_map/all_to_all | solution.py:344
  25.7 117.5 %all-gather.2.cloned.1.call-start = ((), (), s32[]{:S(2)}) async-start(), calls=%async_computation.9 | async-start | bytes 2162688 | tf_op jit(solution)/shard_map/all_gather | solution.py:354
  42.1 49.9 %copy-start.13 = (f32[128,128]{1,0:T(8,128)S(1)}, f32[128,128]{1,0:T(8,128)}, u32[]{:S(2)}) copy-start(f32[128,128]{1,0:T(8,128)} %constant.90.clone.modes_t32) | copy-start | bytes 196612
  64.7 42.9 %copy-start.14 = (f32[8,16384]{1,0:T(8,128)S(1)}, f32[8,16384]{1,0:T(8,128)}, u32[]{:S(2)}) copy-start(f32[8,16384]{1,0:T(8,128)} %param.23) | copy-start | bytes 1572868
  83.2 20.4 %all-to-all-start.4 = ((f32[32,32,128]{2,1,0:T(8,128)}), f32[32,32,128]{2,1,0:T(8,128)S(1)}, u32[]{:S(2)}, u32[]{:S(2)}) async-start(f32[32,32,128]{2,1,0:T(8,128)} %get-tuple-element.13), calls=%async_computation.4 | async-start | bytes 1048576 | tf_op jit(solution)/shard_map/all_to_all | solution.py:344
  103.6 15.7 %all-to-all-start.3 = ((f32[32,32,128]{2,1,0:T(8,128)}), f32[32,32,128]{2,1,0:T(8,128)S(1)}, u32[]{:S(2)}, u32[]{:S(2)}) async-start(f32[32,32,128]{2,1,0:T(8,128)} %shard_map.187), calls=%async_computation.3 | async-start | bytes 1048576 | tf_op jit(solution)/shard_map/all_to_all | solution.py:344
  107.6 11.7 %copy-start.12 = (bf16[2,128,128]{2,1,0:T(8,128)(2,1)S(1)}, bf16[2,128,128]{2,1,0:T(8,128)(2,1)}, u32[]{:S(2)}) copy-start(bf16[2,128,128]{2,1,0:T(8,128)(2,1)} %constant.87.clone.x_table) | copy-start | bytes 196612
  119.2 1.6 copy-start.2
  120.8 22.4 %copy-start.8 = (bf16[2,256,256]{2,1,0:T(8,128)(2,1)S(1)}, bf16[2,256,256]{2,1,0:T(8,128)(2,1)}, u32[]{:S(2)}) copy-start(bf16[2,256,256]{2,1,0:T(8,128)(2,1)} %constant.83.clone.table) | copy-start | bytes 786436
  125.4 39.0 %copy-start.4 = (f32[1,128,256]{2,1,0:T(8,128)S(1)}, f32[1,128,256]{2,1,0:T(8,128)}, u32[]{:S(2)}) copy-start(f32[1,128,256]{2,1,0:T(8,128)} %param.17) | copy-start | bytes 393220
  125.4 39.0 %copy-start.10 = (f32[1,128,256]{2,1,0:T(8,128)S(1)}, f32[1,128,256]{2,1,0:T(8,128)}, u32[]{:S(2)}) copy-start(f32[1,128,256]{2,1,0:T(8,128)} %param.18) | copy-start | bytes 393220
  125.4 17.8 %all-to-all-start.5 = ((f32[16,16,128]{2,1,0:T(8,128)}), f32[16,16,128]{2,1,0:T(8,128)S(1)}, u32[]{:S(2)}, u32[]{:S(2)}) async-start(f32[16,16,128]{2,1,0:T(8,128)} %shard_map.189), calls=%async_computation.5 | async-start | bytes 262144 | tf_op jit(solution)/shard_map/all_to_all | solution.py:344
  143.2 1.6 copy-start
  144.8 19.6 %copy-start.1 = (bf16[32,128,256]{2,1,0:T(8,128)(2,1)S(1)}, bf16[32,128,256]{2,1,0:T(8,128)(2,1)}, u32[]{:S(2)}) copy-start(bf16[32,128,256]{2,1,0:T(8,128)(2,1)} %all-gather.2.cloned.1.call-done.occ_all) | copy-start | bytes 6291460
  146.7 17.7 %all-to-all-start.6 = ((f32[16,1,128]{2,1,0:T(1,128)}), f32[16,1,128]{2,1,0:T(1,128)S(1)}, u32[]{:S(2)}, u32[]{:S(2)}) async-start(f32[16,1,128]{2,1,0:T(1,128)} %get-tuple-element.14), calls=%async_computation.6 | async-start | bytes 16384 | tf_op jit(solution)/shard_map/all_to_all | solution.py:344
  181.0 13.8 %all-to-all-start.8 = ((f32[32,1,128]{2,1,0:T(1,128)}), f32[32,1,128]{2,1,0:T(1,128)S(1)}, u32[]{:S(2)}, u32[]{:S(2)}) async-start(f32[32,1,128]{2,1,0:T(1,128)} %shard_map.192), calls=%async_computation.8 | async-start | bytes 32768 | tf_op jit(solution)/shard_map/all_to_all | solution.py:344
Sparse Core Ops, SparseCore 0:
  29.7 61.7 all-gather.1

commit v2 on v1

v2 whole, which is shorter than its diff:
```python
import math

import jax
import jax.numpy as jnp
import ml_dtypes
import numpy as np
from jax import lax
from jax.experimental import pallas as pl
from jax.experimental.pallas import tpu as pltpu
from jax.sharding import PartitionSpec as P

F32 = jnp.float32
BF16 = jnp.bfloat16
MIB = 1024 * 1024

N = 128
SLABS = 16
PL = N // SLABS
BANDS = 32
AX = N // BANDS
STK = 128
STICKS = SLABS * STK
HALF = 64
NORM = float(N) ** -1.5


def pieces(table):
    high = table.astype(np.float32).astype(ml_dtypes.bfloat16)
    low = (table - high.astype(np.float64)).astype(np.float32).astype(ml_dtypes.bfloat16)
    return np.stack([high, low])


def angle(a, b):
    return 2.0 * np.pi * ((np.asarray(a)[:, None] * np.asarray(b)[None, :]) % N) / N


def tables():
    every = np.arange(N)
    short = np.arange(HALF)
    signed = np.where(short < HALF // 2, short, short - HALF)
    signed_x = signed.reshape(16, 4).T.reshape(-1)

    c, s = np.cos(angle(every, every)), np.sin(angle(every, every))
    by_slab = lambda m: m.reshape(SLABS, 1, PL, -1)
    z_inverse = np.concatenate(
        [
            np.concatenate([by_slab(c), by_slab(-s)], axis=3),
            np.concatenate([by_slab(s), by_slab(c)], axis=3),
        ],
        axis=1,
    ).reshape(2 * N, 2 * N)
    z_forward = np.concatenate(
        [
            np.concatenate([by_slab(c), by_slab(-s)], axis=3),
            np.concatenate([by_slab(s), by_slab(c)], axis=3),
        ],
        axis=1,
    ).reshape(2 * N, 2 * N)

    cy, sy = np.cos(angle(signed, every)), np.sin(angle(signed, every))
    y_inverse = np.tile(np.concatenate([cy, sy], axis=1), (4, 1))
    y_forward = np.block(
        [[np.tile(cy.T, (1, 4)), np.tile(-sy.T, (1, 4))], [np.tile(sy.T, (1, 4)), np.tile(cy.T, (1, 4))]]
    )

    cx, sx = np.cos(angle(every, signed_x)), np.sin(angle(every, signed_x))
    x_inverse = 2.0 * NORM * np.block([[cx, -sx], [sx, cx]])
    x_forward = NORM * np.concatenate([cx.T, sx.T], axis=0)

    modes = np.zeros((N, N))
    modes[0] = 1.0 / math.sqrt(N)
    modes[1:64] = math.sqrt(2.0 / N) * np.cos(angle(np.arange(1, 64), every))
    modes[64] = np.cos(np.pi * every) / math.sqrt(N)
    modes[65:] = math.sqrt(2.0 / N) * np.sin(angle(np.arange(1, 64), every))
    return {
        "z_inverse": pieces(z_inverse),
        "z_forward": pieces(z_forward),
        "y_inverse": pieces(y_inverse),
        "y_forward": pieces(y_forward),
        "x_inverse": pieces(x_inverse),
        "x_forward": pieces(x_forward),
        "modes": pieces(modes),
        "modes_t": pieces(modes.T),
        "modes_t32": modes.T.astype(np.float32),
    }


TABLES = tables()


def split(value):
    high = value.astype(BF16)
    return high, (value - high.astype(F32)).astype(BF16)


def dot(a, b, contract=((1,), (0,))):
    return lax.dot_general(a, b, (contract, ((), ())), preferred_element_type=F32)


def dot3(a, b, contract=((1,), (0,))):
    return dot(a[0], b[0], contract) + (dot(a[1], b[0], contract) + dot(a[0], b[1], contract))


def call(body, out, *args, scratch=(), in_smem=(), in_hbm=(), vmem=16):
    space = lambda i: pltpu.SMEM if i in in_smem else pltpu.HBM if i in in_hbm else pltpu.VMEM
    in_vmem = pl.BlockSpec(memory_space=pltpu.VMEM)
    many = isinstance(out, (list, tuple))
    return pl.pallas_call(
        body,
        out_shape=out,
        in_specs=[pl.BlockSpec(memory_space=space(i)) for i in range(len(args))],
        out_specs=[in_vmem] * len(out) if many else in_vmem,
        scratch_shapes=[
            *(pltpu.VMEM(args[i].shape, args[i].dtype) for i in in_hbm),
            *([pltpu.SemaphoreType.DMA((max(len(in_hbm), BANDS // CHUNK),))] if in_hbm else []),
            *scratch,
        ],
        compiler_params=pltpu.CompilerParams(vmem_limit_bytes=vmem * MIB),
    )(*args)


def fetch(sources, targets, sems):
    copies = [pltpu.make_async_copy(s, t, sems.at[i]) for i, (s, t) in enumerate(zip(sources, targets))]
    for copy in copies:
        copy.start()
    return copies


def shape(*dims, dtype=F32):
    return jax.ShapeDtypeStruct(dims, dtype)


def sticks_to_z(resp_hbm, table_hbm, out, resp, table, sems):
    for copy in fetch((resp_hbm, table_hbm), (resp, table), sems):
        copy.wait()
    out[...] = dot3((table[0], table[1]), split(resp[...]), ((1,), (1,))).reshape(SLABS, 2 * PL, STK)


def q_mask_of(cells, lanes):
    q = lax.broadcasted_iota(jnp.int32, (16, 1), 0)
    return (cells[:, lanes] // 256 == q).astype(F32)


def pick_of(cells, lanes):
    column = lax.broadcasted_iota(jnp.int32, (256, 1), 0)
    return jnp.where(cells[:, lanes] % 256 == column, 1.0, 0.0).astype(BF16)


def planes_to_modes(
    recv, cells, y_hbm, x_hbm, occ_hbm, modes_hbm, modes_t_hbm,
    out, y_table, x_table, occ, modes, modes_t, sems, r_high, r_low, d_high, d_low
):
    copies = fetch(
        (y_hbm, x_hbm, occ_hbm, modes_hbm, modes_t_hbm), (y_table, x_table, occ, modes, modes_t), sems
    )
    grid = jnp.zeros((256, 256), F32)
    for src in range(SLABS):
        lanes = slice(src * STK, (src + 1) * STK)
        high, low = split(recv[src])
        mask = q_mask_of(cells, lanes)
        rows = [
            (part.astype(F32)[:, None, :] * mask[None]).reshape(256, STK).astype(BF16)
            for part in (high, low)
        ]
        chosen = pick_of(cells, lanes)
        grid += dot(
            jnp.concatenate(rows, axis=1), jnp.concatenate([chosen, chosen], axis=1), ((1,), (1,))
        )
    grid = split(grid)
    for copy in copies:
        copy.wait()
    lane_j = lax.broadcasted_iota(jnp.int32, (1, 256), 1) // HALF
    for j in range(4):
        own = (lane_j == j).astype(BF16)
        mixed = dot3((grid[0] * own, grid[1] * own), (y_table[0], y_table[1]))
        real = mixed[:N, :N] - mixed[N:, N:]
        imag = mixed[:N, N:] + mixed[N:, :N]
        for c, part in enumerate((real, imag)):
            high, low = split(part)
            at = slice(c * HALF + j * 16, c * HALF + (j + 1) * 16)
            for p in range(PL):
                r_high[at, p * N : (p + 1) * N] = high[p * 16 : (p + 1) * 16]
                r_low[at, p * N : (p + 1) * N] = low[p * 16 : (p + 1) * 16]
    for p in range(PL):
        lanes = slice(p * N, (p + 1) * N)
        field = dot3((x_table[0], x_table[1]), (r_high[:, lanes], r_low[:, lanes]))
        density = occ[0, p].astype(F32) * field[:N] + occ[1, p].astype(F32) * field[N:]
        half = dot3(split(density), (modes_t[0], modes_t[1]))
        d_high[:, lanes], d_low[:, lanes] = split(half)
    for p in range(PL):
        lanes = slice(p * N, (p + 1) * N)
        out[pl.ds(p, N, stride=PL), :] = dot3(
            (modes[0], modes[1]), (d_high[:, lanes], d_low[:, lanes])
        )


def sum_bands(recv, to_slabs):
    total = recv[0]
    for b in range(1, BANDS):
        total = total + recv[b]
    for i in range(SLABS):
        to_slabs[i] = total


def solve_z(where, recv, modes, modes_t32, out):
    columns = [
        jnp.concatenate([recv[i, a * PL : (a + 1) * PL, :] for i in range(SLABS)], axis=0)
        for a in range(AX)
    ]
    spectrum = dot3((modes[0], modes[1]), split(jnp.concatenate(columns, axis=1)))
    freq = lambda i: jnp.where(i <= N // 2, i, i - N // 2)
    fz = freq(lax.broadcasted_iota(jnp.int32, (N, N), 0))
    fy = freq(lax.broadcasted_iota(jnp.int32, (N, N), 1))
    plane_sq = fz * fz + fy * fy
    weighted = []
    for a in range(AX):
        fx = freq(where[0] * AX + a)
        square = (plane_sq + fx * fx).astype(F32)
        kernel = jnp.where(
            square > 0.0, (0.2 * N) ** 2 / (math.pi * jnp.maximum(square, 1.0)), 0.0
        )
        weighted.append(spectrum[:, a * N : (a + 1) * N] * kernel)
    own = modes_t32[pl.ds(pl.multiple_of(where[1] * PL, PL), PL), :]
    result = dot3(split(own), split(jnp.concatenate(weighted, axis=1)))
    density = recv[where[1]]
    tile = []
    for a in range(AX):
        tile += [result[:, a * N : (a + 1) * N], density[a * PL : (a + 1) * PL]]
    tile = jnp.concatenate(tile, axis=0)
    for i in range(BANDS):
        out[i] = tile


def planes_from_modes(recv, modes, modes_t, p):
    spectrum = jnp.concatenate(
        [recv[pl.ds(i * PL + p, N, stride=2 * PL), :] for i in range(2)], axis=1
    )
    half = dot3((modes_t[0], modes_t[1]), split(spectrum))
    half = jnp.concatenate([half[:, :N], half[:, N:]], axis=0)
    plane = dot3(split(half), (modes[0], modes[1]))
    return plane[:N], plane[N:]


def planes_to_sticks(
    recv, cells, modes_hbm, modes_t_hbm, xc_hbm, occ_hbm, x_hbm, y_hbm,
    out, modes, modes_t, xc, occ, x_table, y_table, sems, l_high, l_low, grid
):
    copies = fetch(
        (modes_hbm, modes_t_hbm, xc_hbm, occ_hbm, x_hbm, y_hbm),
        (modes, modes_t, xc, occ, x_table, y_table),
        sems,
    )
    for copy in copies:
        copy.wait()
    for p in range(PL):
        hartree, density = planes_from_modes(recv, modes, modes_t, p)
        potential = hartree + xc[p] * density
        product = jnp.concatenate(
            [potential * occ[0, p].astype(F32), potential * occ[1, p].astype(F32)], axis=1
        )
        mixed = dot3((x_table[0], x_table[1]), split(product))
        real = mixed[:HALF, :N] + mixed[HALF:, N:]
        imag = mixed[:HALF, N:] - mixed[HALF:, :N]
        for c, part in enumerate((real, imag)):
            high, low = split(part)
            for j in range(4):
                at = slice(j * 2 * N + c * N, j * 2 * N + (c + 1) * N)
                l_high[p * 16 : (p + 1) * 16, at] = high[j * 16 : (j + 1) * 16]
                l_low[p * 16 : (p + 1) * 16, at] = low[j * 16 : (j + 1) * 16]
    lane_j = lax.broadcasted_iota(jnp.int32, (1, 512), 1) // HALF % 4
    spectrum = jnp.zeros((N, 512), F32)
    for j in range(4):
        at = slice(j * 2 * N, (j + 1) * 2 * N)
        mixed = dot3((l_high[:, at], l_low[:, at]), (y_table[0], y_table[1]))
        spectrum = jnp.where(lane_j == j, mixed, spectrum)
    for part in range(2):
        for h in range(2):
            lanes = slice(part * 2 * N + h * N, part * 2 * N + (h + 1) * N)
            grid[h, part * N : (part + 1) * N, :] = spectrum[:, lanes]
    high, low = split(
        jnp.concatenate(
            [
                jnp.concatenate([grid[h, pl.ds(q, 16, stride=16), :] for h in range(2)], axis=1)
                for q in range(16)
            ],
            axis=0,
        )
    )
    for dst in range(SLABS):
        lanes = slice(dst * STK, (dst + 1) * STK)
        pick = pick_of(cells, lanes)
        mask = q_mask_of(cells, lanes)
        chosen = dot(high, pick) + dot(low, pick)
        total = chosen[:16] * mask[:1]
        for q in range(1, 16):
            total = total + chosen[q * 16 : (q + 1) * 16] * mask[q : q + 1]
        out[dst] = total


CHUNK = 8


def orbitals(hbm, held, sems):
    copies = [
        pltpu.make_async_copy(
            hbm.at[pl.ds(i * CHUNK, CHUNK)], held.at[pl.ds(i * CHUNK, CHUNK)], sems.at[i]
        )
        for i in range(BANDS // CHUNK)
    ]
    for copy in copies:
        copy.start()

    def at(w):
        if w % CHUNK == 0:
            copies[w // CHUNK].wait()
        return held[w].astype(F32)

    return at


def overlap_rows(at, probes, sums):
    pairs = [
        (x, jnp.concatenate([x[:, N:], -x[:, :N]], axis=1)) for x in probes
    ]
    for w in range(BANDS):
        orbital = at(w)
        for i, pair in enumerate(pairs):
            for c, probe in enumerate(pair):
                line = jnp.sum(orbital * probe, axis=0, keepdims=True)
                k = c * BANDS + w
                sums[i, k : k + 1, :] = line[:, :N] + line[:, N:]
    rows = []
    for i in range(len(probes)):
        sums[i, 2 * BANDS :, :] = jnp.zeros((N - 2 * BANDS, N), F32)
        rows.append(jnp.sum(sums[i].T, axis=0, keepdims=True))
    return rows


def total_sum(value):
    return jnp.sum(jnp.sum(value, axis=0, keepdims=True), axis=1, keepdims=True)


def lane():
    return lax.broadcasted_iota(jnp.int32, (1, N), 1)


def with_lanes(row, first, values):
    for i, value in enumerate(values):
        row = jnp.where(lane() == first + i, value, row)
    return row


def lower(row):
    return jnp.where(lane() < 2 * BANDS, row, 0.0)


def fixed_overlaps(occ_all, resp, prev, occ, out, held, sems, sums):
    at = orbitals(occ_all, held, sems)
    rows = overlap_rows(at, [resp[...], prev[...], occ[...].astype(F32)], sums)
    for i, row in enumerate(rows):
        out[i : i + 1, :] = row
    out[3:, :] = jnp.zeros((5, N), F32)


def apply_and_overlap(
    recv, table, scalars, resp, prev, fixed, occ_all, applied_out, part_out, held, sems, sums
):
    at = orbitals(occ_all, held, sems)
    values = recv[...].reshape(2 * N, STK).T
    applied = dot3(split(values), (table[0], table[1]))
    applied_out[...] = applied
    margin, along = overlap_rows(at, [applied.astype(BF16).astype(F32), applied], sums)
    response = resp[...]
    first = scalars[0] * response + applied
    rest = first - scalars[1] * prev[...]
    norm = total_sum(response * response)
    slope = total_sum(response * rest) / jnp.where(norm > 0.0, norm, 1.0)
    left = rest - slope * response
    with_resp, with_prev, with_occ = fixed[0:1, :], fixed[1:2, :], fixed[2:3, :]
    along = along + (scalars[0] - slope) * with_resp - scalars[1] * with_prev
    row = jnp.concatenate(
        [
            margin + pltpu.roll(with_occ, 2 * BANDS, 1),
            along,
            with_lanes(
                with_resp,
                2 * BANDS,
                [norm, total_sum(response * first), slope, total_sum(left * left)],
            ),
        ],
        axis=1,
    )
    for i in range(SLABS):
        part_out[i] = row


def join_slabs(recv, margin_out, part_out):
    rows = [jnp.concatenate([recv[i][:, j * N : (j + 1) * N] for i in range(SLABS)], axis=0) for j in range(3)]
    add = lambda v: jnp.sum(v, axis=0, keepdims=True)
    norms, firsts, slopes, lefts = (rows[2][:, 2 * BANDS + i : 2 * BANDS + i + 1] for i in range(4))
    norm = add(norms)
    slope = add(norms * slopes) / jnp.where(norm > 0.0, norm, 1.0)
    spread_ = slopes - slope
    left = add(lefts + norms * spread_ * spread_)
    head = add(rows[0])
    weights = lower(head.astype(BF16).astype(F32))
    with_left = add(rows[1] + spread_ * rows[2])
    with_resp = add(rows[2])
    inner = lambda x: jnp.sum(weights * lower(x), axis=1, keepdims=True)
    removed_resp = inner(with_resp)
    margin_out[...] = head
    row = jnp.concatenate(
        [
            jnp.where(lane() < 2 * BANDS, weights, head),
            with_lanes(
                jnp.zeros((1, N), F32),
                0,
                [norm, add(firsts) - removed_resp, slope, removed_resp, left - 2.0 * inner(with_left)],
            ),
        ],
        axis=1,
    )
    for i in range(BANDS):
        part_out[i] = row


def remove(margin, scalars, resp, prev, applied, occ_all, rest_out, held, sems):
    at = orbitals(occ_all, held, sems)
    weights = margin[...].astype(BF16).astype(F32)
    plain = jnp.zeros((STK, 2 * N), F32)
    turned = jnp.zeros((STK, 2 * N), F32)
    for w in range(BANDS):
        orbital = at(w)
        plain = plain + weights[:, w : w + 1] * orbital
        turned = turned + weights[:, BANDS + w : BANDS + w + 1] * orbital
    removed = plain + jnp.concatenate([-turned[:, N:], turned[:, :N]], axis=1)
    rest_out[...] = scalars[0] * resp[...] + applied[...] - removed - scalars[1] * prev[...]


def finish(recv, resp, rest, next_out, coef_out):
    rows = [jnp.concatenate([recv[i][:, j * N : (j + 1) * N] for i in range(BANDS)], axis=0) for j in range(2)]
    norms, alongs, slopes, removed_resp, lefts = (rows[1][:, i : i + 1] for i in range(5))
    add = lambda v: jnp.sum(v, axis=0, keepdims=True)
    real, imag, same, cross = (rows[0][:, i * BANDS : (i + 1) * BANDS] for i in range(4))
    times = lambda a, b: lax.dot_general(
        a, b, (((1,), (1,)), ((), ())), precision=lax.Precision.HIGHEST, preferred_element_type=F32
    )
    square = total_sum(real * (times(real, same) + 2.0 * times(imag, cross)) + imag * times(imag, same))
    alpha = add(alongs) / add(norms)
    gap = slopes - alpha
    resid_sq = add(lefts + gap * (gap * norms - 2.0 * removed_resp)) + square
    beta = jnp.sqrt(jnp.maximum(resid_sq, 0.0) / float(2 * BANDS * STICKS * N) + 1e-06)
    next_out[...] = (rest[...] - alpha * resp[...]) / beta
    coef_out[...] = with_lanes(jnp.zeros((1, N), F32), 0, [alpha, beta])


def swap(value, axis):
    return lax.all_to_all(value, axis, 0, 0, tiled=True)


def after(value, other):
    return lax.optimization_barrier((value, other))


def per_device(
    response, previous, earlier_beta, band_gap, occupied, occupied_real, xc_kernel, stick_map
):
    t = {name: jnp.asarray(value) for name, value in TABLES.items()}
    where = jnp.stack([lax.axis_index("band"), lax.axis_index("slab")]).astype(jnp.int32)
    resp = response.reshape(STK, 2 * N)
    prev = previous.reshape(STK, 2 * N)

    occ_planes = occupied_real.reshape(2, PL, N, N)
    field = call(sticks_to_z, shape(SLABS, 2 * PL, STK), resp, t["z_inverse"], in_hbm=(0, 1), vmem=60)
    stick_map, _ = after(stick_map, field)
    gx = stick_map // N % HALF
    cells = (gx // 4 * 256 + gx % 4 * HALF + stick_map % HALF).reshape(1, STICKS)
    occ_all = lax.all_gather(occupied.reshape(1, STK, 2 * N), "band", axis=0, tiled=True)
    field = swap(field, "slab")
    bf_scratch = lambda *dims: pltpu.VMEM(dims, BF16)
    partial = call(
        planes_to_modes,
        shape(N * PL, N),
        field, cells, t["y_inverse"], t["x_inverse"], occ_planes, t["modes"], t["modes_t"],
        in_hbm=(2, 3, 4, 5, 6),
        scratch=[bf_scratch(N, PL * N) for _ in range(4)],
    )
    partial = swap(partial.reshape(BANDS, AX * PL, N), "band")
    total = call(sum_bands, shape(SLABS, AX * PL, N), partial)
    columns = swap(total, "slab")
    hartree = call(
        solve_z, shape(BANDS, 2 * AX * PL, N), where, columns, t["modes"], t["modes_t32"], in_smem=(0,)
    )
    xc_planes, _ = after(xc_kernel, hartree)
    xc_planes = xc_planes.reshape(PL, N, N)
    hartree = swap(hartree, "band")
    chosen = call(
        planes_to_sticks,
        shape(SLABS, 2 * PL, STK),
        hartree.reshape(2 * N * PL, N), cells,
        t["modes"], t["modes_t"], xc_planes, occ_planes, t["x_forward"], t["y_forward"],
        in_hbm=(2, 3, 4, 5, 6, 7),
        scratch=[bf_scratch(N, 8 * N), bf_scratch(N, 8 * N), pltpu.VMEM((2, 2 * N, N), F32)],
    )
    gathered = swap(chosen, "slab")
    fixed = call(
        fixed_overlaps,
        shape(8, N),
        occ_all, resp, prev, occupied.reshape(STK, 2 * N),
        in_hbm=(0,),
        scratch=[pltpu.VMEM((3, N, N), F32)],
    )
    scalars = jnp.stack([band_gap[0], earlier_beta[0]])
    applied, parts = call(
        apply_and_overlap,
        [shape(STK, 2 * N), shape(SLABS, 1, 3 * N)],
        gathered, t["z_forward"], scalars, resp, prev, fixed, occ_all,
        in_smem=(2,),
        in_hbm=(6,),
        scratch=[pltpu.VMEM((2, N, N), F32)],
    )
    margin, parts = call(
        join_slabs, [shape(1, N), shape(BANDS, 1, 2 * N)], swap(parts, "slab")
    )
    rest = call(
        remove,
        shape(STK, 2 * N),
        margin, scalars, resp, prev, applied, occ_all,
        in_smem=(1,),
        in_hbm=(5,),
    )
    next_vector, coefficients = call(
        finish, [shape(STK, 2 * N), shape(1, N)], swap(parts, "band"), resp, rest
    )
    return (
        next_vector.reshape(1, STK, 2 * N),
        margin[0, : 2 * BANDS].reshape(2, BANDS, 1),
        coefficients[0, :2],
    )


def solution(mesh):
    placed = (
        P("band", "slab", None),
        P("band", "slab", None),
        P(),
        P("band"),
        P("band", "slab", None),
        P("band", None, "slab", None),
        P("slab", None),
        P(),
    )
    return jax.shard_map(
        per_device,
        mesh=mesh,
        in_specs=placed,
        out_specs=(P("band", "slab", None), P(None, None, "band"), P()),
        check_vma=False,
    )
```

time: 204 us -> 181 us (0.89)
  blocking collectives: 54 us -> 39.8 us
  starting transfers between devices: 47.6 us -> 39.6 us
  waiting for transfers between devices: 58.2 us -> 52 us
  Pallas kernels: 19.1 us -> 24.7 us
    all_to_all x3 -> x2, blocking collectives: 54 us -> 39.8 us  [swap(): return lax.all_to_all(value, axis, 0, 0, tiled=True)]
    all_to_all x6 -> x5, starting transfers between devices: 47.5 us -> 39.5 us  [swap(): return lax.all_to_all(value, axis, 0, 0, tiled=True)]
    all_to_all x6 -> x5, waiting for transfers between devices: 57.5 us -> 51.4 us  [swap(): return lax.all_to_all(value, axis, 0, 0, tiled=True)]
    pallas_call x10, Pallas kernels: 19.1 us -> 24.7 us  [call(): pl.pallas_call(body, out_shape=out, in_specs=[pl.BlockSpec(memory_space=s...]
  transfers between devices with their start and end apart: 7 -> 6, of which waited for: 6 -> 5; matrix products, arithmetic and copies ran while one was open for 2% -> 2% of each run, Pallas kernels for 6% -> 11%
where the time goes in v2:
time: 181 us; the launch traced here: 180 us
  waiting for transfers between devices  52 us (29%)
  blocking collectives  39.8 us (22%)
  starting transfers between devices  39.6 us (22%)
  Pallas kernels  24.7 us (14%)
  between operations  15.5 us (9%)
  local copies, waits for them, and re-layouts  7.77 us (4%)
    all_to_all x5, waiting for transfers between devices, swap(): return lax.all_to_all(value, axis, 0, 0, tiled=True)  51.4 us
    all_to_all x2, blocking collectives, swap(): return lax.all_to_all(value, axis, 0, 0, tiled=True)  39.8 us
    all_to_all x5, starting transfers between devices, swap(): return lax.all_to_all(value, axis, 0, 0, tiled=True)  39.5 us
    pallas_call x10, Pallas kernels, call(): pl.pallas_call(body, out_shape=out, in_specs=[pl.BlockSpec(memory_space=s...  24.7 us
    unnamed x32, local copies, waits for them, and re-layouts  6.59 us
  transfers between devices with their start and end apart: 6, of which 5 were waited for; matrix products, arithmetic and copies ran while one was open for 2% of the time, Pallas kernels for 11%

profile of v2, /device:TPU:1, one launch (start us, length us, event | category | flops | bytes accessed | tf_op | source)
XLA Modules:
  0.0 180.2 jit_solution(9322898733012300932)
XLA Ops:
  7.2 0.7 all-gather.2.cloned.1.call-update
  7.9 2.0 %shard_map.184 = f32[16,16,128]{2,1,0:T(8,128)} custom-call(f32[128,256]{1,0:T(8,128)} %bitcast.24, bf16[2,256,256]{2,1,0:T(8,128)(2,1)} %constant.83.clone.table_hbm.table), custom_call_target="tpu_custom_call" | custom-call | tf_op jit(solution)/shard_map/pallas_call | solution.py:108
  9.9 15.8 %all-to-all-start = ((f32[16,16,128]{2,1,0:T(8,128)}), f32[16,16,128]{2,1,0:T(8,128)S(1)}, u32[]{:S(2)}, u32[]{:S(2)}) async-start(f32[16,16,128]{2,1,0:T(8,128)} %shard_map.184), calls=%async_computation | async-start | bytes 262144 | tf_op jit(solution)/shard_map/all_to_all | solution.py:458
  25.7 1.2 copy.27
  26.9 0.7 fusion.4
  27.6 10.1 %all-to-all-done.recv = f32[16,16,128]{2,1,0:T(8,128)S(1)} async-done(((f32[16,16,128]{2,1,0:T(8,128)}), f32[16,16,128]{2,1,0:T(8,128)S(1)}, u32[]{:S(2)}, u32[]{:S(2)}) %all-to-all-start) | async-done | bytes 131104 | tf_op jit(solution)/shard_map/all_to_all | solution.py:458
  37.7 0.8 copy-done.5
  38.5 0.8 copy-done.10
  39.3 0.9 copy-done.12
  40.3 4.9 %shard_map.185 = f32[1024,128]{1,0:T(8,128)S(1)} custom-call(f32[16,16,128]{2,1,0:T(8,128)S(1)} %all-to-all-done.recv, s32[1,2048]{1,0:T(1,128)S(1)} %bitcast.35, bf16[2,256,256]{2,1,0:T(8,128)(2,1)S(1)} %copy-done.9, bf16[2,256,128]{2,1,0:T(8,128)(2,1)S(1)} %copy-done.12, bf16[2,8,128,128]{3,2,1,0:T(8,128)(2,1)S(1)} %copy.27, ...), custom_call_target="tpu_custom_call" | custom-call | tf_op jit(solution)/shard_map/pallas_call | solution.py:108
  45.2 22.1 %all_to_all.35.recv = f32[32,32,128]{2,1,0:T(8,128)S(1)} all-to-all(f32[32,32,128]{2,1,0:T(8,128)S(1)} %bitcast.29), channel_id=1, replica_groups=mesh['band'=32,'slab'=16] {'band'}, dimensions={0} | all-to-all | bytes 1048576 | tf_op jit(solution)/shard_map/all_to_all | solution.py:458
  67.2 0.8 shard_map.186
  68.0 3.6 %all-to-all-start.2 = ((f32[16,32,128]{2,1,0:T(8,128)}), f32[16,32,128]{2,1,0:T(8,128)S(1)}, u32[]{:S(2)}, u32[]{:S(2)}) async-start(f32[16,32,128]{2,1,0:T(8,128)} %shard_map.186), calls=%async_computation.2 | async-start | bytes 524288 | tf_op jit(solution)/shard_map/all_to_all | solution.py:458
  71.7 13.7 %all-to-all-done.2.recv = f32[16,32,128]{2,1,0:T(8,128)S(1)} async-done(((f32[16,32,128]{2,1,0:T(8,128)}), f32[16,32,128]{2,1,0:T(8,128)S(1)}, u32[]{:S(2)}, u32[]{:S(2)}) %all-to-all-start.2) | async-done | bytes 262176 | tf_op jit(solution)/shard_map/all_to_all | solution.py:458
  85.4 2.0 %shard_map.187 = f32[32,64,128]{2,1,0:T(8,128)} custom-call(s32[2]{0:T(128)S(1)} %pad_add_fusion.where, f32[16,32,128]{2,1,0:T(8,128)S(1)} %all-to-all-done.2.recv, bf16[2,128,128]{2,1,0:T(8,128)(2,1)S(1)} %copy-done.6, f32[128,128]{1,0:T(8,128)S(1)} %copy-done.14), custom_call_target="tpu_custom_call" | custom-call | tf_op jit(solution)/shard_map/pallas_call | solution.py:108
  87.4 8.9 %all-to-all-start.3 = ((f32[32,64,128]{2,1,0:T(8,128)}), f32[32,64,128]{2,1,0:T(8,128)S(1)}, u32[]{:S(2)}, u32[]{:S(2)}) async-start(f32[32,64,128]{2,1,0:T(8,128)} %shard_map.187), calls=%async_computation.3 | async-start | bytes 2097152 | tf_op jit(solution)/shard_map/all_to_all | solution.py:458
  96.4 1.2 copy.26
  97.6 16.1 %all-to-all-done.3 = f32[32,64,128]{2,1,0:T(8,128)S(1)} async-done(((f32[32,64,128]{2,1,0:T(8,128)}), f32[32,64,128]{2,1,0:T(8,128)S(1)}, u32[]{:S(2)}, u32[]{:S(2)}) %all-to-all-start.3) | async-done | bytes 1048608 | tf_op jit(solution)/shard_map/all_to_all | solution.py:458
  113.7 5.9 %shard_map.188 = f32[16,16,128]{2,1,0:T(8,128)} custom-call(f32[2048,128]{1,0:T(8,128)S(1)} %bitcast.23, s32[1,2048]{1,0:T(1,128)S(1)} %bitcast.36, bf16[2,128,128]{2,1,0:T(8,128)(2,1)S(1)} %copy-done.6, bf16[2,128,128]{2,1,0:T(8,128)(2,1)S(1)} %copy-done.11, f32[8,128,128]{2,1,0:T(8,128)S(1)} %bitcast.30, bf16[2,8,128,128]{3,2,1,0:T(8,128)(2,1)S(1)} %copy.27, ...), custom_call_target="tpu_custom_call" | custom-call | tf_op jit(solution)/shard_map/pallas_call | solution.py:108
  119.5 5.7 %all-to-all-start.4 = ((f32[16,16,128]{2,1,0:T(8,128)}), f32[16,16,128]{2,1,0:T(8,128)S(1)}, u32[]{:S(2)}, u32[]{:S(2)}) async-start(f32[16,16,128]{2,1,0:T(8,128)} %shard_map.188), calls=%async_computation.4 | async-start | bytes 262144 | tf_op jit(solution)/shard_map/all_to_all | solution.py:458
  126.6 1.6 copy-done
  128.2 2.3 %shard_map.189.fixed = f32[8,128]{1,0:T(8,128)S(1)} custom-call(bf16[32,128,256]{2,1,0:T(8,128)(2,1)S(1)} %copy-done, f32[128,256]{1,0:T(8,128)S(1)} %bitcast.25, f32[128,256]{1,0:T(8,128)S(1)} %bitcast.31, bf16[128,256]{1,0:T(8,128)(2,1)S(1)} %bitcast.34), custom_call_target="tpu_custom_call" | custom-call | tf_op jit(solution)/shard_map/pallas_call | solution.py:108
  130.5 6.9 %all-to-all-done.4.recv = f32[16,16,128]{2,1,0:T(8,128)S(1)} async-done(((f32[16,16,128]{2,1,0:T(8,128)}), f32[16,16,128]{2,1,0:T(8,128)S(1)}, u32[]{:S(2)}, u32[]{:S(2)}) %all-to-all-start.4) | async-done | bytes 131104 | tf_op jit(solution)/shard_map/all_to_all | solution.py:458
  137.3 2.6 %shard_map.190 = (f32[128,256]{1,0:T(8,128)S(1)}, f32[16,1,384]{2,1,0:T(1,128)S(1)}) custom-call(f32[16,16,128]{2,1,0:T(8,128)S(1)} %all-to-all-done.4.recv, bf16[2,256,256]{2,1,0:T(8,128)(2,1)S(1)} %copy-done.4, f32[2]{0:T(128)S(1)} %pad_maximum_fusion.scalars, f32[128,256]{1,0:T(8,128)S(1)} %bitcast.26, f32[128,256]{1,0:T(8,128)S(1)} %bitcast.32, ...), custom_call_target="tpu_custom_call" | custom-call | tf_op jit(solution)/shard_map/pallas_call | solution.py:108
  140.0 17.7 %all_to_all.36.recv = f32[16,1,384]{2,1,0:T(1,128)S(1)} all-to-all(f32[16,1,384]{2,1,0:T(1,128)S(1)} %get-tuple-element.13), channel_id=1, replica_groups=mesh['band'=32,'slab'=16] {'slab'}, dimensions={0} | all-to-all | bytes 49152 | tf_op jit(solution)/shard_map/all_to_all | solution.py:458
  157.7 1.0 shard_map.191
  158.7 5.6 %all-to-all-start.6 = ((f32[32,1,256]{2,1,0:T(1,128)}), f32[32,1,256]{2,1,0:T(1,128)S(1)}, u32[]{:S(2)}, u32[]{:S(2)}) async-start(f32[32,1,256]{2,1,0:T(1,128)} %get-tuple-element.14), calls=%async_computation.6 | async-start | bytes 65536 | tf_op jit(solution)/shard_map/all_to_all | solution.py:458
  164.3 0.6 reshape_squeeze.3
  165.0 2.0 %shard_map.192.rest = f32[128,256]{1,0:T(8,128)S(1)} custom-call(f32[1,128]{1,0:T(1,128)S(1)} %get-tuple-element.15.margin, f32[2]{0:T(128)S(1)} %pad_maximum_fusion.scalars, f32[128,256]{1,0:T(8,128)S(1)} %bitcast.27, f32[128,256]{1,0:T(8,128)S(1)} %bitcast.33, f32[128,256]{1,0:T(8,128)S(1)} %get-tuple-element.16.applied, bf16[32,128,256]{2,1,0:T(8,128)(2,1)S(1)} %copy-done.1), custom_call_target="tpu_custom_call" | custom-call | tf_op jit(solution)/shard_map/pallas_call | solution.py:108
  167.0 4.6 %all-to-all-done.6.recv = f32[32,1,256]{2,1,0:T(1,128)S(1)} async-done(((f32[32,1,256]{2,1,0:T(1,128)}), f32[32,1,256]{2,1,0:T(1,128)S(1)}, u32[]{:S(2)}, u32[]{:S(2)}) %all-to-all-start.6) | async-done | bytes 32800 | tf_op jit(solution)/shard_map/all_to_all | solution.py:458
  171.6 1.3 shard_map.193
  172.9 0.5 slice_bitcast_fusion
  (31 shorter events, 0.3 us)
Async XLA Ops:
  7.2 30.5 %copy-start.9 = (bf16[2,256,256]{2,1,0:T(8,128)(2,1)S(1)}, bf16[2,256,256]{2,1,0:T(8,128)(2,1)}, u32[]{:S(2)}) copy-start(bf16[2,256,256]{2,1,0:T(8,128)(2,1)} %constant.84.clone.y_hbm) | copy-start | bytes 786436
  7.2 119.4 %all-gather.2.cloned.1.call-start = ((), (), s32[]{:S(2)}) async-start(), calls=%async_computation.7 | async-start | bytes 2162688 | tf_op jit(solution)/shard_map/all_gather | solution.py:478
  9.9 27.8 %all-to-all-start = ((f32[16,16,128]{2,1,0:T(8,128)}), f32[16,16,128]{2,1,0:T(8,128)S(1)}, u32[]{:S(2)}, u32[]{:S(2)}) async-start(f32[16,16,128]{2,1,0:T(8,128)} %shard_map.184), calls=%async_computation | async-start | bytes 262144 | tf_op jit(solution)/shard_map/all_to_all | solution.py:458
  25.7 59.7 %copy-start.6 = (bf16[2,128,128]{2,1,0:T(8,128)(2,1)S(1)}, bf16[2,128,128]{2,1,0:T(8,128)(2,1)}, u32[]{:S(2)}) copy-start(bf16[2,128,128]{2,1,0:T(8,128)(2,1)} %constant.88.clone.modes_hbm.modes) | copy-start | bytes 196612
  25.7 59.7 %copy-start.14 = (f32[128,128]{1,0:T(8,128)S(1)}, f32[128,128]{1,0:T(8,128)}, u32[]{:S(2)}) copy-start(f32[128,128]{1,0:T(8,128)} %constant.90.clone.modes_t32) | copy-start | bytes 196612
  37.7 0.8 copy-start.5
  38.5 0.8 copy-start.10
  39.3 0.9 copy-start.12
  68.0 17.4 %all-to-all-start.2 = ((f32[16,32,128]{2,1,0:T(8,128)}), f32[16,32,128]{2,1,0:T(8,128)S(1)}, u32[]{:S(2)}, u32[]{:S(2)}) async-start(f32[16,32,128]{2,1,0:T(8,128)} %shard_map.186), calls=%async_computation.2 | async-start | bytes 524288 | tf_op jit(solution)/shard_map/all_to_all | solution.py:458
  71.7 42.0 %copy-start.7 = (bf16[2,256,512]{2,1,0:T(8,128)(2,1)S(1)}, bf16[2,256,512]{2,1,0:T(8,128)(2,1)}, u32[]{:S(2)}) copy-start(bf16[2,256,512]{2,1,0:T(8,128)(2,1)} %constant.85.clone.y_hbm) | copy-start | bytes 1572868
  71.7 42.0 %copy-start.11 = (bf16[2,128,128]{2,1,0:T(8,128)(2,1)S(1)}, bf16[2,128,128]{2,1,0:T(8,128)(2,1)}, u32[]{:S(2)}) copy-start(bf16[2,128,128]{2,1,0:T(8,128)(2,1)} %constant.89.clone.modes_t_hbm) | copy-start | bytes 196612
  71.7 42.0 %copy-start.13 = (bf16[2,128,128]{2,1,0:T(8,128)(2,1)S(1)}, bf16[2,128,128]{2,1,0:T(8,128)(2,1)}, u32[]{:S(2)}) copy-start(bf16[2,128,128]{2,1,0:T(8,128)(2,1)} %constant.87.clone.x_hbm) | copy-start | bytes 196612
  87.4 26.2 %all-to-all-start.3 = ((f32[32,64,128]{2,1,0:T(8,128)}), f32[32,64,128]{2,1,0:T(8,128)S(1)}, u32[]{:S(2)}, u32[]{:S(2)}) async-start(f32[32,64,128]{2,1,0:T(8,128)} %shard_map.187), calls=%async_computation.3 | async-start | bytes 2097152 | tf_op jit(solution)/shard_map/all_to_all | solution.py:458
  96.3 30.2 %copy-start.2 = (f32[1,128,256]{2,1,0:T(8,128)S(1)}, f32[1,128,256]{2,1,0:T(8,128)}, u32[]{:S(2)}) copy-start(f32[1,128,256]{2,1,0:T(8,128)} %param.17) | copy-start | bytes 393220
  96.4 30.2 %copy-start.3 = (f32[1,128,256]{2,1,0:T(8,128)S(1)}, f32[1,128,256]{2,1,0:T(8,128)}, u32[]{:S(2)}) copy-start(f32[1,128,256]{2,1,0:T(8,128)} %param.18) | copy-start | bytes 393220
  96.4 30.2 %copy-start.8 = (bf16[1,128,256]{2,1,0:T(8,128)(2,1)S(1)}, bf16[1,128,256]{2,1,0:T(8,128)(2,1)}, u32[]{:S(2)}) copy-start(bf16[1,128,256]{2,1,0:T(8,128)(2,1)} %param.21) | copy-start | bytes 196612
  113.6 23.7 %copy-start.4 = (bf16[2,256,256]{2,1,0:T(8,128)(2,1)S(1)}, bf16[2,256,256]{2,1,0:T(8,128)(2,1)}, u32[]{:S(2)}) copy-start(bf16[2,256,256]{2,1,0:T(8,128)(2,1)} %constant.83.clone.table_hbm.table) | copy-start | bytes 786436
  119.5 17.8 %all-to-all-start.4 = ((f32[16,16,128]{2,1,0:T(8,128)}), f32[16,16,128]{2,1,0:T(8,128)S(1)}, u32[]{:S(2)}, u32[]{:S(2)}) async-start(f32[16,16,128]{2,1,0:T(8,128)} %shard_map.188), calls=%async_computation.4 | async-start | bytes 262144 | tf_op jit(solution)/shard_map/all_to_all | solution.py:458
  126.6 1.6 copy-start
  128.2 9.2 %copy-start.1 = (bf16[32,128,256]{2,1,0:T(8,128)(2,1)S(1)}, bf16[32,128,256]{2,1,0:T(8,128)(2,1)}, u32[]{:S(2)}) copy-start(bf16[32,128,256]{2,1,0:T(8,128)(2,1)} %all-gather.2.cloned.1.call-done.occ_all) | copy-start | bytes 6291460
  158.7 12.9 %all-to-all-start.6 = ((f32[32,1,256]{2,1,0:T(1,128)}), f32[32,1,256]{2,1,0:T(1,128)S(1)}, u32[]{:S(2)}, u32[]{:S(2)}) async-start(f32[32,1,256]{2,1,0:T(1,128)} %get-tuple-element.14), calls=%async_computation.6 | async-start | bytes 65536 | tf_op jit(solution)/shard_map/all_to_all | solution.py:458
Sparse Core Ops, SparseCore 0:
  11.1 65.5 all-gather.1

commit v3 on v2

--- a/solution.py
+++ b/solution.py
@@ -28,6 +28,15 @@
     high = table.astype(np.float32).astype(ml_dtypes.bfloat16)
     low = (table - high.astype(np.float64)).astype(np.float32).astype(ml_dtypes.bfloat16)
     return np.stack([high, low])
+
+
+def left(table):
+    high, low = pieces(table)
+    return np.concatenate([np.concatenate([high, high], 1), np.concatenate([low, np.zeros_like(low)], 1)], 0)
+
+
+def right(table):
+    return left(table.T).T.copy()
 
 
 def angle(a, b):
@@ -58,10 +67,9 @@
     ).reshape(2 * N, 2 * N)
 
     cy, sy = np.cos(angle(signed, every)), np.sin(angle(signed, every))
-    y_inverse = np.tile(np.concatenate([cy, sy], axis=1), (4, 1))
-    y_forward = np.block(
-        [[np.tile(cy.T, (1, 4)), np.tile(-sy.T, (1, 4))], [np.tile(sy.T, (1, 4)), np.tile(cy.T, (1, 4))]]
-    )
+    high, low = pieces(np.concatenate([cy, sy], axis=1))
+    y_inverse = np.concatenate([high, high, low, np.zeros_like(low)], axis=0)
+    y_forward = np.concatenate(pieces(np.block([[cy.T, -sy.T], [sy.T, cy.T]])), axis=1)
 
     cx, sx = np.cos(angle(every, signed_x)), np.sin(angle(every, signed_x))
     x_inverse = 2.0 * NORM * np.block([[cx, -sx], [sx, cx]])
@@ -75,12 +83,14 @@
     return {
         "z_inverse": pieces(z_inverse),
         "z_forward": pieces(z_forward),
-        "y_inverse": pieces(y_inverse),
-        "y_forward": pieces(y_forward),
-        "x_inverse": pieces(x_inverse),
-        "x_forward": pieces(x_forward),
-        "modes": pieces(modes),
-        "modes_t": pieces(modes.T),
+        "y_inverse": y_inverse,
+        "y_forward": y_forward,
+        "x_inverse": left(x_inverse),
+        "x_forward": left(x_forward),
+        "modes_left": left(modes),
+        "modes_right": right(modes),
+        "modes_t_left": left(modes.T),
+        "modes_t_right": right(modes.T),
         "modes_t32": modes.T.astype(np.float32),
     }
 
@@ -101,14 +111,34 @@
     return dot(a[0], b[0], contract) + (dot(a[1], b[0], contract) + dot(a[0], b[1], contract))
 
 
-def call(body, out, *args, scratch=(), in_smem=(), in_hbm=(), vmem=16):
+def both(value, axis):
+    return jnp.concatenate(split(value), axis=axis)
+
+
+def times_left(table, value):
+    out = dot(table[...], both(value, 0) if value.dtype == F32 else value)
+    half = out.shape[0] // 2
+    return out[:half] + out[half:]
+
+
+def times_right(value, table):
+    out = dot(both(value, 1), table[...])
+    return out[:, :N] + out[:, N:]
+
+
+def call(body, out, *args, scratch=(), in_smem=(), in_hbm=(), vmem=16, late=()):
     space = lambda i: pltpu.SMEM if i in in_smem else pltpu.HBM if i in in_hbm else pltpu.VMEM
     in_vmem = pl.BlockSpec(memory_space=pltpu.VMEM)
     many = isinstance(out, (list, tuple))
+    n = len(args)
+    inner = (lambda *refs: body(*refs[:n], *refs[n + len(late) :])) if late else body
     return pl.pallas_call(
-        body,
+        inner,
         out_shape=out,
-        in_specs=[pl.BlockSpec(memory_space=space(i)) for i in range(len(args))],
+        in_specs=[
+            *(pl.BlockSpec(memory_space=space(i)) for i in range(len(args))),
+            *(pl.BlockSpec(memory_space=pltpu.HBM) for _ in late),
+        ],
         out_specs=[in_vmem] * len(out) if many else in_vmem,
         scratch_shapes=[
             *(pltpu.VMEM(args[i].shape, args[i].dtype) for i in in_hbm),
@@ -116,7 +146,7 @@
             *scratch,
         ],
         compiler_params=pltpu.CompilerParams(vmem_limit_bytes=vmem * MIB),
-    )(*args)
+    )(*args, *late)
 
 
 def fetch(sources, targets, sems):
@@ -148,50 +178,62 @@
 
 def planes_to_modes(
     recv, cells, y_hbm, x_hbm, occ_hbm, modes_hbm, modes_t_hbm,
-    out, y_table, x_table, occ, modes, modes_t, sems, r_high, r_low, d_high, d_low
+    out, y_table, x_table, occ, modes, modes_t, sems, field, spectrum
 ):
     copies = fetch(
         (y_hbm, x_hbm, occ_hbm, modes_hbm, modes_t_hbm), (y_table, x_table, occ, modes, modes_t), sems
     )
-    grid = jnp.zeros((256, 256), F32)
-    for src in range(SLABS):
-        lanes = slice(src * STK, (src + 1) * STK)
-        high, low = split(recv[src])
-        mask = q_mask_of(cells, lanes)
-        rows = [
-            (part.astype(F32)[:, None, :] * mask[None]).reshape(256, STK).astype(BF16)
-            for part in (high, low)
-        ]
-        chosen = pick_of(cells, lanes)
-        grid += dot(
-            jnp.concatenate(rows, axis=1), jnp.concatenate([chosen, chosen], axis=1), ((1,), (1,))
-        )
-    grid = split(grid)
+    grid = jnp.zeros((512, 256), F32)
+    for pair in range(SLABS // 2):
+        rows = []
+        for src in (2 * pair, 2 * pair + 1):
+            mask = q_mask_of(cells, slice(src * STK, (src + 1) * STK))
+            rows.append(
+                jnp.concatenate(
+                    [
+                        (part.astype(F32)[:, None, :] * mask[None]).reshape(256, STK).astype(BF16)
+                        for part in split(recv[src])
+                    ],
+                    axis=0,
+                )
+            )
+        chosen = pick_of(cells, slice(2 * pair * STK, 2 * (pair + 1) * STK))
+        grid += dot(jnp.concatenate(rows, axis=1), chosen, ((1,), (1,)))
+    high, low = split(grid[:256] + grid[256:])
+    first = lax.broadcasted_iota(jnp.int32, (1, N), 1) < HALF
+    swap_halves = lambda v: jnp.concatenate([v[:, HALF:], v[:, :HALF]], axis=1)
+    rows = []
+    for j in range(4):
+        h, l = (v[:, j // 2 * N : (j // 2 + 1) * N] for v in (high, low))
+        if j % 2 == 0:
+            l = swap_halves(l)
+        else:
+            h = swap_halves(h)
+        rows.append(jnp.concatenate([jnp.where(first, h, l), h], axis=1))
     for copy in copies:
         copy.wait()
-    lane_j = lax.broadcasted_iota(jnp.int32, (1, 256), 1) // HALF
+    mixed = dot(jnp.concatenate(rows, axis=0), y_table[...])
     for j in range(4):
-        own = (lane_j == j).astype(BF16)
-        mixed = dot3((grid[0] * own, grid[1] * own), (y_table[0], y_table[1]))
-        real = mixed[:N, :N] - mixed[N:, N:]
-        imag = mixed[:N, N:] + mixed[N:, :N]
+        block = mixed[j * 256 : (j + 1) * 256]
+        real = block[:N, :N] - block[N:, N:]
+        imag = block[:N, N:] + block[N:, :N]
         for c, part in enumerate((real, imag)):
-            high, low = split(part)
-            at = slice(c * HALF + j * 16, c * HALF + (j + 1) * 16)
-            for p in range(PL):
-                r_high[at, p * N : (p + 1) * N] = high[p * 16 : (p + 1) * 16]
-                r_low[at, p * N : (p + 1) * N] = low[p * 16 : (p + 1) * 16]
-    for p in range(PL):
-        lanes = slice(p * N, (p + 1) * N)
-        field = dot3((x_table[0], x_table[1]), (r_high[:, lanes], r_low[:, lanes]))
-        density = occ[0, p].astype(F32) * field[:N] + occ[1, p].astype(F32) * field[N:]
-        half = dot3(split(density), (modes_t[0], modes_t[1]))
-        d_high[:, lanes], d_low[:, lanes] = split(half)
-    for p in range(PL):
-        lanes = slice(p * N, (p + 1) * N)
-        out[pl.ds(p, N, stride=PL), :] = dot3(
-            (modes[0], modes[1]), (d_high[:, lanes], d_low[:, lanes])
-        )
+            for k, piece in enumerate(split(part)):
+                at = slice(k * N + c * HALF + j * 16, k * N + c * HALF + (j + 1) * 16)
+                for p in range(PL):
+                    field[at, p * N : (p + 1) * N] = piece[p * 16 : (p + 1) * 16]
+    for pair in range(PL // 2):
+        lanes = slice(pair * 2 * N, (pair + 1) * 2 * N)
+        values = times_left(x_table, field[:, lanes])
+        for i in range(2):
+            p = 2 * pair + i
+            at = slice(i * N, (i + 1) * N)
+            density = occ[0, p].astype(F32) * values[:N, at] + occ[1, p].astype(F32) * values[N:, at]
+            spectrum[:, p * N : (p + 1) * N] = both(times_right(density, modes_t), 0)
+    for pair in range(PL // 2):
+        values = times_left(modes, spectrum[:, pair * 2 * N : (pair + 1) * 2 * N])
+        for i in range(2):
+            out[pl.ds(2 * pair + i, N, stride=PL), :] = values[:, i * N : (i + 1) * N]
 
 
 def sum_bands(recv, to_slabs):
@@ -207,7 +249,7 @@
         jnp.concatenate([recv[i, a * PL : (a + 1) * PL, :] for i in range(SLABS)], axis=0)
         for a in range(AX)
     ]
-    spectrum = dot3((modes[0], modes[1]), split(jnp.concatenate(columns, axis=1)))
+    spectrum = times_left(modes, jnp.concatenate(columns, axis=1))
     freq = lambda i: jnp.where(i <= N // 2, i, i - N // 2)
     fz = freq(lax.broadcasted_iota(jnp.int32, (N, N), 0))
     fy = freq(lax.broadcasted_iota(jnp.int32, (N, N), 1))
@@ -231,89 +273,88 @@
         out[i] = tile
 
 
-def planes_from_modes(recv, modes, modes_t, p):
-    spectrum = jnp.concatenate(
-        [recv[pl.ds(i * PL + p, N, stride=2 * PL), :] for i in range(2)], axis=1
-    )
-    half = dot3((modes_t[0], modes_t[1]), split(spectrum))
-    half = jnp.concatenate([half[:, :N], half[:, N:]], axis=0)
-    plane = dot3(split(half), (modes[0], modes[1]))
-    return plane[:N], plane[N:]
-
-
 def planes_to_sticks(
-    recv, cells, modes_hbm, modes_t_hbm, xc_hbm, occ_hbm, x_hbm, y_hbm,
-    out, modes, modes_t, xc, occ, x_table, y_table, sems, l_high, l_low, grid
+    recv_hbm, modes_hbm, modes_t_hbm, xc_hbm, occ_hbm, x_hbm, y_hbm, cells,
+    out, recv, modes, modes_t, xc, occ, x_table, y_table, sems, half, rows, grid
 ):
     copies = fetch(
-        (modes_hbm, modes_t_hbm, xc_hbm, occ_hbm, x_hbm, y_hbm),
-        (modes, modes_t, xc, occ, x_table, y_table),
+        (recv_hbm, modes_hbm, modes_t_hbm, xc_hbm, occ_hbm, x_hbm, y_hbm),
+        (recv, modes, modes_t, xc, occ, x_table, y_table),
         sems,
     )
-    for copy in copies:
+    for copy in copies[:3]:
+        copy.wait()
+    for i in range(8):
+        at = slice(i * 256, (i + 1) * 256)
+        half[at, :] = times_right(recv[at, :], modes)
+    for copy in copies[3:]:
         copy.wait()
     for p in range(PL):
-        hartree, density = planes_from_modes(recv, modes, modes_t, p)
-        potential = hartree + xc[p] * density
+        value = jnp.concatenate(
+            [half[pl.ds(i * PL + p, N, stride=2 * PL), :] for i in range(2)], axis=1
+        )
+        value = times_left(modes_t, value)
+        potential = value[:, :N] + xc[p] * value[:, N:]
         product = jnp.concatenate(
             [potential * occ[0, p].astype(F32), potential * occ[1, p].astype(F32)], axis=1
         )
-        mixed = dot3((x_table[0], x_table[1]), split(product))
+        mixed = times_left(x_table, product)
         real = mixed[:HALF, :N] + mixed[HALF:, N:]
         imag = mixed[:HALF, N:] - mixed[HALF:, :N]
         for c, part in enumerate((real, imag)):
-            high, low = split(part)
-            for j in range(4):
-                at = slice(j * 2 * N + c * N, j * 2 * N + (c + 1) * N)
-                l_high[p * 16 : (p + 1) * 16, at] = high[j * 16 : (j + 1) * 16]
-                l_low[p * 16 : (p + 1) * 16, at] = low[j * 16 : (j + 1) * 16]
-    lane_j = lax.broadcasted_iota(jnp.int32, (1, 512), 1) // HALF % 4
-    spectrum = jnp.zeros((N, 512), F32)
-    for j in range(4):
-        at = slice(j * 2 * N, (j + 1) * 2 * N)
-        mixed = dot3((l_high[:, at], l_low[:, at]), (y_table[0], y_table[1]))
-        spectrum = jnp.where(lane_j == j, mixed, spectrum)
-    for part in range(2):
-        for h in range(2):
-            lanes = slice(part * 2 * N + h * N, part * 2 * N + (h + 1) * N)
-            grid[h, part * N : (part + 1) * N, :] = spectrum[:, lanes]
-    high, low = split(
+            for k, piece in enumerate(split(part)):
+                for j in range(4):
+                    at = slice(k * 512 + j * N + p * 16, k * 512 + j * N + (p + 1) * 16)
+                    rows[at, c * N : (c + 1) * N] = piece[j * 16 : (j + 1) * 16]
+    mixed = dot(rows[:512], y_table[...])
+    mixed = mixed[:, :N] + mixed[:, N:] + dot(rows[512:], y_table[:, :N])
+    by_j = [mixed[j * N : (j + 1) * N] for j in range(4)]
+    first = lax.broadcasted_iota(jnp.int32, (1, N), 1) < HALF
+    for h in range(2):
+        even, odd = by_j[2 * h], by_j[2 * h + 1]
+        grid[h, :N, :] = jnp.where(first, even, pltpu.roll(odd, HALF, 1))
+        grid[h, N:, :] = jnp.where(first, pltpu.roll(even, HALF, 1), odd)
+    values = both(
         jnp.concatenate(
             [
                 jnp.concatenate([grid[h, pl.ds(q, 16, stride=16), :] for h in range(2)], axis=1)
                 for q in range(16)
             ],
             axis=0,
-        )
-    )
-    for dst in range(SLABS):
-        lanes = slice(dst * STK, (dst + 1) * STK)
-        pick = pick_of(cells, lanes)
+        ),
+        0,
+    )
+    for pair in range(SLABS // 2):
+        lanes = slice(2 * pair * STK, 2 * (pair + 1) * STK)
         mask = q_mask_of(cells, lanes)
-        chosen = dot(high, pick) + dot(low, pick)
-        total = chosen[:16] * mask[:1]
-        for q in range(1, 16):
-            total = total + chosen[q * 16 : (q + 1) * 16] * mask[q : q + 1]
-        out[dst] = total
+        chosen = dot(values, pick_of(cells, lanes))
+        total = jnp.zeros((2 * PL, 2 * STK), F32)
+        for q in range(16):
+            at = slice(q * 16, (q + 1) * 16)
+            total = total + (chosen[:256][at] + chosen[256:][at]) * mask[q : q + 1]
+        out[2 * pair] = total[:, :STK]
+        out[2 * pair + 1] = total[:, STK:]
 
 
 CHUNK = 8
 
 
 def orbitals(hbm, held, sems):
+    parts = BANDS // 2 // CHUNK
     copies = [
         pltpu.make_async_copy(
-            hbm.at[pl.ds(i * CHUNK, CHUNK)], held.at[pl.ds(i * CHUNK, CHUNK)], sems.at[i]
+            ref.at[pl.ds(i * CHUNK, CHUNK)], to.at[pl.ds(i * CHUNK, CHUNK)], sems.at[h * parts + i]
         )
-        for i in range(BANDS // CHUNK)
+        for h, (ref, to) in enumerate(zip(hbm, held))
+        for i in range(parts)
     ]
     for copy in copies:
         copy.start()
 
-    def at(w):
-        if w % CHUNK == 0:
-            copies[w // CHUNK].wait()
-        return held[w].astype(F32)
+    def at(k):
+        if k % CHUNK == 0:
+            copies[k // CHUNK].wait()
+        return held[k * 2 // BANDS][k % (BANDS // 2)].astype(F32)
 
     return at
 
@@ -354,8 +395,8 @@
     return jnp.where(lane() < 2 * BANDS, row, 0.0)
 
 
-def fixed_overlaps(occ_all, resp, prev, occ, out, held, sems, sums):
-    at = orbitals(occ_all, held, sems)
+def fixed_overlaps(low, high, resp, prev, occ, out, low_held, high_held, sems, sums):
+    at = orbitals((low, high), (low_held, high_held), sems)
     rows = overlap_rows(at, [resp[...], prev[...], occ[...].astype(F32)], sums)
     for i, row in enumerate(rows):
         out[i : i + 1, :] = row
@@ -363,9 +404,10 @@
 
 
 def apply_and_overlap(
-    recv, table, scalars, resp, prev, fixed, occ_all, applied_out, part_out, held, sems, sums
+    recv, table, scalars, resp, prev, fixed, low, high,
+    applied_out, part_out, low_held, high_held, sems, sums
 ):
-    at = orbitals(occ_all, held, sems)
+    at = orbitals((low, high), (low_held, high_held), sems)
     values = recv[...].reshape(2 * N, STK).T
     applied = dot3(split(values), (table[0], table[1]))
     applied_out[...] = applied
@@ -394,7 +436,7 @@
         part_out[i] = row
 
 
-def join_slabs(recv, margin_out, part_out):
+def join_slabs(where, recv, margin_out, place_out, part_out):
     rows = [jnp.concatenate([recv[i][:, j * N : (j + 1) * N] for i in range(SLABS)], axis=0) for j in range(3)]
     add = lambda v: jnp.sum(v, axis=0, keepdims=True)
     norms, firsts, slopes, lefts = (rows[2][:, 2 * BANDS + i : 2 * BANDS + i + 1] for i in range(4))
@@ -408,10 +450,17 @@
     with_resp = add(rows[2])
     inner = lambda x: jnp.sum(weights * lower(x), axis=1, keepdims=True)
     removed_resp = inner(with_resp)
-    margin_out[...] = head
+    place_out[...] = head
+    i = lax.broadcasted_iota(jnp.int32, (N, 1), 0)
+    k = i % BANDS
+    band = (k % 4 * 2 + k // 4 % 4 * 8 + k // 16) ^ where[0]
+    to_band = (i // BANDS * BANDS + band == lane()).astype(F32)
+    heads = jnp.concatenate([head, jnp.where(lane() < 2 * BANDS, weights, head)], axis=0)
+    heads = jnp.dot(heads, to_band, precision=lax.Precision.HIGHEST, preferred_element_type=F32)
+    margin_out[...] = heads[:1]
     row = jnp.concatenate(
         [
-            jnp.where(lane() < 2 * BANDS, weights, head),
+            heads[1:],
             with_lanes(
                 jnp.zeros((1, N), F32),
                 0,
@@ -424,8 +473,8 @@
         part_out[i] = row
 
 
-def remove(margin, scalars, resp, prev, applied, occ_all, rest_out, held, sems):
-    at = orbitals(occ_all, held, sems)
+def remove(margin, scalars, resp, prev, applied, low, high, rest_out, low_held, high_held, sems):
+    at = orbitals((low, high), (low_held, high_held), sems)
     weights = margin[...].astype(BF16).astype(F32)
     plain = jnp.zeros((STK, 2 * N), F32)
     turned = jnp.zeros((STK, 2 * N), F32)
@@ -458,6 +507,10 @@
     return lax.all_to_all(value, axis, 0, 0, tiled=True)
 
 
+def across(blocks, bit):
+    return lax.ppermute(blocks, "band", [(i, i ^ bit) for i in range(BANDS)])
+
+
 def after(value, other):
     return lax.optimization_barrier((value, other))
 
@@ -475,59 +528,74 @@
     stick_map, _ = after(stick_map, field)
     gx = stick_map // N % HALF
     cells = (gx // 4 * 256 + gx % 4 * HALF + stick_map % HALF).reshape(1, STICKS)
-    occ_all = lax.all_gather(occupied.reshape(1, STK, 2 * N), "band", axis=0, tiled=True)
+    own, cells = after(occupied.reshape(1, STK, 2 * N), cells)
+    x1, x3 = across(own, 2), across(own, 6)
     field = swap(field, "slab")
     bf_scratch = lambda *dims: pltpu.VMEM(dims, BF16)
     partial = call(
         planes_to_modes,
         shape(N * PL, N),
-        field, cells, t["y_inverse"], t["x_inverse"], occ_planes, t["modes"], t["modes_t"],
+        field, cells, t["y_inverse"], t["x_inverse"], occ_planes, t["modes_left"], t["modes_t_right"],
         in_hbm=(2, 3, 4, 5, 6),
-        scratch=[bf_scratch(N, PL * N) for _ in range(4)],
+        late=(x1, x3),
+        scratch=[bf_scratch(2 * N, PL * N), bf_scratch(2 * N, PL * N)],
     )
     partial = swap(partial.reshape(BANDS, AX * PL, N), "band")
-    total = call(sum_bands, shape(SLABS, AX * PL, N), partial)
+    x2 = across(own, 4)
+    total = call(sum_bands, shape(SLABS, AX * PL, N), partial, late=(x2,))
+    row = jnp.concatenate([own, x1, x2, x3], axis=0)
+    y1, y3 = across(row, 8), across(row, 24)
     columns = swap(total, "slab")
     hartree = call(
-        solve_z, shape(BANDS, 2 * AX * PL, N), where, columns, t["modes"], t["modes_t32"], in_smem=(0,)
-    )
+        solve_z, shape(BANDS, 2 * AX * PL, N), where, columns, t["modes_left"], t["modes_t32"],
+        in_smem=(0,),
+        late=(y1, y3),
+    )
+    y2 = across(row, 16)
     xc_planes, _ = after(xc_kernel, hartree)
     xc_planes = xc_planes.reshape(PL, N, N)
     hartree = swap(hartree, "band")
     chosen = call(
         planes_to_sticks,
         shape(SLABS, 2 * PL, STK),
-        hartree.reshape(2 * N * PL, N), cells,
-        t["modes"], t["modes_t"], xc_planes, occ_planes, t["x_forward"], t["y_forward"],
-        in_hbm=(2, 3, 4, 5, 6, 7),
-        scratch=[bf_scratch(N, 8 * N), bf_scratch(N, 8 * N), pltpu.VMEM((2, 2 * N, N), F32)],
-    )
+        hartree.reshape(2 * N * PL, N), t["modes_right"], t["modes_t_left"],
+        xc_planes, occ_planes, t["x_forward"], t["y_forward"], cells,
+        in_hbm=(0, 1, 2, 3, 4, 5, 6),
+        vmem=60,
+        late=(y2,),
+        scratch=[pltpu.VMEM((2 * N * PL, N), F32), bf_scratch(8 * N, 2 * N), pltpu.VMEM((2, 2 * N, N), F32)],
+    )
+    low = jnp.concatenate([row, y1, y2, y3], axis=0)
+    high = across(low, 1)
     gathered = swap(chosen, "slab")
     fixed = call(
         fixed_overlaps,
         shape(8, N),
-        occ_all, resp, prev, occupied.reshape(STK, 2 * N),
-        in_hbm=(0,),
+        low, high, resp, prev, occupied.reshape(STK, 2 * N),
+        in_hbm=(0, 1),
         scratch=[pltpu.VMEM((3, N, N), F32)],
     )
     scalars = jnp.stack([band_gap[0], earlier_beta[0]])
     applied, parts = call(
         apply_and_overlap,
         [shape(STK, 2 * N), shape(SLABS, 1, 3 * N)],
-        gathered, t["z_forward"], scalars, resp, prev, fixed, occ_all,
+        gathered, t["z_forward"], scalars, resp, prev, fixed, low, high,
         in_smem=(2,),
-        in_hbm=(6,),
+        in_hbm=(6, 7),
         scratch=[pltpu.VMEM((2, N, N), F32)],
     )
-    margin, parts = call(
-        join_slabs, [shape(1, N), shape(BANDS, 1, 2 * N)], swap(parts, "slab")
+    margin, placed_margin, parts = call(
+        join_slabs,
+        [shape(1, N), shape(1, N), shape(BANDS, 1, 2 * N)],
+        where, swap(parts, "slab"),
+        in_smem=(0,),
     )
     rest = call(
         remove,
         shape(STK, 2 * N),
-        margin, scalars, resp, prev, applied, occ_all,
+        placed_margin, scalars, resp, prev, applied, low, high,
         in_smem=(1,),
-        in_hbm=(5,),
+        in_hbm=(5, 6),
     )
     next_vector, coefficients = call(
         finish, [shape(STK, 2 * N), shape(1, N)], swap(parts, "band"), resp, rest

time: 181 us -> 171 us (0.945)
  starting transfers between devices: 39.6 us -> 79.6 us
  blocking collectives: 39.8 us -> 17.7 us
  between operations: 15.5 us -> 2.35 us
  waiting for transfers between devices: 52 us -> 42.6 us
  local copies, waits for them, and re-layouts: 7.77 us -> 3.01 us
    ppermute x0 -> x7, starting transfers between devices: none -> 22.9 us  [across(): return lax.ppermute(blocks, 'band', [(i, i ^ bit) for i in range(BANDS)])]
    all_to_all x2 -> x1, blocking collectives: 39.8 us -> 17.7 us  [swap(): return lax.all_to_all(value, axis, 0, 0, tiled=True)]
    all_to_all x5 -> x6, waiting for transfers between devices: 51.4 us -> 31.3 us  [swap(): return lax.all_to_all(value, axis, 0, 0, tiled=True)]
    all_to_all x5 -> x6, starting transfers between devices: 39.5 us -> 56.7 us  [swap(): return lax.all_to_all(value, axis, 0, 0, tiled=True)]
    ppermute x0 -> x7, waiting for transfers between devices: none -> 11.4 us  [across(): return lax.ppermute(blocks, 'band', [(i, i ^ bit) for i in range(BANDS)])]
    unnamed x32 -> x38, local copies, waits for them, and re-layouts: 6.59 us -> 1.82 us
  transfers between devices with their start and end apart: 6 -> 13, of which waited for: 5 -> 10; matrix products, arithmetic and copies ran while one was open for 2% -> 1% of each run, Pallas kernels for 11% -> 7%
where the time goes in v3:
time: 171 us; the launch traced here: 170 us
  starting transfers between devices  79.6 us (47%)
  waiting for transfers between devices  42.6 us (25%)
  Pallas kernels  24.3 us (14%)
  blocking collectives  17.7 us (10%)
  local copies, waits for them, and re-layouts  3.01 us (2%)
  between operations  2.35 us (1%)
    all_to_all x6, starting transfers between devices, swap(): return lax.all_to_all(value, axis, 0, 0, tiled=True)  56.7 us
    all_to_all x6, waiting for transfers between devices, swap(): return lax.all_to_all(value, axis, 0, 0, tiled=True)  31.3 us
    pallas_call x10, Pallas kernels, call(): pl.pallas_call(inner, out_shape=out, in_specs=[*(pl.BlockSpec(memory_spac...  24.3 us
    ppermute x7, starting transfers between devices, across(): return lax.ppermute(blocks, 'band', [(i, i ^ bit) for i in range(BANDS)])  22.9 us
    all_to_all x1, blocking collectives, swap(): return lax.all_to_all(value, axis, 0, 0, tiled=True)  17.7 us
    ppermute x7, waiting for transfers between devices, across(): return lax.ppermute(blocks, 'band', [(i, i ^ bit) for i in range(BANDS)])  11.4 us
  transfers between devices with their start and end apart: 13, of which 10 were waited for; matrix products, arithmetic and copies ran while one was open for 1% of the time, Pallas kernels for 7%

profile of v3, /device:TPU:1, one launch (start us, length us, event | category | flops | bytes accessed | tf_op | source)
XLA Modules:
  0.0 169.8 jit_solution(7087206302401266279)
XLA Ops:
  0.6 2.0 %shard_map.202 = f32[16,16,128]{2,1,0:T(8,128)} custom-call(f32[128,256]{1,0:T(8,128)} %bitcast.23, bf16[2,256,256]{2,1,0:T(8,128)(2,1)} %constant.87.clone.table_hbm.table), custom_call_target="tpu_custom_call" | custom-call | tf_op jit(solution)/shard_map/pallas_call | solution.py:135
  2.7 15.9 %all-to-all-start = ((f32[16,16,128]{2,1,0:T(8,128)}), f32[16,16,128]{2,1,0:T(8,128)S(1)}, u32[]{:S(2)}, u32[]{:S(2)}) async-start(f32[16,16,128]{2,1,0:T(8,128)} %shard_map.202), calls=%async_computation | async-start | bytes 262144 | tf_op jit(solution)/shard_map/all_to_all | solution.py:507
  18.7 4.4 %collective-permute-start.1 = (bf16[1,128,256]{2,1,0:T(8,128)(2,1)S(1)}, bf16[1,128,256]{2,1,0:T(8,128)(2,1)S(1)}, u32[]{:S(2)}, u32[]{:S(2)}) collective-permute-start(bf16[1,128,256]{2,1,0:T(8,128)(2,1)S(1)} %copy-done.6), channel_id=1, source_target_pairs={{0,96},{16,112},{32,64},{48,80},{64,32},{80,48},{96,0},{112,16},{1... | collective-permute-start | bytes 196616 | tf_op jit(solution)/shard_map/ppermute | solution.py:511
  23.1 1.9 %collective-permute-start = (bf16[1,128,256]{2,1,0:T(8,128)(2,1)S(1)}, bf16[1,128,256]{2,1,0:T(8,128)(2,1)S(1)}, u32[]{:S(2)}, u32[]{:S(2)}) collective-permute-start(bf16[1,128,256]{2,1,0:T(8,128)(2,1)S(1)} %copy-done.6), channel_id=1, source_target_pairs={{0,32},{16,48},{32,0},{48,16},{64,96},{80,112},{96,64},{112,80},{1... | collective-permute-start | bytes 196616 | tf_op jit(solution)/shard_map/ppermute | solution.py:511
  25.2 3.2 %collective-permute-done.refs_7_ = bf16[1,128,256]{2,1,0:T(8,128)(2,1)S(1)} collective-permute-done((bf16[1,128,256]{2,1,0:T(8,128)(2,1)S(1)}, bf16[1,128,256]{2,1,0:T(8,128)(2,1)S(1)}, u32[]{:S(2)}, u32[]{:S(2)}) %collective-permute-start) | collective-permute-done | bytes 65568 | tf_op jit(solution)/shard_map/ppermute | solution.py:511
  28.4 2.2 %all-to-all-done.refs_0_ = f32[16,16,128]{2,1,0:T(8,128)S(1)} async-done(((f32[16,16,128]{2,1,0:T(8,128)}), f32[16,16,128]{2,1,0:T(8,128)S(1)}, u32[]{:S(2)}, u32[]{:S(2)}) %all-to-all-start) | async-done | bytes 131104 | tf_op jit(solution)/shard_map/all_to_all | solution.py:507
  30.6 4.7 %shard_map.203 = f32[1024,128]{1,0:T(8,128)} custom-call(f32[16,16,128]{2,1,0:T(8,128)S(1)} %all-to-all-done.refs_0_, s32[1,2048]{1,0:T(1,128)S(1)} %bitcast.32, bf16[256,256]{1,0:T(8,128)(2,1)S(1)} %copy-done.8, bf16[512,256]{1,0:T(8,128)(2,1)S(1)} %copy-done.5, bf16[2,8,128,128]{3,2,1,0:T(8,128)(2,1)S(1)} %copy.28, bf16[256,256]{1,0:T(8,128)(2,1)S(1)} %copy-done.4, ...), custom_call_target="tpu_custom_call" | custom-call | tf_op jit(solution)/shard_map/pallas_call | solution.py:135
  35.4 10.8 %all-to-all-start.1 = ((f32[32,32,128]{2,1,0:T(8,128)}), f32[32,32,128]{2,1,0:T(8,128)S(1)}, u32[]{:S(2)}, u32[]{:S(2)}) async-start(f32[32,32,128]{2,1,0:T(8,128)} %bitcast.4), calls=%async_computation.1 | async-start | bytes 1048576 | tf_op jit(solution)/shard_map/all_to_all | solution.py:507
  46.1 4.8 %collective-permute-start.2 = (bf16[1,128,256]{2,1,0:T(8,128)(2,1)S(1)}, bf16[1,128,256]{2,1,0:T(8,128)(2,1)S(1)}, u32[]{:S(2)}, u32[]{:S(2)}) collective-permute-start(bf16[1,128,256]{2,1,0:T(8,128)(2,1)S(1)} %copy-done.6), channel_id=1, source_target_pairs={{0,64},{16,80},{32,96},{48,112},{64,0},{80,16},{96,32},{112,48},{1... | collective-permute-start | bytes 196616 | tf_op jit(solution)/shard_map/ppermute | solution.py:511
  50.9 6.0 %collective-permute-done.2.refs_1_ = bf16[1,128,256]{2,1,0:T(8,128)(2,1)S(1)} collective-permute-done((bf16[1,128,256]{2,1,0:T(8,128)(2,1)S(1)}, bf16[1,128,256]{2,1,0:T(8,128)(2,1)S(1)}, u32[]{:S(2)}, u32[]{:S(2)}) %collective-permute-start.2) | collective-permute-done | bytes 65568 | tf_op jit(solution)/shard_map/ppermute | solution.py:511
  58.4 5.7 %all-to-all-start.2 = ((f32[16,32,128]{2,1,0:T(8,128)}), f32[16,32,128]{2,1,0:T(8,128)S(1)}, u32[]{:S(2)}, u32[]{:S(2)}) async-start(f32[16,32,128]{2,1,0:T(8,128)} %shard_map.204), calls=%async_computation.2 | async-start | bytes 524288 | tf_op jit(solution)/shard_map/all_to_all | solution.py:507
  64.3 3.6 %collective-permute-start.4 = (bf16[4,128,256]{2,1,0:T(8,128)(2,1)S(1)}, bf16[4,128,256]{2,1,0:T(8,128)(2,1)S(1)}, u32[]{:S(2)}, u32[]{:S(2)}) collective-permute-start(bf16[4,128,256]{2,1,0:T(8,128)(2,1)S(1)} %get-tuple-element.29), channel_id=1, source_target_pairs={{0,384},{16,400},{32,416},{48,432},{64,448},{80,464},{96,480},{112... | collective-permute-start | bytes 786440 | tf_op jit(solution)/shard_map/ppermute | solution.py:511
  67.9 1.9 %collective-permute-start.3 = (bf16[4,128,256]{2,1,0:T(8,128)(2,1)S(1)}, bf16[4,128,256]{2,1,0:T(8,128)(2,1)S(1)}, u32[]{:S(2)}, u32[]{:S(2)}) collective-permute-start(bf16[4,128,256]{2,1,0:T(8,128)(2,1)S(1)} %get-tuple-element.29), channel_id=1, source_target_pairs={{0,128},{16,144},{32,160},{48,176},{64,192},{80,208},{96,224},{112... | collective-permute-start | bytes 786440 | tf_op jit(solution)/shard_map/ppermute | solution.py:511
  69.8 4.1 %collective-permute-start.5 = (bf16[4,128,256]{2,1,0:T(8,128)(2,1)S(1)}, bf16[4,128,256]{2,1,0:T(8,128)(2,1)S(1)}, u32[]{:S(2)}, u32[]{:S(2)}) collective-permute-start(bf16[4,128,256]{2,1,0:T(8,128)(2,1)S(1)} %get-tuple-element.29), channel_id=1, source_target_pairs={{0,256},{16,272},{32,288},{48,304},{64,320},{80,336},{96,352},{112... | collective-permute-start | bytes 786440 | tf_op jit(solution)/shard_map/ppermute | solution.py:511
  74.5 1.7 collective-permute-done.3.refs_4_
  76.1 1.8 %all-to-all-done.2.refs_1_ = f32[16,32,128]{2,1,0:T(8,128)S(1)} async-done(((f32[16,32,128]{2,1,0:T(8,128)}), f32[16,32,128]{2,1,0:T(8,128)S(1)}, u32[]{:S(2)}, u32[]{:S(2)}) %all-to-all-start.2) | async-done | bytes 262176 | tf_op jit(solution)/shard_map/all_to_all | solution.py:507
  78.0 2.0 %shard_map.205 = f32[32,64,128]{2,1,0:T(8,128)} custom-call(s32[2]{0:T(128)S(1)} %pad_add_fusion.refs_0_.where, f32[16,32,128]{2,1,0:T(8,128)S(1)} %all-to-all-done.2.refs_1_, bf16[256,256]{1,0:T(8,128)(2,1)S(1)} %copy-done.4, f32[128,128]{1,0:T(8,128)S(1)} %copy-done.10, bf16[4,128,256]{2,1,0:T(8,128)(2,1)S(1)} %collective-permute-done.3.refs_4_, ...), custom_call_target="tpu_custom_call" | custom-call | tf_op jit(solution)/shard_map/pallas_call | solution.py:135
  79.9 10.0 %all-to-all-start.3 = ((f32[32,64,128]{2,1,0:T(8,128)}), f32[32,64,128]{2,1,0:T(8,128)}, u32[]{:S(2)}, u32[]{:S(2)}) async-start(f32[32,64,128]{2,1,0:T(8,128)} %shard_map.205), calls=%async_computation.3 | async-start | bytes 2097152 | tf_op jit(solution)/shard_map/all_to_all | solution.py:507
  90.7 2.2 %collective-permute-start.6 = (bf16[16,128,256]{2,1,0:T(8,128)(2,1)S(1)}, bf16[16,128,256]{2,1,0:T(8,128)(2,1)S(1)}, u32[]{:S(2)}, u32[]{:S(2)}) collective-permute-start(bf16[16,128,256]{2,1,0:T(8,128)(2,1)S(1)} %constant_dynamic-update-slice_fusion.4.low), channel_id=1, source_target_pairs={{0,16},{16,0},{32,48},{48,32},{64,80},{80,64},{96,112},{112,96},{1... | collective-permute-start | bytes 3145736 | tf_op jit(solution)/shard_map/ppermute | solution.py:511
  92.9 0.9 copy.27
  93.8 13.3 %all-to-all-done.3 = f32[32,64,128]{2,1,0:T(8,128)} async-done(((f32[32,64,128]{2,1,0:T(8,128)}), f32[32,64,128]{2,1,0:T(8,128)}, u32[]{:S(2)}, u32[]{:S(2)}) %all-to-all-start.3) | async-done | bytes 1048608 | tf_op jit(solution)/shard_map/all_to_all | solution.py:507
  107.2 5.1 %shard_map.206 = f32[16,16,128]{2,1,0:T(8,128)} custom-call(f32[2048,128]{1,0:T(8,128)} %bitcast.5.refs_0_, bf16[256,256]{1,0:T(8,128)(2,1)} %constant.93.clone.refs_1_, bf16[256,256]{1,0:T(8,128)(2,1)} %constant.94.clone.refs_2_, f32[8,128,128]{2,1,0:T(8,128)} %bitcast.34, bf16[2,8,128,128]{3,2,1,0:T(8,128)(2,1)} %copy-done, ...), custom_call_target="tpu_custom_call" | custom-call | tf_op jit(solution)/shard_map/pallas_call | solution.py:135
  112.3 8.7 %all-to-all-start.4 = ((f32[16,16,128]{2,1,0:T(8,128)}), f32[16,16,128]{2,1,0:T(8,128)S(1)}, u32[]{:S(2)}, u32[]{:S(2)}) async-start(f32[16,16,128]{2,1,0:T(8,128)} %shard_map.206), calls=%async_computation.4 | async-start | bytes 262144 | tf_op jit(solution)/shard_map/all_to_all | solution.py:507
  122.5 2.3 %shard_map.207.fixed = f32[8,128]{1,0:T(8,128)S(1)} custom-call(bf16[16,128,256]{2,1,0:T(8,128)(2,1)S(1)} %constant_dynamic-update-slice_fusion.4.low, bf16[16,128,256]{2,1,0:T(8,128)(2,1)S(1)} %collective-permute-done.6.high, f32[128,256]{1,0:T(8,128)S(1)} %bitcast.24, f32[128,256]{1,0:T(8,128)S(1)} %bitcast.28, bf16[128,256]{1,0:T(8,128)(2,1)S(1)} %bitcast.31), custom_call_target="tpu_custom_call" | custom-call | tf_op jit(solution)/shard_map/pallas_call | solution.py:135
  124.7 8.4 %all-to-all-done.4.recv = f32[16,16,128]{2,1,0:T(8,128)S(1)} async-done(((f32[16,16,128]{2,1,0:T(8,128)}), f32[16,16,128]{2,1,0:T(8,128)S(1)}, u32[]{:S(2)}, u32[]{:S(2)}) %all-to-all-start.4) | async-done | bytes 131104 | tf_op jit(solution)/shard_map/all_to_all | solution.py:507
  133.2 2.6 %shard_map.208 = (f32[128,256]{1,0:T(8,128)S(1)}, f32[16,1,384]{2,1,0:T(1,128)S(1)}) custom-call(f32[16,16,128]{2,1,0:T(8,128)S(1)} %all-to-all-done.4.recv, bf16[2,256,256]{2,1,0:T(8,128)(2,1)S(1)} %copy-done.3, f32[2]{0:T(128)S(1)} %pad_maximum_fusion.scalars, f32[128,256]{1,0:T(8,128)S(1)} %bitcast.25, f32[128,256]{1,0:T(8,128)S(1)} %bitcast.29, ...), custom_call_target="tpu_custom_call" | custom-call | tf_op jit(solution)/shard_map/pallas_call | solution.py:135
  135.8 17.7 %all_to_all.35.recv = f32[16,1,384]{2,1,0:T(1,128)S(1)} all-to-all(f32[16,1,384]{2,1,0:T(1,128)S(1)} %get-tuple-element.18), channel_id=1, replica_groups=mesh['band'=32,'slab'=16] {'slab'}, dimensions={0} | all-to-all | bytes 49152 | tf_op jit(solution)/shard_map/all_to_all | solution.py:507
  153.5 1.6 shard_map.209
  155.1 5.6 %all-to-all-start.6 = ((f32[32,1,256]{2,1,0:T(1,128)}), f32[32,1,256]{2,1,0:T(1,128)S(1)}, u32[]{:S(2)}, u32[]{:S(2)}) async-start(f32[32,1,256]{2,1,0:T(1,128)} %get-tuple-element.19), calls=%async_computation.6 | async-start | bytes 65536 | tf_op jit(solution)/shard_map/all_to_all | solution.py:507
  161.4 2.0 %shard_map.210.rest = f32[128,256]{1,0:T(8,128)S(1)} custom-call(f32[1,128]{1,0:T(1,128)S(1)} %get-tuple-element.20.margin, f32[2]{0:T(128)S(1)} %pad_maximum_fusion.scalars, f32[128,256]{1,0:T(8,128)S(1)} %bitcast.26, f32[128,256]{1,0:T(8,128)S(1)} %bitcast.30, f32[128,256]{1,0:T(8,128)S(1)} %get-tuple-element.21.applied, ...), custom_call_target="tpu_custom_call" | custom-call | tf_op jit(solution)/shard_map/pallas_call | solution.py:135
  163.4 4.7 %all-to-all-done.6.recv = f32[32,1,256]{2,1,0:T(1,128)S(1)} async-done(((f32[32,1,256]{2,1,0:T(1,128)}), f32[32,1,256]{2,1,0:T(1,128)S(1)}, u32[]{:S(2)}, u32[]{:S(2)}) %all-to-all-start.6) | async-done | bytes 32800 | tf_op jit(solution)/shard_map/all_to_all | solution.py:507
  168.0 1.3 shard_map.211
  (50 shorter events, 4.4 us)
Async XLA Ops:
  0.6 24.4 %copy-start.12 = (bf16[1,2,8,16384]{3,2,1,0:T(8,128)(2,1)S(1)}, bf16[1,2,8,16384]{3,2,1,0:T(8,128)(2,1)}, u32[]{:S(2)}) copy-start(bf16[1,2,8,16384]{3,2,1,0:T(8,128)(2,1)} %param.24) | copy-start | bytes 1572868
  2.7 15.9 %copy-start.14 = (s32[2048]{0:T(1024)S(1)}, s32[2048]{0:T(1024)}, u32[]{:S(2)}) copy-start(s32[2048]{0:T(1024)} %param.26) | copy-start | bytes 24580
  2.7 16.0 %copy-start.6 = (bf16[1,128,256]{2,1,0:T(8,128)(2,1)S(1)}, bf16[1,128,256]{2,1,0:T(8,128)(2,1)}, u32[]{:S(2)}) copy-start(bf16[1,128,256]{2,1,0:T(8,128)(2,1)} %param.23) | copy-start | bytes 196612
  2.7 27.9 %all-to-all-start = ((f32[16,16,128]{2,1,0:T(8,128)}), f32[16,16,128]{2,1,0:T(8,128)S(1)}, u32[]{:S(2)}, u32[]{:S(2)}) async-start(f32[16,16,128]{2,1,0:T(8,128)} %shard_map.202), calls=%async_computation | async-start | bytes 262144 | tf_op jit(solution)/shard_map/all_to_all | solution.py:507
  18.6 12.0 %copy-start.9 = (s32[2048]{0:T(1024)}, s32[2048]{0:T(1024)S(1)}, u32[]{:S(2)}) copy-start(s32[2048]{0:T(1024)S(1)} %fusion.4) | copy-start | bytes 24580
  18.7 6.5 %collective-permute-start.1 = (bf16[1,128,256]{2,1,0:T(8,128)(2,1)S(1)}, bf16[1,128,256]{2,1,0:T(8,128)(2,1)S(1)}, u32[]{:S(2)}, u32[]{:S(2)}) collective-permute-start(bf16[1,128,256]{2,1,0:T(8,128)(2,1)S(1)} %copy-done.6), channel_id=1, source_target_pairs={{0,96},{16,112},{32,64},{48,80},{64,32},{80,48},{96,0},{112,16},{1... | collective-permute-start | bytes 196616 | tf_op jit(solution)/shard_map/ppermute | solution.py:511
  23.1 5.3 %collective-permute-start = (bf16[1,128,256]{2,1,0:T(8,128)(2,1)S(1)}, bf16[1,128,256]{2,1,0:T(8,128)(2,1)S(1)}, u32[]{:S(2)}, u32[]{:S(2)}) collective-permute-start(bf16[1,128,256]{2,1,0:T(8,128)(2,1)S(1)} %copy-done.6), channel_id=1, source_target_pairs={{0,32},{16,48},{32,0},{48,16},{64,96},{80,112},{96,64},{112,80},{1... | collective-permute-start | bytes 196616 | tf_op jit(solution)/shard_map/ppermute | solution.py:511
  25.0 5.6 %copy-start.4 = (bf16[256,256]{1,0:T(8,128)(2,1)S(1)}, bf16[256,256]{1,0:T(8,128)(2,1)}, u32[]{:S(2)}) copy-start(bf16[256,256]{1,0:T(8,128)(2,1)} %constant.92.clone.refs_5_.refs_2_) | copy-start | bytes 393220
  25.0 5.6 %copy-start.5 = (bf16[512,256]{1,0:T(8,128)(2,1)S(1)}, bf16[512,256]{1,0:T(8,128)(2,1)}, u32[]{:S(2)}) copy-start(bf16[512,256]{1,0:T(8,128)(2,1)} %constant.90.clone.refs_3_) | copy-start | bytes 786436
  25.0 5.6 %copy-start.7 = (bf16[256,256]{1,0:T(8,128)(2,1)S(1)}, bf16[256,256]{1,0:T(8,128)(2,1)}, u32[]{:S(2)}) copy-start(bf16[256,256]{1,0:T(8,128)(2,1)} %constant.95.clone.refs_6_) | copy-start | bytes 393220
  25.0 5.6 %copy-start.8 = (bf16[256,256]{1,0:T(8,128)(2,1)S(1)}, bf16[256,256]{1,0:T(8,128)(2,1)}, u32[]{:S(2)}) copy-start(bf16[256,256]{1,0:T(8,128)(2,1)} %constant.88.clone.refs_2_) | copy-start | bytes 393220
  25.1 10.2 %copy-start = (bf16[2,8,128,128]{3,2,1,0:T(8,128)(2,1)}, bf16[2,8,128,128]{3,2,1,0:T(8,128)(2,1)S(1)}, u32[]{:S(2)}) copy-start(bf16[2,8,128,128]{3,2,1,0:T(8,128)(2,1)S(1)} %copy.28) | copy-start | bytes 1572868
  35.4 22.3 %all-to-all-start.1 = ((f32[32,32,128]{2,1,0:T(8,128)}), f32[32,32,128]{2,1,0:T(8,128)S(1)}, u32[]{:S(2)}, u32[]{:S(2)}) async-start(f32[32,32,128]{2,1,0:T(8,128)} %bitcast.4), calls=%async_computation.1 | async-start | bytes 1048576 | tf_op jit(solution)/shard_map/all_to_all | solution.py:507
  46.1 10.8 %collective-permute-start.2 = (bf16[1,128,256]{2,1,0:T(8,128)(2,1)S(1)}, bf16[1,128,256]{2,1,0:T(8,128)(2,1)S(1)}, u32[]{:S(2)}, u32[]{:S(2)}) collective-permute-start(bf16[1,128,256]{2,1,0:T(8,128)(2,1)S(1)} %copy-done.6), channel_id=1, source_target_pairs={{0,64},{16,80},{32,96},{48,112},{64,0},{80,16},{96,32},{112,48},{1... | collective-permute-start | bytes 196616 | tf_op jit(solution)/shard_map/ppermute | solution.py:511
  58.4 19.5 %all-to-all-start.2 = ((f32[16,32,128]{2,1,0:T(8,128)}), f32[16,32,128]{2,1,0:T(8,128)S(1)}, u32[]{:S(2)}, u32[]{:S(2)}) async-start(f32[16,32,128]{2,1,0:T(8,128)} %shard_map.204), calls=%async_computation.2 | async-start | bytes 524288 | tf_op jit(solution)/shard_map/all_to_all | solution.py:507
  64.2 13.8 %copy-start.10 = (f32[128,128]{1,0:T(8,128)S(1)}, f32[128,128]{1,0:T(8,128)}, u32[]{:S(2)}) copy-start(f32[128,128]{1,0:T(8,128)} %constant.96.clone.refs_3_) | copy-start | bytes 196612
  64.3 10.2 %collective-permute-start.4 = (bf16[4,128,256]{2,1,0:T(8,128)(2,1)S(1)}, bf16[4,128,256]{2,1,0:T(8,128)(2,1)S(1)}, u32[]{:S(2)}, u32[]{:S(2)}) collective-permute-start(bf16[4,128,256]{2,1,0:T(8,128)(2,1)S(1)} %get-tuple-element.29), channel_id=1, source_target_pairs={{0,384},{16,400},{32,416},{48,432},{64,448},{80,464},{96,480},{112... | collective-permute-start | bytes 786440 | tf_op jit(solution)/shard_map/ppermute | solution.py:511
  67.9 8.3 %collective-permute-start.3 = (bf16[4,128,256]{2,1,0:T(8,128)(2,1)S(1)}, bf16[4,128,256]{2,1,0:T(8,128)(2,1)S(1)}, u32[]{:S(2)}, u32[]{:S(2)}) collective-permute-start(bf16[4,128,256]{2,1,0:T(8,128)(2,1)S(1)} %get-tuple-element.29), channel_id=1, source_target_pairs={{0,128},{16,144},{32,160},{48,176},{64,192},{80,208},{96,224},{112... | collective-permute-start | bytes 786440 | tf_op jit(solution)/shard_map/ppermute | solution.py:511
  69.8 20.2 %collective-permute-start.5 = (bf16[4,128,256]{2,1,0:T(8,128)(2,1)S(1)}, bf16[4,128,256]{2,1,0:T(8,128)(2,1)S(1)}, u32[]{:S(2)}, u32[]{:S(2)}) collective-permute-start(bf16[4,128,256]{2,1,0:T(8,128)(2,1)S(1)} %get-tuple-element.29), channel_id=1, source_target_pairs={{0,256},{16,272},{32,288},{48,304},{64,320},{80,336},{96,352},{112... | collective-permute-start | bytes 786440 | tf_op jit(solution)/shard_map/ppermute | solution.py:511
  79.9 27.2 %all-to-all-start.3 = ((f32[32,64,128]{2,1,0:T(8,128)}), f32[32,64,128]{2,1,0:T(8,128)}, u32[]{:S(2)}, u32[]{:S(2)}) async-start(f32[32,64,128]{2,1,0:T(8,128)} %shard_map.205), calls=%async_computation.3 | async-start | bytes 2097152 | tf_op jit(solution)/shard_map/all_to_all | solution.py:507
  90.0 3.0 %copy-start.13 = (f32[8,16384]{1,0:T(8,128)S(1)}, f32[8,16384]{1,0:T(8,128)}, u32[]{:S(2)}) copy-start(f32[8,16384]{1,0:T(8,128)} %param.25) | copy-start | bytes 1572868
  90.0 0.7 copy-start.11
  90.7 31.7 %collective-permute-start.6 = (bf16[16,128,256]{2,1,0:T(8,128)(2,1)S(1)}, bf16[16,128,256]{2,1,0:T(8,128)(2,1)S(1)}, u32[]{:S(2)}, u32[]{:S(2)}) collective-permute-start(bf16[16,128,256]{2,1,0:T(8,128)(2,1)S(1)} %constant_dynamic-update-slice_fusion.4.low), channel_id=1, source_target_pairs={{0,16},{16,0},{32,48},{48,32},{64,80},{80,64},{96,112},{112,96},{1... | collective-permute-start | bytes 3145736 | tf_op jit(solution)/shard_map/ppermute | solution.py:511
  112.3 10.2 %copy-start.1 = (f32[1,128,256]{2,1,0:T(8,128)S(1)}, f32[1,128,256]{2,1,0:T(8,128)}, u32[]{:S(2)}) copy-start(f32[1,128,256]{2,1,0:T(8,128)} %param.19) | copy-start | bytes 393220
  112.3 10.1 %copy-start.2 = (f32[1,128,256]{2,1,0:T(8,128)S(1)}, f32[1,128,256]{2,1,0:T(8,128)}, u32[]{:S(2)}) copy-start(f32[1,128,256]{2,1,0:T(8,128)} %param.20) | copy-start | bytes 393220
  112.3 20.9 %all-to-all-start.4 = ((f32[16,16,128]{2,1,0:T(8,128)}), f32[16,16,128]{2,1,0:T(8,128)S(1)}, u32[]{:S(2)}, u32[]{:S(2)}) async-start(f32[16,16,128]{2,1,0:T(8,128)} %shard_map.206), calls=%async_computation.4 | async-start | bytes 262144 | tf_op jit(solution)/shard_map/all_to_all | solution.py:507
  122.4 10.8 %copy-start.3 = (bf16[2,256,256]{2,1,0:T(8,128)(2,1)S(1)}, bf16[2,256,256]{2,1,0:T(8,128)(2,1)}, u32[]{:S(2)}) copy-start(bf16[2,256,256]{2,1,0:T(8,128)(2,1)} %constant.87.clone.table_hbm.table) | copy-start | bytes 786436
  155.1 12.9 %all-to-all-start.6 = ((f32[32,1,256]{2,1,0:T(1,128)}), f32[32,1,256]{2,1,0:T(1,128)S(1)}, u32[]{:S(2)}, u32[]{:S(2)}) async-start(f32[32,1,256]{2,1,0:T(1,128)} %get-tuple-element.19), calls=%async_computation.6 | async-start | bytes 65536 | tf_op jit(solution)/shard_map/all_to_all | solution.py:507

commit v4 on v3

--- a/solution.py
+++ b/solution.py
@@ -126,9 +126,8 @@
     return out[:, :N] + out[:, N:]
 
 
-def call(body, out, *args, scratch=(), in_smem=(), in_hbm=(), vmem=16, late=()):
+def call(body, out, *args, scratch=(), in_smem=(), in_hbm=(), out_smem=(), vmem=16, late=()):
     space = lambda i: pltpu.SMEM if i in in_smem else pltpu.HBM if i in in_hbm else pltpu.VMEM
-    in_vmem = pl.BlockSpec(memory_space=pltpu.VMEM)
     many = isinstance(out, (list, tuple))
     n = len(args)
     inner = (lambda *refs: body(*refs[:n], *refs[n + len(late) :])) if late else body
@@ -139,13 +138,17 @@
             *(pl.BlockSpec(memory_space=space(i)) for i in range(len(args))),
             *(pl.BlockSpec(memory_space=pltpu.HBM) for _ in late),
         ],
-        out_specs=[in_vmem] * len(out) if many else in_vmem,
+        out_specs=[
+            pl.BlockSpec(memory_space=pltpu.SMEM if i in out_smem else pltpu.VMEM) for i in range(len(out))
+        ]
+        if many
+        else pl.BlockSpec(memory_space=pltpu.VMEM),
         scratch_shapes=[
             *(pltpu.VMEM(args[i].shape, args[i].dtype) for i in in_hbm),
-            *([pltpu.SemaphoreType.DMA((max(len(in_hbm), BANDS // CHUNK),))] if in_hbm else []),
+            *([pltpu.SemaphoreType.DMA((16,))] if in_hbm else []),
             *scratch,
         ],
-        compiler_params=pltpu.CompilerParams(vmem_limit_bytes=vmem * MIB),
+        compiler_params=pltpu.CompilerParams(vmem_limit_bytes=int(vmem * MIB)),
     )(*args, *late)
 
 
@@ -236,18 +239,46 @@
             out[pl.ds(2 * pair + i, N, stride=PL), :] = values[:, i * N : (i + 1) * N]
 
 
-def sum_bands(recv, to_slabs):
+TOP = 32767.0
+
+
+def code(value):
+    top = jnp.maximum(jnp.max(jnp.abs(value), axis=0, keepdims=True), 1e-30)
+    log = jnp.ceil(jnp.log(top) * (4.0 / math.log(2.0)) + 0.01)
+    codes = jnp.round(value * (TOP / jnp.exp2(log * 0.25)))
+    return jnp.clip(codes, -TOP, TOP), log
+
+
+def scale_of(log):
+    return jnp.exp2(log * 0.25) * (1.0 / TOP)
+
+
+def narrow(value):
+    return value.astype(jnp.int32).astype(jnp.int16)
+
+
+def widen(value):
+    return value.astype(jnp.int32).astype(F32)
+
+
+def sum_bands(recv, total_out, to_slabs):
     total = recv[0]
     for b in range(1, BANDS):
         total = total + recv[b]
+    total_out[...] = total
+    codes, log = code(total)
+    tile = narrow(jnp.concatenate([codes, jnp.broadcast_to(log, (8, N))], axis=0))
     for i in range(SLABS):
-        to_slabs[i] = total
-
-
-def solve_z(where, recv, modes, modes_t32, out):
+        to_slabs[i] = tile
+
+
+def solve_z(where, recv, density, modes, modes_t32, out):
+    slabs = []
+    for i in range(SLABS):
+        tile = widen(recv[i])
+        slabs.append(tile[: AX * PL] * scale_of(tile[AX * PL : AX * PL + 1]))
     columns = [
-        jnp.concatenate([recv[i, a * PL : (a + 1) * PL, :] for i in range(SLABS)], axis=0)
-        for a in range(AX)
+        jnp.concatenate([tile[a * PL : (a + 1) * PL] for tile in slabs], axis=0) for a in range(AX)
     ]
     spectrum = times_left(modes, jnp.concatenate(columns, axis=1))
     freq = lambda i: jnp.where(i <= N // 2, i, i - N // 2)
@@ -264,30 +295,38 @@
         weighted.append(spectrum[:, a * N : (a + 1) * N] * kernel)
     own = modes_t32[pl.ds(pl.multiple_of(where[1] * PL, PL), PL), :]
     result = dot3(split(own), split(jnp.concatenate(weighted, axis=1)))
-    density = recv[where[1]]
+    result = jnp.concatenate([result[:, a * N : (a + 1) * N] for a in range(AX)], axis=0)
+    values, logs = zip(code(result), code(density[...]))
     tile = []
     for a in range(AX):
-        tile += [result[:, a * N : (a + 1) * N], density[a * PL : (a + 1) * PL]]
-    tile = jnp.concatenate(tile, axis=0)
+        tile += [value[a * PL : (a + 1) * PL] for value in values]
+    tile += [jnp.broadcast_to(log, (4, N)) for log in logs]
+    tile = narrow(jnp.concatenate(tile, axis=0))
     for i in range(BANDS):
         out[i] = tile
 
 
 def planes_to_sticks(
-    recv_hbm, modes_hbm, modes_t_hbm, xc_hbm, occ_hbm, x_hbm, y_hbm, cells,
-    out, recv, modes, modes_t, xc, occ, x_table, y_table, sems, half, rows, grid
+    recv, cells, modes_hbm, modes_t_hbm, xc_hbm, occ_hbm, x_hbm, y_hbm,
+    out, modes, modes_t, xc, occ, x_table, y_table, sems, half, rows, grid
 ):
     copies = fetch(
-        (recv_hbm, modes_hbm, modes_t_hbm, xc_hbm, occ_hbm, x_hbm, y_hbm),
-        (recv, modes, modes_t, xc, occ, x_table, y_table),
+        (modes_hbm, modes_t_hbm, xc_hbm, occ_hbm, x_hbm, y_hbm),
+        (modes, modes_t, xc, occ, x_table, y_table),
         sems,
     )
-    for copy in copies[:3]:
-        copy.wait()
-    for i in range(8):
-        at = slice(i * 256, (i + 1) * 256)
-        half[at, :] = times_right(recv[at, :], modes)
-    for copy in copies[3:]:
+    copies[0].wait()
+    size = 2 * AX * PL
+    for i in range(0, BANDS, 4):
+        tiles = []
+        for b in range(i, i + 4):
+            tile = widen(recv[b])
+            scales = [
+                jnp.broadcast_to(scale_of(tile[size + 4 * k : size + 4 * k + 1]), (PL, N)) for k in range(2)
+            ]
+            tiles.append(tile[:size] * jnp.concatenate(scales * AX, axis=0))
+        half[i * size : (i + 4) * size, :] = times_right(jnp.concatenate(tiles, axis=0), modes)
+    for copy in copies[1:]:
         copy.wait()
     for p in range(PL):
         value = jnp.concatenate(
@@ -359,17 +398,21 @@
     return at
 
 
-def overlap_rows(at, probes, sums):
+def band_of(place, me):
+    return (place % 4 * 2 + place // 4 % 4 * 8 + place // 16) ^ me
+
+
+def overlap_rows(at, where, probes, sums):
     pairs = [
         (x, jnp.concatenate([x[:, N:], -x[:, :N]], axis=1)) for x in probes
     ]
-    for w in range(BANDS):
-        orbital = at(w)
+    for place in range(BANDS):
+        orbital = at(place)
+        w = band_of(place, where[0])
         for i, pair in enumerate(pairs):
             for c, probe in enumerate(pair):
                 line = jnp.sum(orbital * probe, axis=0, keepdims=True)
-                k = c * BANDS + w
-                sums[i, k : k + 1, :] = line[:, :N] + line[:, N:]
+                sums[i, pl.ds(c * BANDS + w, 1), :] = line[:, :N] + line[:, N:]
     rows = []
     for i in range(len(probes)):
         sums[i, 2 * BANDS :, :] = jnp.zeros((N - 2 * BANDS, N), F32)
@@ -395,23 +438,23 @@
     return jnp.where(lane() < 2 * BANDS, row, 0.0)
 
 
-def fixed_overlaps(low, high, resp, prev, occ, out, low_held, high_held, sems, sums):
+def fixed_overlaps(where, low, high, resp, prev, occ, out, low_held, high_held, sems, sums):
     at = orbitals((low, high), (low_held, high_held), sems)
-    rows = overlap_rows(at, [resp[...], prev[...], occ[...].astype(F32)], sums)
+    rows = overlap_rows(at, where, [resp[...], prev[...], occ[...].astype(F32)], sums)
     for i, row in enumerate(rows):
         out[i : i + 1, :] = row
     out[3:, :] = jnp.zeros((5, N), F32)
 
 
 def apply_and_overlap(
-    recv, table, scalars, resp, prev, fixed, low, high,
+    recv, table, where, scalars, resp, prev, fixed, low, high,
     applied_out, part_out, low_held, high_held, sems, sums
 ):
     at = orbitals((low, high), (low_held, high_held), sems)
     values = recv[...].reshape(2 * N, STK).T
     applied = dot3(split(values), (table[0], table[1]))
     applied_out[...] = applied
-    margin, along = overlap_rows(at, [applied.astype(BF16).astype(F32), applied], sums)
+    margin, along = overlap_rows(at, where, [applied.astype(BF16).astype(F32), applied], sums)
     response = resp[...]
     first = scalars[0] * response + applied
     rest = first - scalars[1] * prev[...]
@@ -436,7 +479,7 @@
         part_out[i] = row
 
 
-def join_slabs(where, recv, margin_out, place_out, part_out):
+def join_slabs(recv, margin_out, part_out):
     rows = [jnp.concatenate([recv[i][:, j * N : (j + 1) * N] for i in range(SLABS)], axis=0) for j in range(3)]
     add = lambda v: jnp.sum(v, axis=0, keepdims=True)
     norms, firsts, slopes, lefts = (rows[2][:, 2 * BANDS + i : 2 * BANDS + i + 1] for i in range(4))
@@ -450,17 +493,10 @@
     with_resp = add(rows[2])
     inner = lambda x: jnp.sum(weights * lower(x), axis=1, keepdims=True)
     removed_resp = inner(with_resp)
-    place_out[...] = head
-    i = lax.broadcasted_iota(jnp.int32, (N, 1), 0)
-    k = i % BANDS
-    band = (k % 4 * 2 + k // 4 % 4 * 8 + k // 16) ^ where[0]
-    to_band = (i // BANDS * BANDS + band == lane()).astype(F32)
-    heads = jnp.concatenate([head, jnp.where(lane() < 2 * BANDS, weights, head)], axis=0)
-    heads = jnp.dot(heads, to_band, precision=lax.Precision.HIGHEST, preferred_element_type=F32)
-    margin_out[...] = heads[:1]
+    margin_out[...] = head
     row = jnp.concatenate(
         [
-            heads[1:],
+            jnp.where(lane() < 2 * BANDS, weights, head),
             with_lanes(
                 jnp.zeros((1, N), F32),
                 0,
@@ -473,9 +509,13 @@
         part_out[i] = row
 
 
-def remove(margin, scalars, resp, prev, applied, low, high, rest_out, low_held, high_held, sems):
+def remove(margin, where, scalars, resp, prev, applied, low, high, rest_out, low_held, high_held, sems):
     at = orbitals((low, high), (low_held, high_held), sems)
-    weights = margin[...].astype(BF16).astype(F32)
+    weights = margin[...].astype(BF16)
+    i = lax.broadcasted_iota(jnp.int32, (1, N), 1)
+    band = i // BANDS * BANDS + band_of(i % BANDS, where[0])
+    to_place = lax.broadcasted_iota(jnp.int32, (N, 1), 0) == band
+    weights = dot(weights, jnp.where(to_place, 1.0, 0.0).astype(BF16))
     plain = jnp.zeros((STK, 2 * N), F32)
     turned = jnp.zeros((STK, 2 * N), F32)
     for w in range(BANDS):
@@ -500,7 +540,8 @@
     resid_sq = add(lefts + gap * (gap * norms - 2.0 * removed_resp)) + square
     beta = jnp.sqrt(jnp.maximum(resid_sq, 0.0) / float(2 * BANDS * STICKS * N) + 1e-06)
     next_out[...] = (rest[...] - alpha * resp[...]) / beta
-    coef_out[...] = with_lanes(jnp.zeros((1, N), F32), 0, [alpha, beta])
+    coef_out[0] = alpha[0, 0]
+    coef_out[1] = beta[0, 0]
 
 
 def swap(value, axis):
@@ -542,26 +583,32 @@
     )
     partial = swap(partial.reshape(BANDS, AX * PL, N), "band")
     x2 = across(own, 4)
-    total = call(sum_bands, shape(SLABS, AX * PL, N), partial, late=(x2,))
+    own_modes, total = call(
+        sum_bands,
+        [shape(AX * PL, N), shape(SLABS, AX * PL + 8, N, dtype=jnp.int16)],
+        partial,
+        late=(x2,),
+    )
     row = jnp.concatenate([own, x1, x2, x3], axis=0)
     y1, y3 = across(row, 8), across(row, 24)
     columns = swap(total, "slab")
     hartree = call(
-        solve_z, shape(BANDS, 2 * AX * PL, N), where, columns, t["modes_left"], t["modes_t32"],
+        solve_z, shape(BANDS, 2 * AX * PL + 8, N, dtype=jnp.int16), where, columns, own_modes, t["modes_left"], t["modes_t32"],
         in_smem=(0,),
         late=(y1, y3),
     )
-    y2 = across(row, 16)
+    near, hartree = after(y1, hartree)
+    y2 = across(near, 24)
     xc_planes, _ = after(xc_kernel, hartree)
     xc_planes = xc_planes.reshape(PL, N, N)
     hartree = swap(hartree, "band")
     chosen = call(
         planes_to_sticks,
         shape(SLABS, 2 * PL, STK),
-        hartree.reshape(2 * N * PL, N), t["modes_right"], t["modes_t_left"],
-        xc_planes, occ_planes, t["x_forward"], t["y_forward"], cells,
-        in_hbm=(0, 1, 2, 3, 4, 5, 6),
-        vmem=60,
+        hartree, cells, t["modes_right"], t["modes_t_left"],
+        xc_planes, occ_planes, t["x_forward"], t["y_forward"],
+        in_hbm=(2, 3, 4, 5, 6, 7),
+        vmem=59.8,
         late=(y2,),
         scratch=[pltpu.VMEM((2 * N * PL, N), F32), bf_scratch(8 * N, 2 * N), pltpu.VMEM((2, 2 * N, N), F32)],
     )
@@ -571,39 +618,40 @@
     fixed = call(
         fixed_overlaps,
         shape(8, N),
-        low, high, resp, prev, occupied.reshape(STK, 2 * N),
-        in_hbm=(0, 1),
+        where, low, high, resp, prev, occupied.reshape(STK, 2 * N),
+        in_smem=(0,),
+        in_hbm=(1, 2),
         scratch=[pltpu.VMEM((3, N, N), F32)],
     )
     scalars = jnp.stack([band_gap[0], earlier_beta[0]])
     applied, parts = call(
         apply_and_overlap,
         [shape(STK, 2 * N), shape(SLABS, 1, 3 * N)],
-        gathered, t["z_forward"], scalars, resp, prev, fixed, low, high,
-        in_smem=(2,),
-        in_hbm=(6, 7),
+        gathered, t["z_forward"], where, scalars, resp, prev, fixed, low, high,
+        in_smem=(2, 3),
+        in_hbm=(7, 8),
         scratch=[pltpu.VMEM((2, N, N), F32)],
     )
-    margin, placed_margin, parts = call(
-        join_slabs,
-        [shape(1, N), shape(1, N), shape(BANDS, 1, 2 * N)],
-        where, swap(parts, "slab"),
-        in_smem=(0,),
+    margin, parts = call(
+        join_slabs, [shape(1, N), shape(BANDS, 1, 2 * N)], swap(parts, "slab")
     )
     rest = call(
         remove,
         shape(STK, 2 * N),
-        placed_margin, scalars, resp, prev, applied, low, high,
-        in_smem=(1,),
-        in_hbm=(5, 6),
+        margin, where, scalars, resp, prev, applied, low, high,
+        in_smem=(1, 2),
+        in_hbm=(6, 7),
     )
     next_vector, coefficients = call(
-        finish, [shape(STK, 2 * N), shape(1, N)], swap(parts, "band"), resp, rest
+        finish,
+        [shape(STK, 2 * N), shape(2)],
+        swap(parts, "band"), resp, rest,
+        out_smem=(1,),
     )
     return (
         next_vector.reshape(1, STK, 2 * N),
         margin[0, : 2 * BANDS].reshape(2, BANDS, 1),
-        coefficients[0, :2],
+        coefficients,
     )
 
 

time: 171 us -> 169 us (0.988)
  waiting for transfers between devices: 42.6 us -> 36.8 us
  starting transfers between devices: 79.6 us -> 82.2 us
    all_to_all x6, waiting for transfers between devices: 31.3 us -> 22.5 us  [swap(): return lax.all_to_all(value, axis, 0, 0, tiled=True)]
    ppermute x7, waiting for transfers between devices: 11.4 us -> 14.3 us  [across(): return lax.ppermute(blocks, 'band', [(i, i ^ bit) for i in range(BANDS)])]
    ppermute x7, starting transfers between devices: 22.9 us -> 24.8 us  [across(): return lax.ppermute(blocks, 'band', [(i, i ^ bit) for i in range(BANDS)])]
  transfers between devices with their start and end apart: 13 -> 13, of which waited for: 10 -> 10; matrix products, arithmetic and copies ran while one was open for 1% -> 1% of each run, Pallas kernels for 7% -> 6%
where the time goes in v4:
time: 169 us; the launch traced here: 168 us
  starting transfers between devices  82.2 us (49%)
  waiting for transfers between devices  36.8 us (22%)
  Pallas kernels  25 us (15%)
  blocking collectives  17.6 us (10%)
  local copies, waits for them, and re-layouts  3.33 us (2%)
  between operations  2.51 us (1%)
    all_to_all x6, starting transfers between devices, swap(): return lax.all_to_all(value, axis, 0, 0, tiled=True)  57.4 us
    pallas_call x10, Pallas kernels, call(): pl.pallas_call(inner, out_shape=out, in_specs=[*(pl.BlockSpec(memory_spac...  25 us
    ppermute x7, starting transfers between devices, across(): return lax.ppermute(blocks, 'band', [(i, i ^ bit) for i in range(BANDS)])  24.8 us
    all_to_all x6, waiting for transfers between devices, swap(): return lax.all_to_all(value, axis, 0, 0, tiled=True)  22.5 us
    all_to_all x1, blocking collectives, swap(): return lax.all_to_all(value, axis, 0, 0, tiled=True)  17.6 us
    ppermute x7, waiting for transfers between devices, across(): return lax.ppermute(blocks, 'band', [(i, i ^ bit) for i in range(BANDS)])  14.3 us
  transfers between devices with their start and end apart: 13, of which 10 were waited for; matrix products, arithmetic and copies ran while one was open for 1% of the time, Pallas kernels for 6%

profile of v4, /device:TPU:1, one launch (start us, length us, event | category | flops | bytes accessed | tf_op | source)
XLA Modules:
  0.0 167.7 jit_solution(4440876443780075018)
XLA Ops:
  0.6 2.1 %shard_map.202 = f32[16,16,128]{2,1,0:T(8,128)} custom-call(f32[128,256]{1,0:T(8,128)} %bitcast.20, bf16[2,256,256]{2,1,0:T(8,128)(2,1)} %constant.87.clone.table_hbm.table), custom_call_target="tpu_custom_call" | custom-call | tf_op jit(solution)/shard_map/pallas_call | solution.py:134
  2.8 15.9 %all-to-all-start = ((f32[16,16,128]{2,1,0:T(8,128)}), f32[16,16,128]{2,1,0:T(8,128)S(1)}, u32[]{:S(2)}, u32[]{:S(2)}) async-start(f32[16,16,128]{2,1,0:T(8,128)} %shard_map.202), calls=%async_computation | async-start | bytes 262144 | tf_op jit(solution)/shard_map/all_to_all | solution.py:548
  18.8 3.1 %collective-permute-start = (bf16[1,128,256]{2,1,0:T(8,128)(2,1)S(1)}, bf16[1,128,256]{2,1,0:T(8,128)(2,1)S(1)}, u32[]{:S(2)}, u32[]{:S(2)}) collective-permute-start(bf16[1,128,256]{2,1,0:T(8,128)(2,1)S(1)} %copy-done.6), channel_id=1, source_target_pairs={{0,32},{16,48},{32,0},{48,16},{64,96},{80,112},{96,64},{112,80},{1... | collective-permute-start | bytes 196616 | tf_op jit(solution)/shard_map/ppermute | solution.py:552
  21.9 3.7 %collective-permute-start.2 = (bf16[1,128,256]{2,1,0:T(8,128)(2,1)S(1)}, bf16[1,128,256]{2,1,0:T(8,128)(2,1)S(1)}, u32[]{:S(2)}, u32[]{:S(2)}) collective-permute-start(bf16[1,128,256]{2,1,0:T(8,128)(2,1)S(1)} %copy-done.6), channel_id=1, source_target_pairs={{0,96},{16,112},{32,64},{48,80},{64,32},{80,48},{96,0},{112,16},{1... | collective-permute-start | bytes 196616 | tf_op jit(solution)/shard_map/ppermute | solution.py:552
  25.8 2.6 %collective-permute-done.2.refs_8_ = bf16[1,128,256]{2,1,0:T(8,128)(2,1)S(1)} collective-permute-done((bf16[1,128,256]{2,1,0:T(8,128)(2,1)S(1)}, bf16[1,128,256]{2,1,0:T(8,128)(2,1)S(1)}, u32[]{:S(2)}, u32[]{:S(2)}) %collective-permute-start.2) | collective-permute-done | bytes 65568 | tf_op jit(solution)/shard_map/ppermute | solution.py:552
  28.4 2.3 %all-to-all-done.refs_0_ = f32[16,16,128]{2,1,0:T(8,128)S(1)} async-done(((f32[16,16,128]{2,1,0:T(8,128)}), f32[16,16,128]{2,1,0:T(8,128)S(1)}, u32[]{:S(2)}, u32[]{:S(2)}) %all-to-all-start) | async-done | bytes 131104 | tf_op jit(solution)/shard_map/all_to_all | solution.py:548
  30.7 4.8 %shard_map.203 = f32[1024,128]{1,0:T(8,128)} custom-call(f32[16,16,128]{2,1,0:T(8,128)S(1)} %all-to-all-done.refs_0_, s32[1,2048]{1,0:T(1,128)S(1)} %bitcast.29, bf16[256,256]{1,0:T(8,128)(2,1)S(1)} %copy-done.7, bf16[512,256]{1,0:T(8,128)(2,1)S(1)} %copy-done.5, bf16[2,8,128,128]{3,2,1,0:T(8,128)(2,1)S(1)} %copy.28, bf16[256,256]{1,0:T(8,128)(2,1)S(1)} %copy-done.4, ...), custom_call_target="tpu_custom_call" | custom-call | tf_op jit(solution)/shard_map/pallas_call | solution.py:134
  35.6 10.7 %all-to-all-start.1 = ((f32[32,32,128]{2,1,0:T(8,128)}), f32[32,32,128]{2,1,0:T(8,128)S(1)}, u32[]{:S(2)}, u32[]{:S(2)}) async-start(f32[32,32,128]{2,1,0:T(8,128)} %bitcast.4), calls=%async_computation.1 | async-start | bytes 1048576 | tf_op jit(solution)/shard_map/all_to_all | solution.py:548
  46.3 4.8 %collective-permute-start.1 = (bf16[1,128,256]{2,1,0:T(8,128)(2,1)S(1)}, bf16[1,128,256]{2,1,0:T(8,128)(2,1)S(1)}, u32[]{:S(2)}, u32[]{:S(2)}) collective-permute-start(bf16[1,128,256]{2,1,0:T(8,128)(2,1)S(1)} %copy-done.6), channel_id=1, source_target_pairs={{0,64},{16,80},{32,96},{48,112},{64,0},{80,16},{96,32},{112,48},{1... | collective-permute-start | bytes 196616 | tf_op jit(solution)/shard_map/ppermute | solution.py:552
  51.1 6.0 %collective-permute-done.1.refs_1_ = bf16[1,128,256]{2,1,0:T(8,128)(2,1)S(1)} collective-permute-done((bf16[1,128,256]{2,1,0:T(8,128)(2,1)S(1)}, bf16[1,128,256]{2,1,0:T(8,128)(2,1)S(1)}, u32[]{:S(2)}, u32[]{:S(2)}) %collective-permute-start.1) | collective-permute-done | bytes 65568 | tf_op jit(solution)/shard_map/ppermute | solution.py:552
  58.6 7.0 %all-to-all-start.2 = ((s16[16,40,128]{2,1,0:T(8,128)(2,1)}), s16[16,40,128]{2,1,0:T(8,128)(2,1)S(1)}, u32[]{:S(2)}, u32[]{:S(2)}) async-start(s16[16,40,128]{2,1,0:T(8,128)(2,1)} %get-tuple-element.20), calls=%async_computation.2 | async-start | bytes 327680 | tf_op jit(solution)/shard_map/all_to_all | solution.py:548
  65.7 2.3 %collective-permute-start.3 = (bf16[4,128,256]{2,1,0:T(8,128)(2,1)S(1)}, bf16[4,128,256]{2,1,0:T(8,128)(2,1)S(1)}, u32[]{:S(2)}, u32[]{:S(2)}) collective-permute-start(bf16[4,128,256]{2,1,0:T(8,128)(2,1)S(1)} %get-tuple-element.35), channel_id=1, source_target_pairs={{0,128},{16,144},{32,160},{48,176},{64,192},{80,208},{96,224},{112... | collective-permute-start | bytes 786440 | tf_op jit(solution)/shard_map/ppermute | solution.py:552
  68.0 3.7 %collective-permute-start.4 = (bf16[4,128,256]{2,1,0:T(8,128)(2,1)S(1)}, bf16[4,128,256]{2,1,0:T(8,128)(2,1)S(1)}, u32[]{:S(2)}, u32[]{:S(2)}) collective-permute-start(bf16[4,128,256]{2,1,0:T(8,128)(2,1)S(1)} %get-tuple-element.35), channel_id=1, source_target_pairs={{0,384},{16,400},{32,416},{48,432},{64,448},{80,464},{96,480},{112... | collective-permute-start | bytes 786440 | tf_op jit(solution)/shard_map/ppermute | solution.py:552
  71.8 2.9 %collective-permute-done.3.refs_5_ = bf16[4,128,256]{2,1,0:T(8,128)(2,1)S(1)} collective-permute-done((bf16[4,128,256]{2,1,0:T(8,128)(2,1)S(1)}, bf16[4,128,256]{2,1,0:T(8,128)(2,1)S(1)}, u32[]{:S(2)}, u32[]{:S(2)}) %collective-permute-start.3) | collective-permute-done | bytes 262176 | tf_op jit(solution)/shard_map/ppermute | solution.py:552
  74.7 2.8 %collective-permute-done.4.refs_6_ = bf16[4,128,256]{2,1,0:T(8,128)(2,1)S(1)} collective-permute-done((bf16[4,128,256]{2,1,0:T(8,128)(2,1)S(1)}, bf16[4,128,256]{2,1,0:T(8,128)(2,1)S(1)}, u32[]{:S(2)}, u32[]{:S(2)}) %collective-permute-start.4) | collective-permute-done | bytes 262176 | tf_op jit(solution)/shard_map/ppermute | solution.py:552
  78.0 1.9 %shard_map.205 = s16[32,72,128]{2,1,0:T(8,128)(2,1)} custom-call(s32[2]{0:T(128)S(1)} %pad_add_fusion.refs_0_.where, s16[16,40,128]{2,1,0:T(8,128)(2,1)S(1)} %all-to-all-done.2.refs_1_, f32[32,128]{1,0:T(8,128)S(1)} %get-tuple-element.21.refs_2_, bf16[256,256]{1,0:T(8,128)(2,1)S(1)} %copy-done.4, f32[128,128]{1,0:T(8,128)S(1)} %copy-done.10, ...), custom_call_target="tpu_custom_call" | custom-call | tf_op jit(solution)/shard_map/pallas_call | solution.py:134
  79.9 3.4 %collective-permute-start.5 = (bf16[4,128,256]{2,1,0:T(8,128)(2,1)S(1)}, bf16[4,128,256]{2,1,0:T(8,128)(2,1)S(1)}, u32[]{:S(2)}, u32[]{:S(2)}) collective-permute-start(bf16[4,128,256]{2,1,0:T(8,128)(2,1)S(1)} %collective-permute-done.3.refs_5_), channel_id=1, source_target_pairs={{0,384},{16,400},{32,416},{48,432},{64,448},{80,464},{96,480},{112... | collective-permute-start | bytes 786440 | tf_op jit(solution)/shard_map/ppermute | solution.py:552
  83.3 8.2 %all-to-all-start.3 = ((s16[32,72,128]{2,1,0:T(8,128)(2,1)}), s16[32,72,128]{2,1,0:T(8,128)(2,1)S(1)}, u32[]{:S(2)}, u32[]{:S(2)}) async-start(s16[32,72,128]{2,1,0:T(8,128)(2,1)} %shard_map.205), calls=%async_computation.3 | async-start | bytes 1179648 | tf_op jit(solution)/shard_map/all_to_all | solution.py:548
  92.2 3.8 %collective-permute-start.6 = (bf16[16,128,256]{2,1,0:T(8,128)(2,1)S(1)}, bf16[16,128,256]{2,1,0:T(8,128)(2,1)S(1)}, u32[]{:S(2)}, u32[]{:S(2)}) collective-permute-start(bf16[16,128,256]{2,1,0:T(8,128)(2,1)S(1)} %constant_dynamic-update-slice_fusion.4.low), channel_id=1, source_target_pairs={{0,16},{16,0},{32,48},{48,32},{64,80},{80,64},{96,112},{112,96},{1... | collective-permute-start | bytes 3145736 | tf_op jit(solution)/shard_map/ppermute | solution.py:552
  96.0 0.9 copy.27
  96.9 6.9 %all-to-all-done.3.refs_0_ = s16[32,72,128]{2,1,0:T(8,128)(2,1)S(1)} async-done(((s16[32,72,128]{2,1,0:T(8,128)(2,1)}), s16[32,72,128]{2,1,0:T(8,128)(2,1)S(1)}, u32[]{:S(2)}, u32[]{:S(2)}) %all-to-all-start.3) | async-done | bytes 589856 | tf_op jit(solution)/shard_map/all_to_all | solution.py:548
  104.7 5.3 %shard_map.206 = f32[16,16,128]{2,1,0:T(8,128)} custom-call(s16[32,72,128]{2,1,0:T(8,128)(2,1)} %copy-done.11, s32[1,2048]{1,0:T(1,128)} %bitcast.30, bf16[256,256]{1,0:T(8,128)(2,1)} %constant.93.clone.refs_2_, bf16[256,256]{1,0:T(8,128)(2,1)} %constant.94.clone.refs_3_, f32[8,128,128]{2,1,0:T(8,128)} %bitcast.31, bf16[2,8,128,128]{3,2,1,0:T(8,128)(2,1)} %copy-done, ...), custom_call_target="tpu_custom_call" | custom-call | tf_op jit(solution)/shard_map/pallas_call | solution.py:134
  110.0 9.7 %all-to-all-start.4 = ((f32[16,16,128]{2,1,0:T(8,128)}), f32[16,16,128]{2,1,0:T(8,128)S(1)}, u32[]{:S(2)}, u32[]{:S(2)}) async-start(f32[16,16,128]{2,1,0:T(8,128)} %shard_map.206), calls=%async_computation.4 | async-start | bytes 262144 | tf_op jit(solution)/shard_map/all_to_all | solution.py:548
  121.1 2.9 %shard_map.207.fixed = f32[8,128]{1,0:T(8,128)S(1)} custom-call(s32[2]{0:T(128)S(1)} %pad_add_fusion.refs_0_.where, bf16[16,128,256]{2,1,0:T(8,128)(2,1)S(1)} %constant_dynamic-update-slice_fusion.4.low, bf16[16,128,256]{2,1,0:T(8,128)(2,1)S(1)} %collective-permute-done.6.high, f32[128,256]{1,0:T(8,128)S(1)} %bitcast.21, f32[128,256]{1,0:T(8,128)S(1)} %bitcast.25, ...), custom_call_target="tpu_custom_call" | custom-call | tf_op jit(solution)/shard_map/pallas_call | solution.py:134
  124.1 7.7 %all-to-all-done.4.recv = f32[16,16,128]{2,1,0:T(8,128)S(1)} async-done(((f32[16,16,128]{2,1,0:T(8,128)}), f32[16,16,128]{2,1,0:T(8,128)S(1)}, u32[]{:S(2)}, u32[]{:S(2)}) %all-to-all-start.4) | async-done | bytes 131104 | tf_op jit(solution)/shard_map/all_to_all | solution.py:548
  131.7 2.8 %shard_map.208 = (f32[128,256]{1,0:T(8,128)S(1)}, f32[16,1,384]{2,1,0:T(1,128)S(1)}) custom-call(f32[16,16,128]{2,1,0:T(8,128)S(1)} %all-to-all-done.4.recv, bf16[2,256,256]{2,1,0:T(8,128)(2,1)S(1)} %copy-done.3, s32[2]{0:T(128)S(1)} %pad_add_fusion.refs_0_.where, f32[2]{0:T(128)S(1)} %pad_maximum_fusion.scalars, f32[128,256]{1,0:T(8,128)S(1)} %bitcast.22, ...), custom_call_target="tpu_custom_call" | custom-call | tf_op jit(solution)/shard_map/pallas_call | solution.py:134
  134.5 17.6 %all_to_all.35.recv = f32[16,1,384]{2,1,0:T(1,128)S(1)} all-to-all(f32[16,1,384]{2,1,0:T(1,128)S(1)} %get-tuple-element.25), channel_id=1, replica_groups=mesh['band'=32,'slab'=16] {'slab'}, dimensions={0} | all-to-all | bytes 49152 | tf_op jit(solution)/shard_map/all_to_all | solution.py:548
  152.1 1.0 shard_map.209
  153.1 5.9 %all-to-all-start.6 = ((f32[32,1,256]{2,1,0:T(1,128)}), f32[32,1,256]{2,1,0:T(1,128)S(1)}, u32[]{:S(2)}, u32[]{:S(2)}) async-start(f32[32,1,256]{2,1,0:T(1,128)} %get-tuple-element.26), calls=%async_computation.6 | async-start | bytes 65536 | tf_op jit(solution)/shard_map/all_to_all | solution.py:548
  159.7 2.2 %shard_map.210.rest = f32[128,256]{1,0:T(8,128)S(1)} custom-call(f32[1,128]{1,0:T(1,128)S(1)} %get-tuple-element.27.margin, s32[2]{0:T(128)S(1)} %pad_add_fusion.refs_0_.where, f32[2]{0:T(128)S(1)} %pad_maximum_fusion.scalars, f32[128,256]{1,0:T(8,128)S(1)} %bitcast.23, f32[128,256]{1,0:T(8,128)S(1)} %bitcast.27, f32[128,256]{1,0:T(8,128)S(1)} %get-tuple-element.28.applied, ...), custom_call_target="tpu_custom_call" | custom-call | tf_op jit(solution)/shard_map/pallas_call | solution.py:134
  161.9 4.3 %all-to-all-done.6.recv = f32[32,1,256]{2,1,0:T(1,128)S(1)} async-done(((f32[32,1,256]{2,1,0:T(1,128)}), f32[32,1,256]{2,1,0:T(1,128)S(1)}, u32[]{:S(2)}, u32[]{:S(2)}) %all-to-all-start.6) | async-done | bytes 32800 | tf_op jit(solution)/shard_map/all_to_all | solution.py:548
  166.3 1.3 shard_map.211
  (51 shorter events, 4.7 us)
Async XLA Ops:
  0.6 25.0 %copy-start.13 = (bf16[1,2,8,16384]{3,2,1,0:T(8,128)(2,1)S(1)}, bf16[1,2,8,16384]{3,2,1,0:T(8,128)(2,1)}, u32[]{:S(2)}) copy-start(bf16[1,2,8,16384]{3,2,1,0:T(8,128)(2,1)} %param.24) | copy-start | bytes 1572868
  2.8 15.9 %copy-start.15 = (s32[2048]{0:T(1024)S(1)}, s32[2048]{0:T(1024)}, u32[]{:S(2)}) copy-start(s32[2048]{0:T(1024)} %param.26) | copy-start | bytes 24580
  2.8 16.0 %copy-start.6 = (bf16[1,128,256]{2,1,0:T(8,128)(2,1)S(1)}, bf16[1,128,256]{2,1,0:T(8,128)(2,1)}, u32[]{:S(2)}) copy-start(bf16[1,128,256]{2,1,0:T(8,128)(2,1)} %param.23) | copy-start | bytes 196612
  2.8 27.9 %all-to-all-start = ((f32[16,16,128]{2,1,0:T(8,128)}), f32[16,16,128]{2,1,0:T(8,128)S(1)}, u32[]{:S(2)}, u32[]{:S(2)}) async-start(f32[16,16,128]{2,1,0:T(8,128)} %shard_map.202), calls=%async_computation | async-start | bytes 262144 | tf_op jit(solution)/shard_map/all_to_all | solution.py:548
  18.7 12.0 %copy-start.9 = (s32[2048]{0:T(1024)}, s32[2048]{0:T(1024)S(1)}, u32[]{:S(2)}) copy-start(s32[2048]{0:T(1024)S(1)} %fusion.4) | copy-start | bytes 24580
  18.8 7.0 %collective-permute-start = (bf16[1,128,256]{2,1,0:T(8,128)(2,1)S(1)}, bf16[1,128,256]{2,1,0:T(8,128)(2,1)S(1)}, u32[]{:S(2)}, u32[]{:S(2)}) collective-permute-start(bf16[1,128,256]{2,1,0:T(8,128)(2,1)S(1)} %copy-done.6), channel_id=1, source_target_pairs={{0,32},{16,48},{32,0},{48,16},{64,96},{80,112},{96,64},{112,80},{1... | collective-permute-start | bytes 196616 | tf_op jit(solution)/shard_map/ppermute | solution.py:552
  21.9 6.5 %collective-permute-start.2 = (bf16[1,128,256]{2,1,0:T(8,128)(2,1)S(1)}, bf16[1,128,256]{2,1,0:T(8,128)(2,1)S(1)}, u32[]{:S(2)}, u32[]{:S(2)}) collective-permute-start(bf16[1,128,256]{2,1,0:T(8,128)(2,1)S(1)} %copy-done.6), channel_id=1, source_target_pairs={{0,96},{16,112},{32,64},{48,80},{64,32},{80,48},{96,0},{112,16},{1... | collective-permute-start | bytes 196616 | tf_op jit(solution)/shard_map/ppermute | solution.py:552
  25.6 5.1 %copy-start.4 = (bf16[256,256]{1,0:T(8,128)(2,1)S(1)}, bf16[256,256]{1,0:T(8,128)(2,1)}, u32[]{:S(2)}) copy-start(bf16[256,256]{1,0:T(8,128)(2,1)} %constant.92.clone.refs_5_.refs_3_) | copy-start | bytes 393220
  25.7 5.1 %copy-start.5 = (bf16[512,256]{1,0:T(8,128)(2,1)S(1)}, bf16[512,256]{1,0:T(8,128)(2,1)}, u32[]{:S(2)}) copy-start(bf16[512,256]{1,0:T(8,128)(2,1)} %constant.90.clone.refs_3_) | copy-start | bytes 786436
  25.7 5.1 %copy-start.7 = (bf16[256,256]{1,0:T(8,128)(2,1)S(1)}, bf16[256,256]{1,0:T(8,128)(2,1)}, u32[]{:S(2)}) copy-start(bf16[256,256]{1,0:T(8,128)(2,1)} %constant.88.clone.refs_2_) | copy-start | bytes 393220
  25.7 5.0 %copy-start.8 = (bf16[256,256]{1,0:T(8,128)(2,1)S(1)}, bf16[256,256]{1,0:T(8,128)(2,1)}, u32[]{:S(2)}) copy-start(bf16[256,256]{1,0:T(8,128)(2,1)} %constant.95.clone.refs_6_) | copy-start | bytes 393220
  25.8 9.8 %copy-start = (bf16[2,8,128,128]{3,2,1,0:T(8,128)(2,1)}, bf16[2,8,128,128]{3,2,1,0:T(8,128)(2,1)S(1)}, u32[]{:S(2)}) copy-start(bf16[2,8,128,128]{3,2,1,0:T(8,128)(2,1)S(1)} %copy.28) | copy-start | bytes 1572868
  35.6 22.3 %all-to-all-start.1 = ((f32[32,32,128]{2,1,0:T(8,128)}), f32[32,32,128]{2,1,0:T(8,128)S(1)}, u32[]{:S(2)}, u32[]{:S(2)}) async-start(f32[32,32,128]{2,1,0:T(8,128)} %bitcast.4), calls=%async_computation.1 | async-start | bytes 1048576 | tf_op jit(solution)/shard_map/all_to_all | solution.py:548
  46.3 10.8 %collective-permute-start.1 = (bf16[1,128,256]{2,1,0:T(8,128)(2,1)S(1)}, bf16[1,128,256]{2,1,0:T(8,128)(2,1)S(1)}, u32[]{:S(2)}, u32[]{:S(2)}) collective-permute-start(bf16[1,128,256]{2,1,0:T(8,128)(2,1)S(1)} %copy-done.6), channel_id=1, source_target_pairs={{0,64},{16,80},{32,96},{48,112},{64,0},{80,16},{96,32},{112,48},{1... | collective-permute-start | bytes 196616 | tf_op jit(solution)/shard_map/ppermute | solution.py:552
  58.6 19.4 %all-to-all-start.2 = ((s16[16,40,128]{2,1,0:T(8,128)(2,1)}), s16[16,40,128]{2,1,0:T(8,128)(2,1)S(1)}, u32[]{:S(2)}, u32[]{:S(2)}) async-start(s16[16,40,128]{2,1,0:T(8,128)(2,1)} %get-tuple-element.20), calls=%async_computation.2 | async-start | bytes 327680 | tf_op jit(solution)/shard_map/all_to_all | solution.py:548
  65.6 12.4 %copy-start.10 = (f32[128,128]{1,0:T(8,128)S(1)}, f32[128,128]{1,0:T(8,128)}, u32[]{:S(2)}) copy-start(f32[128,128]{1,0:T(8,128)} %constant.96.clone.refs_4_) | copy-start | bytes 196612
  65.7 9.0 %collective-permute-start.3 = (bf16[4,128,256]{2,1,0:T(8,128)(2,1)S(1)}, bf16[4,128,256]{2,1,0:T(8,128)(2,1)S(1)}, u32[]{:S(2)}, u32[]{:S(2)}) collective-permute-start(bf16[4,128,256]{2,1,0:T(8,128)(2,1)S(1)} %get-tuple-element.35), channel_id=1, source_target_pairs={{0,128},{16,144},{32,160},{48,176},{64,192},{80,208},{96,224},{112... | collective-permute-start | bytes 786440 | tf_op jit(solution)/shard_map/ppermute | solution.py:552
  68.0 9.5 %collective-permute-start.4 = (bf16[4,128,256]{2,1,0:T(8,128)(2,1)S(1)}, bf16[4,128,256]{2,1,0:T(8,128)(2,1)S(1)}, u32[]{:S(2)}, u32[]{:S(2)}) collective-permute-start(bf16[4,128,256]{2,1,0:T(8,128)(2,1)S(1)} %get-tuple-element.35), channel_id=1, source_target_pairs={{0,384},{16,400},{32,416},{48,432},{64,448},{80,464},{96,480},{112... | collective-permute-start | bytes 786440 | tf_op jit(solution)/shard_map/ppermute | solution.py:552
  79.9 11.7 %collective-permute-start.5 = (bf16[4,128,256]{2,1,0:T(8,128)(2,1)S(1)}, bf16[4,128,256]{2,1,0:T(8,128)(2,1)S(1)}, u32[]{:S(2)}, u32[]{:S(2)}) collective-permute-start(bf16[4,128,256]{2,1,0:T(8,128)(2,1)S(1)} %collective-permute-done.3.refs_5_), channel_id=1, source_target_pairs={{0,384},{16,400},{32,416},{48,432},{64,448},{80,464},{96,480},{112... | collective-permute-start | bytes 786440 | tf_op jit(solution)/shard_map/ppermute | solution.py:552
  83.3 20.6 %all-to-all-start.3 = ((s16[32,72,128]{2,1,0:T(8,128)(2,1)}), s16[32,72,128]{2,1,0:T(8,128)(2,1)S(1)}, u32[]{:S(2)}, u32[]{:S(2)}) async-start(s16[32,72,128]{2,1,0:T(8,128)(2,1)} %shard_map.205), calls=%async_computation.3 | async-start | bytes 1179648 | tf_op jit(solution)/shard_map/all_to_all | solution.py:548
  91.5 4.5 %copy-start.14 = (f32[8,16384]{1,0:T(8,128)S(1)}, f32[8,16384]{1,0:T(8,128)}, u32[]{:S(2)}) copy-start(f32[8,16384]{1,0:T(8,128)} %param.25) | copy-start | bytes 1572868
  91.5 0.7 copy-start.12
  92.2 28.9 %collective-permute-start.6 = (bf16[16,128,256]{2,1,0:T(8,128)(2,1)S(1)}, bf16[16,128,256]{2,1,0:T(8,128)(2,1)S(1)}, u32[]{:S(2)}, u32[]{:S(2)}) collective-permute-start(bf16[16,128,256]{2,1,0:T(8,128)(2,1)S(1)} %constant_dynamic-update-slice_fusion.4.low), channel_id=1, source_target_pairs={{0,16},{16,0},{32,48},{48,32},{64,80},{80,64},{96,112},{112,96},{1... | collective-permute-start | bytes 3145736 | tf_op jit(solution)/shard_map/ppermute | solution.py:552
  103.9 0.8 copy-start.11
  110.0 11.1 %copy-start.1 = (f32[1,128,256]{2,1,0:T(8,128)S(1)}, f32[1,128,256]{2,1,0:T(8,128)}, u32[]{:S(2)}) copy-start(f32[1,128,256]{2,1,0:T(8,128)} %param.19) | copy-start | bytes 393220
  110.0 11.1 %copy-start.2 = (f32[1,128,256]{2,1,0:T(8,128)S(1)}, f32[1,128,256]{2,1,0:T(8,128)}, u32[]{:S(2)}) copy-start(f32[1,128,256]{2,1,0:T(8,128)} %param.20) | copy-start | bytes 393220
  110.0 21.7 %all-to-all-start.4 = ((f32[16,16,128]{2,1,0:T(8,128)}), f32[16,16,128]{2,1,0:T(8,128)S(1)}, u32[]{:S(2)}, u32[]{:S(2)}) async-start(f32[16,16,128]{2,1,0:T(8,128)} %shard_map.206), calls=%async_computation.4 | async-start | bytes 262144 | tf_op jit(solution)/shard_map/all_to_all | solution.py:548
  121.1 10.6 %copy-start.3 = (bf16[2,256,256]{2,1,0:T(8,128)(2,1)S(1)}, bf16[2,256,256]{2,1,0:T(8,128)(2,1)}, u32[]{:S(2)}) copy-start(bf16[2,256,256]{2,1,0:T(8,128)(2,1)} %constant.87.clone.table_hbm.table) | copy-start | bytes 786436
  153.1 13.1 %all-to-all-start.6 = ((f32[32,1,256]{2,1,0:T(1,128)}), f32[32,1,256]{2,1,0:T(1,128)S(1)}, u32[]{:S(2)}, u32[]{:S(2)}) async-start(f32[32,1,256]{2,1,0:T(1,128)} %get-tuple-element.26), calls=%async_computation.6 | async-start | bytes 65536 | tf_op jit(solution)/shard_map/all_to_all | solution.py:548

commit v5 on v4

--- a/solution.py
+++ b/solution.py
@@ -597,8 +597,7 @@
         in_smem=(0,),
         late=(y1, y3),
     )
-    near, hartree = after(y1, hartree)
-    y2 = across(near, 24)
+    (row, y1, y2, y3), _ = after((row, y1, across(y1, 24), y3), hartree)
     xc_planes, _ = after(xc_kernel, hartree)
     xc_planes = xc_planes.reshape(PL, N, N)
     hartree = swap(hartree, "band")
@@ -609,7 +608,6 @@
         xc_planes, occ_planes, t["x_forward"], t["y_forward"],
         in_hbm=(2, 3, 4, 5, 6, 7),
         vmem=59.8,
-        late=(y2,),
         scratch=[pltpu.VMEM((2 * N * PL, N), F32), bf_scratch(8 * N, 2 * N), pltpu.VMEM((2, 2 * N, N), F32)],
     )
     low = jnp.concatenate([row, y1, y2, y3], axis=0)

time: 169 us -> 164 us (0.970)
  starting transfers between devices: 82.2 us -> 78.8 us
    ppermute x7, starting transfers between devices: 24.8 us -> 22.6 us  [across(): return lax.ppermute(blocks, 'band', [(i, i ^ bit) for i in range(BANDS)])]
    ppermute x7, waiting for transfers between devices: 14.3 us -> 12.1 us  [across(): return lax.ppermute(blocks, 'band', [(i, i ^ bit) for i in range(BANDS)])]
  transfers between devices with their start and end apart: 13 -> 13, of which waited for: 10 -> 9; matrix products, arithmetic and copies ran while one was open for 1% -> 1% of each run, Pallas kernels for 6% -> 8%
where the time goes in v5:
time: 164 us; the launch traced here: 163 us
  starting transfers between devices  78.8 us (48%)
  waiting for transfers between devices  36.2 us (22%)
  Pallas kernels  25 us (15%)
  blocking collectives  17.6 us (11%)
  local copies, waits for them, and re-layouts  2.65 us (2%)
  between operations  2.5 us (2%)
    all_to_all x6, starting transfers between devices, swap(): return lax.all_to_all(value, axis, 0, 0, tiled=True)  56.2 us
    pallas_call x10, Pallas kernels, call(): pl.pallas_call(inner, out_shape=out, in_specs=[*(pl.BlockSpec(memory_spac...  25 us
    all_to_all x6, waiting for transfers between devices, swap(): return lax.all_to_all(value, axis, 0, 0, tiled=True)  24.1 us
    ppermute x7, starting transfers between devices, across(): return lax.ppermute(blocks, 'band', [(i, i ^ bit) for i in range(BANDS)])  22.6 us
    all_to_all x1, blocking collectives, swap(): return lax.all_to_all(value, axis, 0, 0, tiled=True)  17.6 us
    ppermute x7, waiting for transfers between devices, across(): return lax.ppermute(blocks, 'band', [(i, i ^ bit) for i in range(BANDS)])  12.1 us
  transfers between devices with their start and end apart: 13, of which 9 were waited for; matrix products, arithmetic and copies ran while one was open for 1% of the time, Pallas kernels for 8%

profile of v5, /device:TPU:1, one launch (start us, length us, event | category | flops | bytes accessed | tf_op | source)
XLA Modules:
  0.0 162.9 jit_solution(13846884744586701484)
XLA Ops:
  0.6 2.1 %shard_map.202 = f32[16,16,128]{2,1,0:T(8,128)} custom-call(f32[128,256]{1,0:T(8,128)} %bitcast.20, bf16[2,256,256]{2,1,0:T(8,128)(2,1)} %constant.87.clone.table_hbm.table), custom_call_target="tpu_custom_call" | custom-call | tf_op jit(solution)/shard_map/pallas_call | solution.py:134
  2.8 15.9 %all-to-all-start = ((f32[16,16,128]{2,1,0:T(8,128)}), f32[16,16,128]{2,1,0:T(8,128)S(1)}, u32[]{:S(2)}, u32[]{:S(2)}) async-start(f32[16,16,128]{2,1,0:T(8,128)} %shard_map.202), calls=%async_computation | async-start | bytes 262144 | tf_op jit(solution)/shard_map/all_to_all | solution.py:548
  18.8 4.4 %collective-permute-start.1 = (bf16[1,128,256]{2,1,0:T(8,128)(2,1)S(1)}, bf16[1,128,256]{2,1,0:T(8,128)(2,1)S(1)}, u32[]{:S(2)}, u32[]{:S(2)}) collective-permute-start(bf16[1,128,256]{2,1,0:T(8,128)(2,1)S(1)} %copy-done.6), channel_id=1, source_target_pairs={{0,96},{16,112},{32,64},{48,80},{64,32},{80,48},{96,0},{112,16},{1... | collective-permute-start | bytes 196616 | tf_op jit(solution)/shard_map/ppermute | solution.py:552
  23.2 1.9 %collective-permute-start = (bf16[1,128,256]{2,1,0:T(8,128)(2,1)S(1)}, bf16[1,128,256]{2,1,0:T(8,128)(2,1)S(1)}, u32[]{:S(2)}, u32[]{:S(2)}) collective-permute-start(bf16[1,128,256]{2,1,0:T(8,128)(2,1)S(1)} %copy-done.6), channel_id=1, source_target_pairs={{0,32},{16,48},{32,0},{48,16},{64,96},{80,112},{96,64},{112,80},{1... | collective-permute-start | bytes 196616 | tf_op jit(solution)/shard_map/ppermute | solution.py:552
  25.3 3.2 %collective-permute-done.refs_7_ = bf16[1,128,256]{2,1,0:T(8,128)(2,1)S(1)} collective-permute-done((bf16[1,128,256]{2,1,0:T(8,128)(2,1)S(1)}, bf16[1,128,256]{2,1,0:T(8,128)(2,1)S(1)}, u32[]{:S(2)}, u32[]{:S(2)}) %collective-permute-start) | collective-permute-done | bytes 65568 | tf_op jit(solution)/shard_map/ppermute | solution.py:552
  28.5 2.2 %all-to-all-done.refs_0_ = f32[16,16,128]{2,1,0:T(8,128)S(1)} async-done(((f32[16,16,128]{2,1,0:T(8,128)}), f32[16,16,128]{2,1,0:T(8,128)S(1)}, u32[]{:S(2)}, u32[]{:S(2)}) %all-to-all-start) | async-done | bytes 131104 | tf_op jit(solution)/shard_map/all_to_all | solution.py:548
  30.7 4.8 %shard_map.203 = f32[1024,128]{1,0:T(8,128)} custom-call(f32[16,16,128]{2,1,0:T(8,128)S(1)} %all-to-all-done.refs_0_, s32[1,2048]{1,0:T(1,128)S(1)} %bitcast.29, bf16[256,256]{1,0:T(8,128)(2,1)S(1)} %copy-done.8, bf16[512,256]{1,0:T(8,128)(2,1)S(1)} %copy-done.5, bf16[2,8,128,128]{3,2,1,0:T(8,128)(2,1)S(1)} %copy.28, bf16[256,256]{1,0:T(8,128)(2,1)S(1)} %copy-done.4, ...), custom_call_target="tpu_custom_call" | custom-call | tf_op jit(solution)/shard_map/pallas_call | solution.py:134
  35.6 10.7 %all-to-all-start.1 = ((f32[32,32,128]{2,1,0:T(8,128)}), f32[32,32,128]{2,1,0:T(8,128)S(1)}, u32[]{:S(2)}, u32[]{:S(2)}) async-start(f32[32,32,128]{2,1,0:T(8,128)} %bitcast.4), calls=%async_computation.1 | async-start | bytes 1048576 | tf_op jit(solution)/shard_map/all_to_all | solution.py:548
  46.3 4.8 %collective-permute-start.2 = (bf16[1,128,256]{2,1,0:T(8,128)(2,1)S(1)}, bf16[1,128,256]{2,1,0:T(8,128)(2,1)S(1)}, u32[]{:S(2)}, u32[]{:S(2)}) collective-permute-start(bf16[1,128,256]{2,1,0:T(8,128)(2,1)S(1)} %copy-done.6), channel_id=1, source_target_pairs={{0,64},{16,80},{32,96},{48,112},{64,0},{80,16},{96,32},{112,48},{1... | collective-permute-start | bytes 196616 | tf_op jit(solution)/shard_map/ppermute | solution.py:552
  51.1 5.9 %collective-permute-done.2.refs_1_ = bf16[1,128,256]{2,1,0:T(8,128)(2,1)S(1)} collective-permute-done((bf16[1,128,256]{2,1,0:T(8,128)(2,1)S(1)}, bf16[1,128,256]{2,1,0:T(8,128)(2,1)S(1)}, u32[]{:S(2)}, u32[]{:S(2)}) %collective-permute-start.2) | collective-permute-done | bytes 65568 | tf_op jit(solution)/shard_map/ppermute | solution.py:552
  58.6 5.7 %all-to-all-start.2 = ((s16[16,40,128]{2,1,0:T(8,128)(2,1)}), s16[16,40,128]{2,1,0:T(8,128)(2,1)S(1)}, u32[]{:S(2)}, u32[]{:S(2)}) async-start(s16[16,40,128]{2,1,0:T(8,128)(2,1)} %get-tuple-element.22), calls=%async_computation.2 | async-start | bytes 327680 | tf_op jit(solution)/shard_map/all_to_all | solution.py:548
  64.4 2.3 %collective-permute-start.3 = (bf16[4,128,256]{2,1,0:T(8,128)(2,1)S(1)}, bf16[4,128,256]{2,1,0:T(8,128)(2,1)S(1)}, u32[]{:S(2)}, u32[]{:S(2)}) collective-permute-start(bf16[4,128,256]{2,1,0:T(8,128)(2,1)S(1)} %constant_dynamic-update-slice_fusion), channel_id=1, source_target_pairs={{0,128},{16,144},{32,160},{48,176},{64,192},{80,208},{96,224},{112... | collective-permute-start | bytes 786440 | tf_op jit(solution)/shard_map/ppermute | solution.py:552
  66.7 3.7 %collective-permute-start.4 = (bf16[4,128,256]{2,1,0:T(8,128)(2,1)S(1)}, bf16[4,128,256]{2,1,0:T(8,128)(2,1)S(1)}, u32[]{:S(2)}, u32[]{:S(2)}) collective-permute-start(bf16[4,128,256]{2,1,0:T(8,128)(2,1)S(1)} %constant_dynamic-update-slice_fusion), channel_id=1, source_target_pairs={{0,384},{16,400},{32,416},{48,432},{64,448},{80,464},{96,480},{112... | collective-permute-start | bytes 786440 | tf_op jit(solution)/shard_map/ppermute | solution.py:552
  70.4 3.0 %collective-permute-done.3.refs_5_ = bf16[4,128,256]{2,1,0:T(8,128)(2,1)S(1)} collective-permute-done((bf16[4,128,256]{2,1,0:T(8,128)(2,1)S(1)}, bf16[4,128,256]{2,1,0:T(8,128)(2,1)S(1)}, u32[]{:S(2)}, u32[]{:S(2)}) %collective-permute-start.3) | collective-permute-done | bytes 262176 | tf_op jit(solution)/shard_map/ppermute | solution.py:552
  73.4 3.1 %collective-permute-start.5 = (bf16[4,128,256]{2,1,0:T(8,128)(2,1)S(1)}, bf16[4,128,256]{2,1,0:T(8,128)(2,1)S(1)}, u32[]{:S(2)}, u32[]{:S(2)}) collective-permute-start(bf16[4,128,256]{2,1,0:T(8,128)(2,1)S(1)} %collective-permute-done.3.refs_5_), channel_id=1, source_target_pairs={{0,384},{16,400},{32,416},{48,432},{64,448},{80,464},{96,480},{112... | collective-permute-start | bytes 786440 | tf_op jit(solution)/shard_map/ppermute | solution.py:552
  76.8 1.8 %shard_map.205 = s16[32,72,128]{2,1,0:T(8,128)(2,1)} custom-call(s32[2]{0:T(128)S(1)} %pad_add_fusion.refs_0_.where, s16[16,40,128]{2,1,0:T(8,128)(2,1)S(1)} %all-to-all-done.2.refs_1_, f32[32,128]{1,0:T(8,128)S(1)} %get-tuple-element.23.refs_2_, bf16[256,256]{1,0:T(8,128)(2,1)S(1)} %copy-done.4, f32[128,128]{1,0:T(8,128)S(1)} %copy-done.10, ...), custom_call_target="tpu_custom_call" | custom-call | tf_op jit(solution)/shard_map/pallas_call | solution.py:134
  78.6 8.4 %all-to-all-start.3 = ((s16[32,72,128]{2,1,0:T(8,128)(2,1)}), s16[32,72,128]{2,1,0:T(8,128)(2,1)S(1)}, u32[]{:S(2)}, u32[]{:S(2)}) async-start(s16[32,72,128]{2,1,0:T(8,128)(2,1)} %shard_map.205), calls=%async_computation.3 | async-start | bytes 1179648 | tf_op jit(solution)/shard_map/all_to_all | solution.py:548
  87.2 2.3 %collective-permute-start.6 = (bf16[16,128,256]{2,1,0:T(8,128)(2,1)S(1)}, bf16[16,128,256]{2,1,0:T(8,128)(2,1)S(1)}, u32[]{:S(2)}, u32[]{:S(2)}) collective-permute-start(bf16[16,128,256]{2,1,0:T(8,128)(2,1)S(1)} %constant_dynamic-update-slice_fusion.4.low), channel_id=1, source_target_pairs={{0,16},{16,0},{32,48},{48,32},{64,80},{80,64},{96,112},{112,96},{1... | collective-permute-start | bytes 3145736 | tf_op jit(solution)/shard_map/ppermute | solution.py:552
  89.4 0.9 copy.27
  90.3 8.9 %all-to-all-done.3.recv = s16[32,72,128]{2,1,0:T(8,128)(2,1)S(1)} async-done(((s16[32,72,128]{2,1,0:T(8,128)(2,1)}), s16[32,72,128]{2,1,0:T(8,128)(2,1)S(1)}, u32[]{:S(2)}, u32[]{:S(2)}) %all-to-all-start.3) | async-done | bytes 589856 | tf_op jit(solution)/shard_map/all_to_all | solution.py:548
  99.3 0.8 copy-done.11
  100.1 5.3 %shard_map.206 = f32[16,16,128]{2,1,0:T(8,128)} custom-call(s16[32,72,128]{2,1,0:T(8,128)(2,1)} %copy-done.11, s32[1,2048]{1,0:T(1,128)} %bitcast.30, bf16[256,256]{1,0:T(8,128)(2,1)} %constant.93.clone.modes_hbm, bf16[256,256]{1,0:T(8,128)(2,1)} %constant.94.clone.modes_t_hbm, f32[8,128,128]{2,1,0:T(8,128)} %bitcast.31, bf16[2,8,128,128]{3,2,1,0:T(8,128)(2,1)} %copy-done, ...), custom_call_target="tpu_custom_call" | custom-call | tf_op jit(solution)/shard_map/pallas_call | solution.py:134
  105.4 9.6 %all-to-all-start.4 = ((f32[16,16,128]{2,1,0:T(8,128)}), f32[16,16,128]{2,1,0:T(8,128)S(1)}, u32[]{:S(2)}, u32[]{:S(2)}) async-start(f32[16,16,128]{2,1,0:T(8,128)} %shard_map.206), calls=%async_computation.4 | async-start | bytes 262144 | tf_op jit(solution)/shard_map/all_to_all | solution.py:548
  116.3 2.9 %shard_map.207.fixed = f32[8,128]{1,0:T(8,128)S(1)} custom-call(s32[2]{0:T(128)S(1)} %pad_add_fusion.refs_0_.where, bf16[16,128,256]{2,1,0:T(8,128)(2,1)S(1)} %constant_dynamic-update-slice_fusion.4.low, bf16[16,128,256]{2,1,0:T(8,128)(2,1)S(1)} %collective-permute-done.6.high, f32[128,256]{1,0:T(8,128)S(1)} %bitcast.21, f32[128,256]{1,0:T(8,128)S(1)} %bitcast.25, ...), custom_call_target="tpu_custom_call" | custom-call | tf_op jit(solution)/shard_map/pallas_call | solution.py:134
  119.3 7.7 %all-to-all-done.4.recv = f32[16,16,128]{2,1,0:T(8,128)S(1)} async-done(((f32[16,16,128]{2,1,0:T(8,128)}), f32[16,16,128]{2,1,0:T(8,128)S(1)}, u32[]{:S(2)}, u32[]{:S(2)}) %all-to-all-start.4) | async-done | bytes 131104 | tf_op jit(solution)/shard_map/all_to_all | solution.py:548
  127.0 2.8 %shard_map.208 = (f32[128,256]{1,0:T(8,128)S(1)}, f32[16,1,384]{2,1,0:T(1,128)S(1)}) custom-call(f32[16,16,128]{2,1,0:T(8,128)S(1)} %all-to-all-done.4.recv, bf16[2,256,256]{2,1,0:T(8,128)(2,1)S(1)} %copy-done.3, s32[2]{0:T(128)S(1)} %pad_add_fusion.refs_0_.where, f32[2]{0:T(128)S(1)} %pad_maximum_fusion.scalars, f32[128,256]{1,0:T(8,128)S(1)} %bitcast.22, ...), custom_call_target="tpu_custom_call" | custom-call | tf_op jit(solution)/shard_map/pallas_call | solution.py:134
  129.7 17.6 %all_to_all.35.recv = f32[16,1,384]{2,1,0:T(1,128)S(1)} all-to-all(f32[16,1,384]{2,1,0:T(1,128)S(1)} %get-tuple-element.29), channel_id=1, replica_groups=mesh['band'=32,'slab'=16] {'slab'}, dimensions={0} | all-to-all | bytes 49152 | tf_op jit(solution)/shard_map/all_to_all | solution.py:548
  147.3 1.0 shard_map.209
  148.4 5.8 %all-to-all-start.6 = ((f32[32,1,256]{2,1,0:T(1,128)}), f32[32,1,256]{2,1,0:T(1,128)S(1)}, u32[]{:S(2)}, u32[]{:S(2)}) async-start(f32[32,1,256]{2,1,0:T(1,128)} %get-tuple-element.30), calls=%async_computation.6 | async-start | bytes 65536 | tf_op jit(solution)/shard_map/all_to_all | solution.py:548
  154.9 2.2 %shard_map.210.rest = f32[128,256]{1,0:T(8,128)S(1)} custom-call(f32[1,128]{1,0:T(1,128)S(1)} %get-tuple-element.31.margin, s32[2]{0:T(128)S(1)} %pad_add_fusion.refs_0_.where, f32[2]{0:T(128)S(1)} %pad_maximum_fusion.scalars, f32[128,256]{1,0:T(8,128)S(1)} %bitcast.23, f32[128,256]{1,0:T(8,128)S(1)} %bitcast.27, f32[128,256]{1,0:T(8,128)S(1)} %get-tuple-element.32.applied, ...), custom_call_target="tpu_custom_call" | custom-call | tf_op jit(solution)/shard_map/pallas_call | solution.py:134
  157.1 4.3 %all-to-all-done.6.recv = f32[32,1,256]{2,1,0:T(1,128)S(1)} async-done(((f32[32,1,256]{2,1,0:T(1,128)}), f32[32,1,256]{2,1,0:T(1,128)S(1)}, u32[]{:S(2)}, u32[]{:S(2)}) %all-to-all-start.6) | async-done | bytes 32800 | tf_op jit(solution)/shard_map/all_to_all | solution.py:548
  161.5 1.3 shard_map.211
  (50 shorter events, 2.8 us)
Async XLA Ops:
  0.6 24.5 %copy-start.12 = (bf16[1,2,8,16384]{3,2,1,0:T(8,128)(2,1)S(1)}, bf16[1,2,8,16384]{3,2,1,0:T(8,128)(2,1)}, u32[]{:S(2)}) copy-start(bf16[1,2,8,16384]{3,2,1,0:T(8,128)(2,1)} %param.24) | copy-start | bytes 1572868
  2.8 15.9 %copy-start.14 = (s32[2048]{0:T(1024)S(1)}, s32[2048]{0:T(1024)}, u32[]{:S(2)}) copy-start(s32[2048]{0:T(1024)} %param.26) | copy-start | bytes 24580
  2.8 16.0 %copy-start.6 = (bf16[1,128,256]{2,1,0:T(8,128)(2,1)S(1)}, bf16[1,128,256]{2,1,0:T(8,128)(2,1)}, u32[]{:S(2)}) copy-start(bf16[1,128,256]{2,1,0:T(8,128)(2,1)} %param.23) | copy-start | bytes 196612
  2.8 27.9 %all-to-all-start = ((f32[16,16,128]{2,1,0:T(8,128)}), f32[16,16,128]{2,1,0:T(8,128)S(1)}, u32[]{:S(2)}, u32[]{:S(2)}) async-start(f32[16,16,128]{2,1,0:T(8,128)} %shard_map.202), calls=%async_computation | async-start | bytes 262144 | tf_op jit(solution)/shard_map/all_to_all | solution.py:548
  18.7 12.0 %copy-start.9 = (s32[2048]{0:T(1024)}, s32[2048]{0:T(1024)S(1)}, u32[]{:S(2)}) copy-start(s32[2048]{0:T(1024)S(1)} %fusion.4) | copy-start | bytes 24580
  18.8 6.5 %collective-permute-start.1 = (bf16[1,128,256]{2,1,0:T(8,128)(2,1)S(1)}, bf16[1,128,256]{2,1,0:T(8,128)(2,1)S(1)}, u32[]{:S(2)}, u32[]{:S(2)}) collective-permute-start(bf16[1,128,256]{2,1,0:T(8,128)(2,1)S(1)} %copy-done.6), channel_id=1, source_target_pairs={{0,96},{16,112},{32,64},{48,80},{64,32},{80,48},{96,0},{112,16},{1... | collective-permute-start | bytes 196616 | tf_op jit(solution)/shard_map/ppermute | solution.py:552
  23.2 5.3 %collective-permute-start = (bf16[1,128,256]{2,1,0:T(8,128)(2,1)S(1)}, bf16[1,128,256]{2,1,0:T(8,128)(2,1)S(1)}, u32[]{:S(2)}, u32[]{:S(2)}) collective-permute-start(bf16[1,128,256]{2,1,0:T(8,128)(2,1)S(1)} %copy-done.6), channel_id=1, source_target_pairs={{0,32},{16,48},{32,0},{48,16},{64,96},{80,112},{96,64},{112,80},{1... | collective-permute-start | bytes 196616 | tf_op jit(solution)/shard_map/ppermute | solution.py:552
  25.1 5.6 %copy-start.4 = (bf16[256,256]{1,0:T(8,128)(2,1)S(1)}, bf16[256,256]{1,0:T(8,128)(2,1)}, u32[]{:S(2)}) copy-start(bf16[256,256]{1,0:T(8,128)(2,1)} %constant.92.clone.refs_5_.refs_3_) | copy-start | bytes 393220
  25.1 5.6 %copy-start.5 = (bf16[512,256]{1,0:T(8,128)(2,1)S(1)}, bf16[512,256]{1,0:T(8,128)(2,1)}, u32[]{:S(2)}) copy-start(bf16[512,256]{1,0:T(8,128)(2,1)} %constant.90.clone.refs_3_) | copy-start | bytes 786436
  25.1 5.6 %copy-start.7 = (bf16[256,256]{1,0:T(8,128)(2,1)S(1)}, bf16[256,256]{1,0:T(8,128)(2,1)}, u32[]{:S(2)}) copy-start(bf16[256,256]{1,0:T(8,128)(2,1)} %constant.95.clone.refs_6_) | copy-start | bytes 393220
  25.1 5.6 %copy-start.8 = (bf16[256,256]{1,0:T(8,128)(2,1)S(1)}, bf16[256,256]{1,0:T(8,128)(2,1)}, u32[]{:S(2)}) copy-start(bf16[256,256]{1,0:T(8,128)(2,1)} %constant.88.clone.refs_2_) | copy-start | bytes 393220
  25.2 10.3 %copy-start = (bf16[2,8,128,128]{3,2,1,0:T(8,128)(2,1)}, bf16[2,8,128,128]{3,2,1,0:T(8,128)(2,1)S(1)}, u32[]{:S(2)}) copy-start(bf16[2,8,128,128]{3,2,1,0:T(8,128)(2,1)S(1)} %copy.28) | copy-start | bytes 1572868
  35.6 22.3 %all-to-all-start.1 = ((f32[32,32,128]{2,1,0:T(8,128)}), f32[32,32,128]{2,1,0:T(8,128)S(1)}, u32[]{:S(2)}, u32[]{:S(2)}) async-start(f32[32,32,128]{2,1,0:T(8,128)} %bitcast.4), calls=%async_computation.1 | async-start | bytes 1048576 | tf_op jit(solution)/shard_map/all_to_all | solution.py:548
  46.3 10.8 %collective-permute-start.2 = (bf16[1,128,256]{2,1,0:T(8,128)(2,1)S(1)}, bf16[1,128,256]{2,1,0:T(8,128)(2,1)S(1)}, u32[]{:S(2)}, u32[]{:S(2)}) collective-permute-start(bf16[1,128,256]{2,1,0:T(8,128)(2,1)S(1)} %copy-done.6), channel_id=1, source_target_pairs={{0,64},{16,80},{32,96},{48,112},{64,0},{80,16},{96,32},{112,48},{1... | collective-permute-start | bytes 196616 | tf_op jit(solution)/shard_map/ppermute | solution.py:552
  58.6 18.2 %all-to-all-start.2 = ((s16[16,40,128]{2,1,0:T(8,128)(2,1)}), s16[16,40,128]{2,1,0:T(8,128)(2,1)S(1)}, u32[]{:S(2)}, u32[]{:S(2)}) async-start(s16[16,40,128]{2,1,0:T(8,128)(2,1)} %get-tuple-element.22), calls=%async_computation.2 | async-start | bytes 327680 | tf_op jit(solution)/shard_map/all_to_all | solution.py:548
  64.3 12.4 %copy-start.10 = (f32[128,128]{1,0:T(8,128)S(1)}, f32[128,128]{1,0:T(8,128)}, u32[]{:S(2)}) copy-start(f32[128,128]{1,0:T(8,128)} %constant.96.clone.refs_4_) | copy-start | bytes 196612
  64.4 9.0 %collective-permute-start.3 = (bf16[4,128,256]{2,1,0:T(8,128)(2,1)S(1)}, bf16[4,128,256]{2,1,0:T(8,128)(2,1)S(1)}, u32[]{:S(2)}, u32[]{:S(2)}) collective-permute-start(bf16[4,128,256]{2,1,0:T(8,128)(2,1)S(1)} %constant_dynamic-update-slice_fusion), channel_id=1, source_target_pairs={{0,128},{16,144},{32,160},{48,176},{64,192},{80,208},{96,224},{112... | collective-permute-start | bytes 786440 | tf_op jit(solution)/shard_map/ppermute | solution.py:552
  66.7 9.9 %collective-permute-start.4 = (bf16[4,128,256]{2,1,0:T(8,128)(2,1)S(1)}, bf16[4,128,256]{2,1,0:T(8,128)(2,1)S(1)}, u32[]{:S(2)}, u32[]{:S(2)}) collective-permute-start(bf16[4,128,256]{2,1,0:T(8,128)(2,1)S(1)} %constant_dynamic-update-slice_fusion), channel_id=1, source_target_pairs={{0,384},{16,400},{32,416},{48,432},{64,448},{80,464},{96,480},{112... | collective-permute-start | bytes 786440 | tf_op jit(solution)/shard_map/ppermute | solution.py:552
  73.4 13.7 %collective-permute-start.5 = (bf16[4,128,256]{2,1,0:T(8,128)(2,1)S(1)}, bf16[4,128,256]{2,1,0:T(8,128)(2,1)S(1)}, u32[]{:S(2)}, u32[]{:S(2)}) collective-permute-start(bf16[4,128,256]{2,1,0:T(8,128)(2,1)S(1)} %collective-permute-done.3.refs_5_), channel_id=1, source_target_pairs={{0,384},{16,400},{32,416},{48,432},{64,448},{80,464},{96,480},{112... | collective-permute-start | bytes 786440 | tf_op jit(solution)/shard_map/ppermute | solution.py:552
  78.6 20.7 %all-to-all-start.3 = ((s16[32,72,128]{2,1,0:T(8,128)(2,1)}), s16[32,72,128]{2,1,0:T(8,128)(2,1)S(1)}, u32[]{:S(2)}, u32[]{:S(2)}) async-start(s16[32,72,128]{2,1,0:T(8,128)(2,1)} %shard_map.205), calls=%async_computation.3 | async-start | bytes 1179648 | tf_op jit(solution)/shard_map/all_to_all | solution.py:548
  87.1 2.4 %copy-start.13 = (f32[8,16384]{1,0:T(8,128)S(1)}, f32[8,16384]{1,0:T(8,128)}, u32[]{:S(2)}) copy-start(f32[8,16384]{1,0:T(8,128)} %param.25) | copy-start | bytes 1572868
  87.2 29.2 %collective-permute-start.6 = (bf16[16,128,256]{2,1,0:T(8,128)(2,1)S(1)}, bf16[16,128,256]{2,1,0:T(8,128)(2,1)S(1)}, u32[]{:S(2)}, u32[]{:S(2)}) collective-permute-start(bf16[16,128,256]{2,1,0:T(8,128)(2,1)S(1)} %constant_dynamic-update-slice_fusion.4.low), channel_id=1, source_target_pairs={{0,16},{16,0},{32,48},{48,32},{64,80},{80,64},{96,112},{112,96},{1... | collective-permute-start | bytes 3145736 | tf_op jit(solution)/shard_map/ppermute | solution.py:552
  99.3 0.8 copy-start.11
  105.3 11.0 %copy-start.1 = (f32[1,128,256]{2,1,0:T(8,128)S(1)}, f32[1,128,256]{2,1,0:T(8,128)}, u32[]{:S(2)}) copy-start(f32[1,128,256]{2,1,0:T(8,128)} %param.19) | copy-start | bytes 393220
  105.4 11.0 %copy-start.2 = (f32[1,128,256]{2,1,0:T(8,128)S(1)}, f32[1,128,256]{2,1,0:T(8,128)}, u32[]{:S(2)}) copy-start(f32[1,128,256]{2,1,0:T(8,128)} %param.20) | copy-start | bytes 393220
  105.4 21.6 %all-to-all-start.4 = ((f32[16,16,128]{2,1,0:T(8,128)}), f32[16,16,128]{2,1,0:T(8,128)S(1)}, u32[]{:S(2)}, u32[]{:S(2)}) async-start(f32[16,16,128]{2,1,0:T(8,128)} %shard_map.206), calls=%async_computation.4 | async-start | bytes 262144 | tf_op jit(solution)/shard_map/all_to_all | solution.py:548
  116.3 10.6 %copy-start.3 = (bf16[2,256,256]{2,1,0:T(8,128)(2,1)S(1)}, bf16[2,256,256]{2,1,0:T(8,128)(2,1)}, u32[]{:S(2)}) copy-start(bf16[2,256,256]{2,1,0:T(8,128)(2,1)} %constant.87.clone.table_hbm.table) | copy-start | bytes 786436
  148.4 13.1 %all-to-all-start.6 = ((f32[32,1,256]{2,1,0:T(1,128)}), f32[32,1,256]{2,1,0:T(1,128)S(1)}, u32[]{:S(2)}, u32[]{:S(2)}) async-start(f32[32,1,256]{2,1,0:T(1,128)} %get-tuple-element.30), calls=%async_computation.6 | async-start | bytes 65536 | tf_op jit(solution)/shard_map/all_to_all | solution.py:548

commit v6 on v5

--- a/solution.py
+++ b/solution.py
@@ -590,14 +590,13 @@
         late=(x2,),
     )
     row = jnp.concatenate([own, x1, x2, x3], axis=0)
-    y1, y3 = across(row, 8), across(row, 24)
+    y1, y2, y3 = across(row, 8), across(row, 16), across(row, 24)
     columns = swap(total, "slab")
     hartree = call(
         solve_z, shape(BANDS, 2 * AX * PL + 8, N, dtype=jnp.int16), where, columns, own_modes, t["modes_left"], t["modes_t32"],
         in_smem=(0,),
-        late=(y1, y3),
-    )
-    (row, y1, y2, y3), _ = after((row, y1, across(y1, 24), y3), hartree)
+    )
+    (row, y1, y2, y3), _ = after((row, y1, y2, y3), hartree)
     xc_planes, _ = after(xc_kernel, hartree)
     xc_planes = xc_planes.reshape(PL, N, N)
     hartree = swap(hartree, "band")

time: 164 us -> 161 us (0.982)
  starting transfers between devices: 78.8 us -> 75.4 us
    all_to_all x6, starting transfers between devices: 56.2 us -> 53.1 us  [swap(): return lax.all_to_all(value, axis, 0, 0, tiled=True)]
    all_to_all x6, waiting for transfers between devices: 24.1 us -> 27.2 us  [swap(): return lax.all_to_all(value, axis, 0, 0, tiled=True)]
    ppermute x7, waiting for transfers between devices: 12.1 us -> 9.18 us  [across(): return lax.ppermute(blocks, 'band', [(i, i ^ bit) for i in range(BANDS)])]
  transfers between devices with their start and end apart: 13 -> 13, of which waited for: 9 -> 8; matrix products, arithmetic and copies ran while one was open for 1% -> 1% of each run, Pallas kernels for 8% -> 8%
where the time goes in v6:
time: 161 us; the launch traced here: 160 us
  starting transfers between devices  75.4 us (47%)
  waiting for transfers between devices  36.4 us (23%)
  Pallas kernels  25 us (16%)
  blocking collectives  17.6 us (11%)
  local copies, waits for them, and re-layouts  2.65 us (2%)
  between operations  2.53 us (2%)
    all_to_all x6, starting transfers between devices, swap(): return lax.all_to_all(value, axis, 0, 0, tiled=True)  53.1 us
    all_to_all x6, waiting for transfers between devices, swap(): return lax.all_to_all(value, axis, 0, 0, tiled=True)  27.2 us
    pallas_call x10, Pallas kernels, call(): pl.pallas_call(inner, out_shape=out, in_specs=[*(pl.BlockSpec(memory_spac...  25 us
    ppermute x7, starting transfers between devices, across(): return lax.ppermute(blocks, 'band', [(i, i ^ bit) for i in range(BANDS)])  22.4 us
    all_to_all x1, blocking collectives, swap(): return lax.all_to_all(value, axis, 0, 0, tiled=True)  17.6 us
    ppermute x7, waiting for transfers between devices, across(): return lax.ppermute(blocks, 'band', [(i, i ^ bit) for i in range(BANDS)])  9.18 us
  transfers between devices with their start and end apart: 13, of which 8 were waited for; matrix products, arithmetic and copies ran while one was open for 1% of the time, Pallas kernels for 8%

profile of v6, /device:TPU:1, one launch (start us, length us, event | category | flops | bytes accessed | tf_op | source)
XLA Modules:
  0.0 159.8 jit_solution(7184492404719758000)
XLA Ops:
  0.6 2.1 %shard_map.202 = f32[16,16,128]{2,1,0:T(8,128)} custom-call(f32[128,256]{1,0:T(8,128)} %bitcast.20, bf16[2,256,256]{2,1,0:T(8,128)(2,1)} %constant.87.clone.table_hbm.table), custom_call_target="tpu_custom_call" | custom-call | tf_op jit(solution)/shard_map/pallas_call | solution.py:134
  2.8 15.9 %all-to-all-start = ((f32[16,16,128]{2,1,0:T(8,128)}), f32[16,16,128]{2,1,0:T(8,128)S(1)}, u32[]{:S(2)}, u32[]{:S(2)}) async-start(f32[16,16,128]{2,1,0:T(8,128)} %shard_map.202), calls=%async_computation | async-start | bytes 262144 | tf_op jit(solution)/shard_map/all_to_all | solution.py:548
  18.8 4.4 %collective-permute-start.1 = (bf16[1,128,256]{2,1,0:T(8,128)(2,1)S(1)}, bf16[1,128,256]{2,1,0:T(8,128)(2,1)S(1)}, u32[]{:S(2)}, u32[]{:S(2)}) collective-permute-start(bf16[1,128,256]{2,1,0:T(8,128)(2,1)S(1)} %copy-done.6), channel_id=1, source_target_pairs={{0,96},{16,112},{32,64},{48,80},{64,32},{80,48},{96,0},{112,16},{1... | collective-permute-start | bytes 196616 | tf_op jit(solution)/shard_map/ppermute | solution.py:552
  23.2 1.9 %collective-permute-start = (bf16[1,128,256]{2,1,0:T(8,128)(2,1)S(1)}, bf16[1,128,256]{2,1,0:T(8,128)(2,1)S(1)}, u32[]{:S(2)}, u32[]{:S(2)}) collective-permute-start(bf16[1,128,256]{2,1,0:T(8,128)(2,1)S(1)} %copy-done.6), channel_id=1, source_target_pairs={{0,32},{16,48},{32,0},{48,16},{64,96},{80,112},{96,64},{112,80},{1... | collective-permute-start | bytes 196616 | tf_op jit(solution)/shard_map/ppermute | solution.py:552
  25.3 3.2 %collective-permute-done.refs_7_ = bf16[1,128,256]{2,1,0:T(8,128)(2,1)S(1)} collective-permute-done((bf16[1,128,256]{2,1,0:T(8,128)(2,1)S(1)}, bf16[1,128,256]{2,1,0:T(8,128)(2,1)S(1)}, u32[]{:S(2)}, u32[]{:S(2)}) %collective-permute-start) | collective-permute-done | bytes 65568 | tf_op jit(solution)/shard_map/ppermute | solution.py:552
  28.5 2.2 %all-to-all-done.refs_0_ = f32[16,16,128]{2,1,0:T(8,128)S(1)} async-done(((f32[16,16,128]{2,1,0:T(8,128)}), f32[16,16,128]{2,1,0:T(8,128)S(1)}, u32[]{:S(2)}, u32[]{:S(2)}) %all-to-all-start) | async-done | bytes 131104 | tf_op jit(solution)/shard_map/all_to_all | solution.py:548
  30.7 4.8 %shard_map.203 = f32[1024,128]{1,0:T(8,128)} custom-call(f32[16,16,128]{2,1,0:T(8,128)S(1)} %all-to-all-done.refs_0_, s32[1,2048]{1,0:T(1,128)S(1)} %bitcast.29, bf16[256,256]{1,0:T(8,128)(2,1)S(1)} %copy-done.8, bf16[512,256]{1,0:T(8,128)(2,1)S(1)} %copy-done.5, bf16[2,8,128,128]{3,2,1,0:T(8,128)(2,1)S(1)} %copy.28, bf16[256,256]{1,0:T(8,128)(2,1)S(1)} %copy-done.4, ...), custom_call_target="tpu_custom_call" | custom-call | tf_op jit(solution)/shard_map/pallas_call | solution.py:134
  35.6 10.7 %all-to-all-start.1 = ((f32[32,32,128]{2,1,0:T(8,128)}), f32[32,32,128]{2,1,0:T(8,128)S(1)}, u32[]{:S(2)}, u32[]{:S(2)}) async-start(f32[32,32,128]{2,1,0:T(8,128)} %bitcast.4), calls=%async_computation.1 | async-start | bytes 1048576 | tf_op jit(solution)/shard_map/all_to_all | solution.py:548
  46.3 4.8 %collective-permute-start.2 = (bf16[1,128,256]{2,1,0:T(8,128)(2,1)S(1)}, bf16[1,128,256]{2,1,0:T(8,128)(2,1)S(1)}, u32[]{:S(2)}, u32[]{:S(2)}) collective-permute-start(bf16[1,128,256]{2,1,0:T(8,128)(2,1)S(1)} %copy-done.6), channel_id=1, source_target_pairs={{0,64},{16,80},{32,96},{48,112},{64,0},{80,16},{96,32},{112,48},{1... | collective-permute-start | bytes 196616 | tf_op jit(solution)/shard_map/ppermute | solution.py:552
  51.1 6.0 %collective-permute-done.2.refs_1_ = bf16[1,128,256]{2,1,0:T(8,128)(2,1)S(1)} collective-permute-done((bf16[1,128,256]{2,1,0:T(8,128)(2,1)S(1)}, bf16[1,128,256]{2,1,0:T(8,128)(2,1)S(1)}, u32[]{:S(2)}, u32[]{:S(2)}) %collective-permute-start.2) | collective-permute-done | bytes 65568 | tf_op jit(solution)/shard_map/ppermute | solution.py:552
  58.6 5.7 %all-to-all-start.2 = ((s16[16,40,128]{2,1,0:T(8,128)(2,1)}), s16[16,40,128]{2,1,0:T(8,128)(2,1)S(1)}, u32[]{:S(2)}, u32[]{:S(2)}) async-start(s16[16,40,128]{2,1,0:T(8,128)(2,1)} %get-tuple-element.22), calls=%async_computation.2 | async-start | bytes 327680 | tf_op jit(solution)/shard_map/all_to_all | solution.py:548
  64.4 3.6 %collective-permute-start.5 = (bf16[4,128,256]{2,1,0:T(8,128)(2,1)S(1)}, bf16[4,128,256]{2,1,0:T(8,128)(2,1)S(1)}, u32[]{:S(2)}, u32[]{:S(2)}) collective-permute-start(bf16[4,128,256]{2,1,0:T(8,128)(2,1)S(1)} %constant_dynamic-update-slice_fusion), channel_id=1, source_target_pairs={{0,384},{16,400},{32,416},{48,432},{64,448},{80,464},{96,480},{112... | collective-permute-start | bytes 786440 | tf_op jit(solution)/shard_map/ppermute | solution.py:552
  68.0 2.4 %collective-permute-start.4 = (bf16[4,128,256]{2,1,0:T(8,128)(2,1)S(1)}, bf16[4,128,256]{2,1,0:T(8,128)(2,1)S(1)}, u32[]{:S(2)}, u32[]{:S(2)}) collective-permute-start(bf16[4,128,256]{2,1,0:T(8,128)(2,1)S(1)} %constant_dynamic-update-slice_fusion), channel_id=1, source_target_pairs={{0,256},{16,272},{32,288},{48,304},{64,320},{80,336},{96,352},{112... | collective-permute-start | bytes 786440 | tf_op jit(solution)/shard_map/ppermute | solution.py:552
  70.4 3.0 %collective-permute-start.3 = (bf16[4,128,256]{2,1,0:T(8,128)(2,1)S(1)}, bf16[4,128,256]{2,1,0:T(8,128)(2,1)S(1)}, u32[]{:S(2)}, u32[]{:S(2)}) collective-permute-start(bf16[4,128,256]{2,1,0:T(8,128)(2,1)S(1)} %constant_dynamic-update-slice_fusion), channel_id=1, source_target_pairs={{0,128},{16,144},{32,160},{48,176},{64,192},{80,208},{96,224},{112... | collective-permute-start | bytes 786440 | tf_op jit(solution)/shard_map/ppermute | solution.py:552
  73.5 3.3 %all-to-all-done.2.recv = s16[16,40,128]{2,1,0:T(8,128)(2,1)S(1)} async-done(((s16[16,40,128]{2,1,0:T(8,128)(2,1)}), s16[16,40,128]{2,1,0:T(8,128)(2,1)S(1)}, u32[]{:S(2)}, u32[]{:S(2)}) %all-to-all-start.2) | async-done | bytes 163872 | tf_op jit(solution)/shard_map/all_to_all | solution.py:548
  76.8 1.8 %shard_map.205 = s16[32,72,128]{2,1,0:T(8,128)(2,1)} custom-call(s32[2]{0:T(128)S(1)} %pad_add_fusion.where, s16[16,40,128]{2,1,0:T(8,128)(2,1)S(1)} %all-to-all-done.2.recv, f32[32,128]{1,0:T(8,128)S(1)} %get-tuple-element.23.density, bf16[256,256]{1,0:T(8,128)(2,1)S(1)} %copy-done.4, f32[128,128]{1,0:T(8,128)S(1)} %copy-done.10), custom_call_target="tpu_custom_call" | custom-call | tf_op jit(solution)/shard_map/pallas_call | solution.py:134
  78.6 8.4 %all-to-all-start.3 = ((s16[32,72,128]{2,1,0:T(8,128)(2,1)}), s16[32,72,128]{2,1,0:T(8,128)(2,1)S(1)}, u32[]{:S(2)}, u32[]{:S(2)}) async-start(s16[32,72,128]{2,1,0:T(8,128)(2,1)} %shard_map.205), calls=%async_computation.3 | async-start | bytes 1179648 | tf_op jit(solution)/shard_map/all_to_all | solution.py:548
  87.2 2.3 %collective-permute-start.6 = (bf16[16,128,256]{2,1,0:T(8,128)(2,1)S(1)}, bf16[16,128,256]{2,1,0:T(8,128)(2,1)S(1)}, u32[]{:S(2)}, u32[]{:S(2)}) collective-permute-start(bf16[16,128,256]{2,1,0:T(8,128)(2,1)S(1)} %constant_dynamic-update-slice_fusion.4.low), channel_id=1, source_target_pairs={{0,16},{16,0},{32,48},{48,32},{64,80},{80,64},{96,112},{112,96},{1... | collective-permute-start | bytes 3145736 | tf_op jit(solution)/shard_map/ppermute | solution.py:552
  89.5 0.9 copy.27
  90.4 8.9 %all-to-all-done.3.recv = s16[32,72,128]{2,1,0:T(8,128)(2,1)S(1)} async-done(((s16[32,72,128]{2,1,0:T(8,128)(2,1)}), s16[32,72,128]{2,1,0:T(8,128)(2,1)S(1)}, u32[]{:S(2)}, u32[]{:S(2)}) %all-to-all-start.3) | async-done | bytes 589856 | tf_op jit(solution)/shard_map/all_to_all | solution.py:548
  99.3 0.8 copy-done.11
  100.1 5.3 %shard_map.206 = f32[16,16,128]{2,1,0:T(8,128)} custom-call(s16[32,72,128]{2,1,0:T(8,128)(2,1)} %copy-done.11, s32[1,2048]{1,0:T(1,128)} %bitcast.30, bf16[256,256]{1,0:T(8,128)(2,1)} %constant.93.clone.modes_hbm, bf16[256,256]{1,0:T(8,128)(2,1)} %constant.94.clone.modes_t_hbm, f32[8,128,128]{2,1,0:T(8,128)} %bitcast.31, bf16[2,8,128,128]{3,2,1,0:T(8,128)(2,1)} %copy-done, ...), custom_call_target="tpu_custom_call" | custom-call | tf_op jit(solution)/shard_map/pallas_call | solution.py:134
  105.4 6.4 %all-to-all-start.4 = ((f32[16,16,128]{2,1,0:T(8,128)}), f32[16,16,128]{2,1,0:T(8,128)S(1)}, u32[]{:S(2)}, u32[]{:S(2)}) async-start(f32[16,16,128]{2,1,0:T(8,128)} %shard_map.206), calls=%async_computation.4 | async-start | bytes 262144 | tf_op jit(solution)/shard_map/all_to_all | solution.py:548
  113.2 2.9 %shard_map.207.fixed = f32[8,128]{1,0:T(8,128)S(1)} custom-call(s32[2]{0:T(128)S(1)} %pad_add_fusion.where, bf16[16,128,256]{2,1,0:T(8,128)(2,1)S(1)} %constant_dynamic-update-slice_fusion.4.low, bf16[16,128,256]{2,1,0:T(8,128)(2,1)S(1)} %collective-permute-done.6.high, f32[128,256]{1,0:T(8,128)S(1)} %bitcast.21, f32[128,256]{1,0:T(8,128)S(1)} %bitcast.25, ...), custom_call_target="tpu_custom_call" | custom-call | tf_op jit(solution)/shard_map/pallas_call | solution.py:134
  116.2 7.7 %all-to-all-done.4.recv = f32[16,16,128]{2,1,0:T(8,128)S(1)} async-done(((f32[16,16,128]{2,1,0:T(8,128)}), f32[16,16,128]{2,1,0:T(8,128)S(1)}, u32[]{:S(2)}, u32[]{:S(2)}) %all-to-all-start.4) | async-done | bytes 131104 | tf_op jit(solution)/shard_map/all_to_all | solution.py:548
  123.8 2.8 %shard_map.208 = (f32[128,256]{1,0:T(8,128)S(1)}, f32[16,1,384]{2,1,0:T(1,128)S(1)}) custom-call(f32[16,16,128]{2,1,0:T(8,128)S(1)} %all-to-all-done.4.recv, bf16[2,256,256]{2,1,0:T(8,128)(2,1)S(1)} %copy-done.3, s32[2]{0:T(128)S(1)} %pad_add_fusion.where, f32[2]{0:T(128)S(1)} %pad_maximum_fusion.scalars, f32[128,256]{1,0:T(8,128)S(1)} %bitcast.22, ...), custom_call_target="tpu_custom_call" | custom-call | tf_op jit(solution)/shard_map/pallas_call | solution.py:134
  126.6 17.6 %all_to_all.35.recv = f32[16,1,384]{2,1,0:T(1,128)S(1)} all-to-all(f32[16,1,384]{2,1,0:T(1,128)S(1)} %get-tuple-element.29), channel_id=1, replica_groups=mesh['band'=32,'slab'=16] {'slab'}, dimensions={0} | all-to-all | bytes 49152 | tf_op jit(solution)/shard_map/all_to_all | solution.py:548
  144.2 1.0 shard_map.209
  145.2 5.9 %all-to-all-start.6 = ((f32[32,1,256]{2,1,0:T(1,128)}), f32[32,1,256]{2,1,0:T(1,128)S(1)}, u32[]{:S(2)}, u32[]{:S(2)}) async-start(f32[32,1,256]{2,1,0:T(1,128)} %get-tuple-element.30), calls=%async_computation.6 | async-start | bytes 65536 | tf_op jit(solution)/shard_map/all_to_all | solution.py:548
  151.8 2.2 %shard_map.210.rest = f32[128,256]{1,0:T(8,128)S(1)} custom-call(f32[1,128]{1,0:T(1,128)S(1)} %get-tuple-element.31.margin, s32[2]{0:T(128)S(1)} %pad_add_fusion.where, f32[2]{0:T(128)S(1)} %pad_maximum_fusion.scalars, f32[128,256]{1,0:T(8,128)S(1)} %bitcast.23, f32[128,256]{1,0:T(8,128)S(1)} %bitcast.27, f32[128,256]{1,0:T(8,128)S(1)} %get-tuple-element.32.applied, ...), custom_call_target="tpu_custom_call" | custom-call | tf_op jit(solution)/shard_map/pallas_call | solution.py:134
  154.0 4.3 %all-to-all-done.6.recv = f32[32,1,256]{2,1,0:T(1,128)S(1)} async-done(((f32[32,1,256]{2,1,0:T(1,128)}), f32[32,1,256]{2,1,0:T(1,128)S(1)}, u32[]{:S(2)}, u32[]{:S(2)}) %all-to-all-start.6) | async-done | bytes 32800 | tf_op jit(solution)/shard_map/all_to_all | solution.py:548
  158.3 1.3 shard_map.211
  (50 shorter events, 2.7 us)
Async XLA Ops:
  0.6 24.5 %copy-start.12 = (bf16[1,2,8,16384]{3,2,1,0:T(8,128)(2,1)S(1)}, bf16[1,2,8,16384]{3,2,1,0:T(8,128)(2,1)}, u32[]{:S(2)}) copy-start(bf16[1,2,8,16384]{3,2,1,0:T(8,128)(2,1)} %param.24) | copy-start | bytes 1572868
  2.8 15.9 %copy-start.14 = (s32[2048]{0:T(1024)S(1)}, s32[2048]{0:T(1024)}, u32[]{:S(2)}) copy-start(s32[2048]{0:T(1024)} %param.26) | copy-start | bytes 24580
  2.8 16.0 %copy-start.6 = (bf16[1,128,256]{2,1,0:T(8,128)(2,1)S(1)}, bf16[1,128,256]{2,1,0:T(8,128)(2,1)}, u32[]{:S(2)}) copy-start(bf16[1,128,256]{2,1,0:T(8,128)(2,1)} %param.23) | copy-start | bytes 196612
  2.8 27.9 %all-to-all-start = ((f32[16,16,128]{2,1,0:T(8,128)}), f32[16,16,128]{2,1,0:T(8,128)S(1)}, u32[]{:S(2)}, u32[]{:S(2)}) async-start(f32[16,16,128]{2,1,0:T(8,128)} %shard_map.202), calls=%async_computation | async-start | bytes 262144 | tf_op jit(solution)/shard_map/all_to_all | solution.py:548
  18.7 12.0 %copy-start.9 = (s32[2048]{0:T(1024)}, s32[2048]{0:T(1024)S(1)}, u32[]{:S(2)}) copy-start(s32[2048]{0:T(1024)S(1)} %fusion.4) | copy-start | bytes 24580
  18.8 6.5 %collective-permute-start.1 = (bf16[1,128,256]{2,1,0:T(8,128)(2,1)S(1)}, bf16[1,128,256]{2,1,0:T(8,128)(2,1)S(1)}, u32[]{:S(2)}, u32[]{:S(2)}) collective-permute-start(bf16[1,128,256]{2,1,0:T(8,128)(2,1)S(1)} %copy-done.6), channel_id=1, source_target_pairs={{0,96},{16,112},{32,64},{48,80},{64,32},{80,48},{96,0},{112,16},{1... | collective-permute-start | bytes 196616 | tf_op jit(solution)/shard_map/ppermute | solution.py:552
  23.2 5.3 %collective-permute-start = (bf16[1,128,256]{2,1,0:T(8,128)(2,1)S(1)}, bf16[1,128,256]{2,1,0:T(8,128)(2,1)S(1)}, u32[]{:S(2)}, u32[]{:S(2)}) collective-permute-start(bf16[1,128,256]{2,1,0:T(8,128)(2,1)S(1)} %copy-done.6), channel_id=1, source_target_pairs={{0,32},{16,48},{32,0},{48,16},{64,96},{80,112},{96,64},{112,80},{1... | collective-permute-start | bytes 196616 | tf_op jit(solution)/shard_map/ppermute | solution.py:552
  25.1 5.6 %copy-start.4 = (bf16[256,256]{1,0:T(8,128)(2,1)S(1)}, bf16[256,256]{1,0:T(8,128)(2,1)}, u32[]{:S(2)}) copy-start(bf16[256,256]{1,0:T(8,128)(2,1)} %constant.92.clone.refs_5_.modes) | copy-start | bytes 393220
  25.1 5.6 %copy-start.5 = (bf16[512,256]{1,0:T(8,128)(2,1)S(1)}, bf16[512,256]{1,0:T(8,128)(2,1)}, u32[]{:S(2)}) copy-start(bf16[512,256]{1,0:T(8,128)(2,1)} %constant.90.clone.refs_3_) | copy-start | bytes 786436
  25.1 5.6 %copy-start.7 = (bf16[256,256]{1,0:T(8,128)(2,1)S(1)}, bf16[256,256]{1,0:T(8,128)(2,1)}, u32[]{:S(2)}) copy-start(bf16[256,256]{1,0:T(8,128)(2,1)} %constant.95.clone.refs_6_) | copy-start | bytes 393220
  25.1 5.6 %copy-start.8 = (bf16[256,256]{1,0:T(8,128)(2,1)S(1)}, bf16[256,256]{1,0:T(8,128)(2,1)}, u32[]{:S(2)}) copy-start(bf16[256,256]{1,0:T(8,128)(2,1)} %constant.88.clone.refs_2_) | copy-start | bytes 393220
  25.2 10.3 %copy-start = (bf16[2,8,128,128]{3,2,1,0:T(8,128)(2,1)}, bf16[2,8,128,128]{3,2,1,0:T(8,128)(2,1)S(1)}, u32[]{:S(2)}) copy-start(bf16[2,8,128,128]{3,2,1,0:T(8,128)(2,1)S(1)} %copy.28) | copy-start | bytes 1572868
  35.6 22.3 %all-to-all-start.1 = ((f32[32,32,128]{2,1,0:T(8,128)}), f32[32,32,128]{2,1,0:T(8,128)S(1)}, u32[]{:S(2)}, u32[]{:S(2)}) async-start(f32[32,32,128]{2,1,0:T(8,128)} %bitcast.4), calls=%async_computation.1 | async-start | bytes 1048576 | tf_op jit(solution)/shard_map/all_to_all | solution.py:548
  46.3 10.8 %collective-permute-start.2 = (bf16[1,128,256]{2,1,0:T(8,128)(2,1)S(1)}, bf16[1,128,256]{2,1,0:T(8,128)(2,1)S(1)}, u32[]{:S(2)}, u32[]{:S(2)}) collective-permute-start(bf16[1,128,256]{2,1,0:T(8,128)(2,1)S(1)} %copy-done.6), channel_id=1, source_target_pairs={{0,64},{16,80},{32,96},{48,112},{64,0},{80,16},{96,32},{112,48},{1... | collective-permute-start | bytes 196616 | tf_op jit(solution)/shard_map/ppermute | solution.py:552
  58.6 18.2 %all-to-all-start.2 = ((s16[16,40,128]{2,1,0:T(8,128)(2,1)}), s16[16,40,128]{2,1,0:T(8,128)(2,1)S(1)}, u32[]{:S(2)}, u32[]{:S(2)}) async-start(s16[16,40,128]{2,1,0:T(8,128)(2,1)} %get-tuple-element.22), calls=%async_computation.2 | async-start | bytes 327680 | tf_op jit(solution)/shard_map/all_to_all | solution.py:548
  64.4 12.4 %copy-start.10 = (f32[128,128]{1,0:T(8,128)S(1)}, f32[128,128]{1,0:T(8,128)}, u32[]{:S(2)}) copy-start(f32[128,128]{1,0:T(8,128)} %constant.96.clone.modes_t32) | copy-start | bytes 196612
  64.4 22.6 %collective-permute-start.5 = (bf16[4,128,256]{2,1,0:T(8,128)(2,1)S(1)}, bf16[4,128,256]{2,1,0:T(8,128)(2,1)S(1)}, u32[]{:S(2)}, u32[]{:S(2)}) collective-permute-start(bf16[4,128,256]{2,1,0:T(8,128)(2,1)S(1)} %constant_dynamic-update-slice_fusion), channel_id=1, source_target_pairs={{0,384},{16,400},{32,416},{48,432},{64,448},{80,464},{96,480},{112... | collective-permute-start | bytes 786440 | tf_op jit(solution)/shard_map/ppermute | solution.py:552
  68.0 19.0 %collective-permute-start.4 = (bf16[4,128,256]{2,1,0:T(8,128)(2,1)S(1)}, bf16[4,128,256]{2,1,0:T(8,128)(2,1)S(1)}, u32[]{:S(2)}, u32[]{:S(2)}) collective-permute-start(bf16[4,128,256]{2,1,0:T(8,128)(2,1)S(1)} %constant_dynamic-update-slice_fusion), channel_id=1, source_target_pairs={{0,256},{16,272},{32,288},{48,304},{64,320},{80,336},{96,352},{112... | collective-permute-start | bytes 786440 | tf_op jit(solution)/shard_map/ppermute | solution.py:552
  70.4 16.6 %collective-permute-start.3 = (bf16[4,128,256]{2,1,0:T(8,128)(2,1)S(1)}, bf16[4,128,256]{2,1,0:T(8,128)(2,1)S(1)}, u32[]{:S(2)}, u32[]{:S(2)}) collective-permute-start(bf16[4,128,256]{2,1,0:T(8,128)(2,1)S(1)} %constant_dynamic-update-slice_fusion), channel_id=1, source_target_pairs={{0,128},{16,144},{32,160},{48,176},{64,192},{80,208},{96,224},{112... | collective-permute-start | bytes 786440 | tf_op jit(solution)/shard_map/ppermute | solution.py:552
  78.6 20.7 %all-to-all-start.3 = ((s16[32,72,128]{2,1,0:T(8,128)(2,1)}), s16[32,72,128]{2,1,0:T(8,128)(2,1)S(1)}, u32[]{:S(2)}, u32[]{:S(2)}) async-start(s16[32,72,128]{2,1,0:T(8,128)(2,1)} %shard_map.205), calls=%async_computation.3 | async-start | bytes 1179648 | tf_op jit(solution)/shard_map/all_to_all | solution.py:548
  87.1 2.4 %copy-start.13 = (f32[8,16384]{1,0:T(8,128)S(1)}, f32[8,16384]{1,0:T(8,128)}, u32[]{:S(2)}) copy-start(f32[8,16384]{1,0:T(8,128)} %param.25) | copy-start | bytes 1572868
  87.2 26.0 %collective-permute-start.6 = (bf16[16,128,256]{2,1,0:T(8,128)(2,1)S(1)}, bf16[16,128,256]{2,1,0:T(8,128)(2,1)S(1)}, u32[]{:S(2)}, u32[]{:S(2)}) collective-permute-start(bf16[16,128,256]{2,1,0:T(8,128)(2,1)S(1)} %constant_dynamic-update-slice_fusion.4.low), channel_id=1, source_target_pairs={{0,16},{16,0},{32,48},{48,32},{64,80},{80,64},{96,112},{112,96},{1... | collective-permute-start | bytes 3145736 | tf_op jit(solution)/shard_map/ppermute | solution.py:552
  99.3 0.8 copy-start.11
  105.3 7.9 %copy-start.1 = (f32[1,128,256]{2,1,0:T(8,128)S(1)}, f32[1,128,256]{2,1,0:T(8,128)}, u32[]{:S(2)}) copy-start(f32[1,128,256]{2,1,0:T(8,128)} %param.19) | copy-start | bytes 393220
  105.3 7.8 %copy-start.2 = (f32[1,128,256]{2,1,0:T(8,128)S(1)}, f32[1,128,256]{2,1,0:T(8,128)}, u32[]{:S(2)}) copy-start(f32[1,128,256]{2,1,0:T(8,128)} %param.20) | copy-start | bytes 393220
  105.4 18.5 %all-to-all-start.4 = ((f32[16,16,128]{2,1,0:T(8,128)}), f32[16,16,128]{2,1,0:T(8,128)S(1)}, u32[]{:S(2)}, u32[]{:S(2)}) async-start(f32[16,16,128]{2,1,0:T(8,128)} %shard_map.206), calls=%async_computation.4 | async-start | bytes 262144 | tf_op jit(solution)/shard_map/all_to_all | solution.py:548
  113.2 10.6 %copy-start.3 = (bf16[2,256,256]{2,1,0:T(8,128)(2,1)S(1)}, bf16[2,256,256]{2,1,0:T(8,128)(2,1)}, u32[]{:S(2)}) copy-start(bf16[2,256,256]{2,1,0:T(8,128)(2,1)} %constant.87.clone.table_hbm.table) | copy-start | bytes 786436
  145.2 13.1 %all-to-all-start.6 = ((f32[32,1,256]{2,1,0:T(1,128)}), f32[32,1,256]{2,1,0:T(1,128)S(1)}, u32[]{:S(2)}, u32[]{:S(2)}) async-start(f32[32,1,256]{2,1,0:T(1,128)} %get-tuple-element.30), calls=%async_computation.6 | async-start | bytes 65536 | tf_op jit(solution)/shard_map/all_to_all | solution.py:548

commit v7 on v6

--- a/solution.py
+++ b/solution.py
@@ -578,9 +578,9 @@
         shape(N * PL, N),
         field, cells, t["y_inverse"], t["x_inverse"], occ_planes, t["modes_left"], t["modes_t_right"],
         in_hbm=(2, 3, 4, 5, 6),
-        late=(x1, x3),
         scratch=[bf_scratch(2 * N, PL * N), bf_scratch(2 * N, PL * N)],
     )
+    (x1, x3), partial = after((x1, x3), partial)
     partial = swap(partial.reshape(BANDS, AX * PL, N), "band")
     x2 = across(own, 4)
     own_modes, total = call(

time: 161 us -> 159 us (0.988)
  starting transfers between devices: 75.4 us -> 73.7 us
    all_to_all x6, waiting for transfers between devices: 27.2 us -> 30.4 us  [swap(): return lax.all_to_all(value, axis, 0, 0, tiled=True)]
    ppermute x7, waiting for transfers between devices: 9.18 us -> 5.98 us  [across(): return lax.ppermute(blocks, 'band', [(i, i ^ bit) for i in range(BANDS)])]
    all_to_all x6, starting transfers between devices: 53.1 us -> 51.3 us  [swap(): return lax.all_to_all(value, axis, 0, 0, tiled=True)]
  transfers between devices with their start and end apart: 13 -> 13, of which waited for: 8 -> 7; matrix products, arithmetic and copies ran while one was open for 1% -> 1% of each run, Pallas kernels for 8% -> 11%
where the time goes in v7:
time: 159 us; the launch traced here: 158 us
  starting transfers between devices  73.7 us (46%)
  waiting for transfers between devices  36.4 us (23%)
  Pallas kernels  25 us (16%)
  blocking collectives  17.6 us (11%)
  local copies, waits for them, and re-layouts  2.65 us (2%)
  between operations  2.54 us (2%)
    all_to_all x6, starting transfers between devices, swap(): return lax.all_to_all(value, axis, 0, 0, tiled=True)  51.3 us
    all_to_all x6, waiting for transfers between devices, swap(): return lax.all_to_all(value, axis, 0, 0, tiled=True)  30.4 us
    pallas_call x10, Pallas kernels, call(): pl.pallas_call(inner, out_shape=out, in_specs=[*(pl.BlockSpec(memory_spac...  25 us
    ppermute x7, starting transfers between devices, across(): return lax.ppermute(blocks, 'band', [(i, i ^ bit) for i in range(BANDS)])  22.4 us
    all_to_all x1, blocking collectives, swap(): return lax.all_to_all(value, axis, 0, 0, tiled=True)  17.6 us
    ppermute x7, waiting for transfers between devices, across(): return lax.ppermute(blocks, 'band', [(i, i ^ bit) for i in range(BANDS)])  5.98 us
  transfers between devices with their start and end apart: 13, of which 7 were waited for; matrix products, arithmetic and copies ran while one was open for 1% of the time, Pallas kernels for 11%

profile of v7, /device:TPU:1, one launch (start us, length us, event | category | flops | bytes accessed | tf_op | source)
XLA Modules:
  0.0 158.0 jit_solution(5192021373020486450)
XLA Ops:
  0.6 2.1 %shard_map.202 = f32[16,16,128]{2,1,0:T(8,128)} custom-call(f32[128,256]{1,0:T(8,128)} %bitcast.20, bf16[2,256,256]{2,1,0:T(8,128)(2,1)} %constant.87.clone.table_hbm.table), custom_call_target="tpu_custom_call" | custom-call | tf_op jit(solution)/shard_map/pallas_call | solution.py:134
  2.8 15.9 %all-to-all-start = ((f32[16,16,128]{2,1,0:T(8,128)}), f32[16,16,128]{2,1,0:T(8,128)S(1)}, u32[]{:S(2)}, u32[]{:S(2)}) async-start(f32[16,16,128]{2,1,0:T(8,128)} %shard_map.202), calls=%async_computation | async-start | bytes 262144 | tf_op jit(solution)/shard_map/all_to_all | solution.py:548
  18.8 4.4 %collective-permute-start.1 = (bf16[1,128,256]{2,1,0:T(8,128)(2,1)S(1)}, bf16[1,128,256]{2,1,0:T(8,128)(2,1)S(1)}, u32[]{:S(2)}, u32[]{:S(2)}) collective-permute-start(bf16[1,128,256]{2,1,0:T(8,128)(2,1)S(1)} %copy-done.6), channel_id=1, source_target_pairs={{0,96},{16,112},{32,64},{48,80},{64,32},{80,48},{96,0},{112,16},{1... | collective-permute-start | bytes 196616 | tf_op jit(solution)/shard_map/ppermute | solution.py:552
  23.2 1.9 %collective-permute-start = (bf16[1,128,256]{2,1,0:T(8,128)(2,1)S(1)}, bf16[1,128,256]{2,1,0:T(8,128)(2,1)S(1)}, u32[]{:S(2)}, u32[]{:S(2)}) collective-permute-start(bf16[1,128,256]{2,1,0:T(8,128)(2,1)S(1)} %copy-done.6), channel_id=1, source_target_pairs={{0,32},{16,48},{32,0},{48,16},{64,96},{80,112},{96,64},{112,80},{1... | collective-permute-start | bytes 196616 | tf_op jit(solution)/shard_map/ppermute | solution.py:552
  25.3 5.4 %all-to-all-done.recv = f32[16,16,128]{2,1,0:T(8,128)S(1)} async-done(((f32[16,16,128]{2,1,0:T(8,128)}), f32[16,16,128]{2,1,0:T(8,128)S(1)}, u32[]{:S(2)}, u32[]{:S(2)}) %all-to-all-start) | async-done | bytes 131104 | tf_op jit(solution)/shard_map/all_to_all | solution.py:548
  30.7 4.8 %shard_map.203 = f32[1024,128]{1,0:T(8,128)} custom-call(f32[16,16,128]{2,1,0:T(8,128)S(1)} %all-to-all-done.recv, s32[1,2048]{1,0:T(1,128)S(1)} %bitcast.29, bf16[256,256]{1,0:T(8,128)(2,1)S(1)} %copy-done.8, bf16[512,256]{1,0:T(8,128)(2,1)S(1)} %copy-done.5, bf16[2,8,128,128]{3,2,1,0:T(8,128)(2,1)S(1)} %copy.28, bf16[256,256]{1,0:T(8,128)(2,1)S(1)} %copy-done.4, ...), custom_call_target="tpu_custom_call" | custom-call | tf_op jit(solution)/shard_map/pallas_call | solution.py:134
  35.6 10.7 %all-to-all-start.1 = ((f32[32,32,128]{2,1,0:T(8,128)}), f32[32,32,128]{2,1,0:T(8,128)S(1)}, u32[]{:S(2)}, u32[]{:S(2)}) async-start(f32[32,32,128]{2,1,0:T(8,128)} %bitcast.4), calls=%async_computation.1 | async-start | bytes 1048576 | tf_op jit(solution)/shard_map/all_to_all | solution.py:548
  46.3 4.8 %collective-permute-start.2 = (bf16[1,128,256]{2,1,0:T(8,128)(2,1)S(1)}, bf16[1,128,256]{2,1,0:T(8,128)(2,1)S(1)}, u32[]{:S(2)}, u32[]{:S(2)}) collective-permute-start(bf16[1,128,256]{2,1,0:T(8,128)(2,1)S(1)} %copy-done.6), channel_id=1, source_target_pairs={{0,64},{16,80},{32,96},{48,112},{64,0},{80,16},{96,32},{112,48},{1... | collective-permute-start | bytes 196616 | tf_op jit(solution)/shard_map/ppermute | solution.py:552
  51.1 6.0 %collective-permute-done.2.refs_1_ = bf16[1,128,256]{2,1,0:T(8,128)(2,1)S(1)} collective-permute-done((bf16[1,128,256]{2,1,0:T(8,128)(2,1)S(1)}, bf16[1,128,256]{2,1,0:T(8,128)(2,1)S(1)}, u32[]{:S(2)}, u32[]{:S(2)}) %collective-permute-start.2) | collective-permute-done | bytes 65568 | tf_op jit(solution)/shard_map/ppermute | solution.py:552
  57.1 0.8 all-to-all-done.1.refs_0_
  58.6 4.0 %all-to-all-start.2 = ((s16[16,40,128]{2,1,0:T(8,128)(2,1)}), s16[16,40,128]{2,1,0:T(8,128)(2,1)S(1)}, u32[]{:S(2)}, u32[]{:S(2)}) async-start(s16[16,40,128]{2,1,0:T(8,128)(2,1)} %get-tuple-element.26), calls=%async_computation.2 | async-start | bytes 327680 | tf_op jit(solution)/shard_map/all_to_all | solution.py:548
  62.7 3.6 %collective-permute-start.5 = (bf16[4,128,256]{2,1,0:T(8,128)(2,1)S(1)}, bf16[4,128,256]{2,1,0:T(8,128)(2,1)S(1)}, u32[]{:S(2)}, u32[]{:S(2)}) collective-permute-start(bf16[4,128,256]{2,1,0:T(8,128)(2,1)S(1)} %constant_dynamic-update-slice_fusion), channel_id=1, source_target_pairs={{0,384},{16,400},{32,416},{48,432},{64,448},{80,464},{96,480},{112... | collective-permute-start | bytes 786440 | tf_op jit(solution)/shard_map/ppermute | solution.py:552
  66.3 2.4 %collective-permute-start.4 = (bf16[4,128,256]{2,1,0:T(8,128)(2,1)S(1)}, bf16[4,128,256]{2,1,0:T(8,128)(2,1)S(1)}, u32[]{:S(2)}, u32[]{:S(2)}) collective-permute-start(bf16[4,128,256]{2,1,0:T(8,128)(2,1)S(1)} %constant_dynamic-update-slice_fusion), channel_id=1, source_target_pairs={{0,256},{16,272},{32,288},{48,304},{64,320},{80,336},{96,352},{112... | collective-permute-start | bytes 786440 | tf_op jit(solution)/shard_map/ppermute | solution.py:552
  68.7 3.0 %collective-permute-start.3 = (bf16[4,128,256]{2,1,0:T(8,128)(2,1)S(1)}, bf16[4,128,256]{2,1,0:T(8,128)(2,1)S(1)}, u32[]{:S(2)}, u32[]{:S(2)}) collective-permute-start(bf16[4,128,256]{2,1,0:T(8,128)(2,1)S(1)} %constant_dynamic-update-slice_fusion), channel_id=1, source_target_pairs={{0,128},{16,144},{32,160},{48,176},{64,192},{80,208},{96,224},{112... | collective-permute-start | bytes 786440 | tf_op jit(solution)/shard_map/ppermute | solution.py:552
  71.7 3.3 %all-to-all-done.2.recv = s16[16,40,128]{2,1,0:T(8,128)(2,1)S(1)} async-done(((s16[16,40,128]{2,1,0:T(8,128)(2,1)}), s16[16,40,128]{2,1,0:T(8,128)(2,1)S(1)}, u32[]{:S(2)}, u32[]{:S(2)}) %all-to-all-start.2) | async-done | bytes 163872 | tf_op jit(solution)/shard_map/all_to_all | solution.py:548
  75.0 1.8 %shard_map.205 = s16[32,72,128]{2,1,0:T(8,128)(2,1)} custom-call(s32[2]{0:T(128)S(1)} %pad_add_fusion.where, s16[16,40,128]{2,1,0:T(8,128)(2,1)S(1)} %all-to-all-done.2.recv, f32[32,128]{1,0:T(8,128)S(1)} %get-tuple-element.27.density, bf16[256,256]{1,0:T(8,128)(2,1)S(1)} %copy-done.4, f32[128,128]{1,0:T(8,128)S(1)} %copy-done.10), custom_call_target="tpu_custom_call" | custom-call | tf_op jit(solution)/shard_map/pallas_call | solution.py:134
  76.9 8.4 %all-to-all-start.3 = ((s16[32,72,128]{2,1,0:T(8,128)(2,1)}), s16[32,72,128]{2,1,0:T(8,128)(2,1)S(1)}, u32[]{:S(2)}, u32[]{:S(2)}) async-start(s16[32,72,128]{2,1,0:T(8,128)(2,1)} %shard_map.205), calls=%async_computation.3 | async-start | bytes 1179648 | tf_op jit(solution)/shard_map/all_to_all | solution.py:548
  85.4 2.3 %collective-permute-start.6 = (bf16[16,128,256]{2,1,0:T(8,128)(2,1)S(1)}, bf16[16,128,256]{2,1,0:T(8,128)(2,1)S(1)}, u32[]{:S(2)}, u32[]{:S(2)}) collective-permute-start(bf16[16,128,256]{2,1,0:T(8,128)(2,1)S(1)} %constant_dynamic-update-slice_fusion.4.low), channel_id=1, source_target_pairs={{0,16},{16,0},{32,48},{48,32},{64,80},{80,64},{96,112},{112,96},{1... | collective-permute-start | bytes 3145736 | tf_op jit(solution)/shard_map/ppermute | solution.py:552
  87.7 0.9 copy.27
  88.6 8.9 %all-to-all-done.3.recv = s16[32,72,128]{2,1,0:T(8,128)(2,1)S(1)} async-done(((s16[32,72,128]{2,1,0:T(8,128)(2,1)}), s16[32,72,128]{2,1,0:T(8,128)(2,1)S(1)}, u32[]{:S(2)}, u32[]{:S(2)}) %all-to-all-start.3) | async-done | bytes 589856 | tf_op jit(solution)/shard_map/all_to_all | solution.py:548
  97.5 0.8 copy-done.11
  98.3 5.3 %shard_map.206 = f32[16,16,128]{2,1,0:T(8,128)} custom-call(s16[32,72,128]{2,1,0:T(8,128)(2,1)} %copy-done.11, s32[1,2048]{1,0:T(1,128)} %bitcast.30, bf16[256,256]{1,0:T(8,128)(2,1)} %constant.93.clone.modes_hbm, bf16[256,256]{1,0:T(8,128)(2,1)} %constant.94.clone.modes_t_hbm, f32[8,128,128]{2,1,0:T(8,128)} %bitcast.31, bf16[2,8,128,128]{3,2,1,0:T(8,128)(2,1)} %copy-done, ...), custom_call_target="tpu_custom_call" | custom-call | tf_op jit(solution)/shard_map/pallas_call | solution.py:134
  103.6 6.4 %all-to-all-start.4 = ((f32[16,16,128]{2,1,0:T(8,128)}), f32[16,16,128]{2,1,0:T(8,128)S(1)}, u32[]{:S(2)}, u32[]{:S(2)}) async-start(f32[16,16,128]{2,1,0:T(8,128)} %shard_map.206), calls=%async_computation.4 | async-start | bytes 262144 | tf_op jit(solution)/shard_map/all_to_all | solution.py:548
  111.5 2.9 %shard_map.207.fixed = f32[8,128]{1,0:T(8,128)S(1)} custom-call(s32[2]{0:T(128)S(1)} %pad_add_fusion.where, bf16[16,128,256]{2,1,0:T(8,128)(2,1)S(1)} %constant_dynamic-update-slice_fusion.4.low, bf16[16,128,256]{2,1,0:T(8,128)(2,1)S(1)} %collective-permute-done.6.high, f32[128,256]{1,0:T(8,128)S(1)} %bitcast.21, f32[128,256]{1,0:T(8,128)S(1)} %bitcast.25, ...), custom_call_target="tpu_custom_call" | custom-call | tf_op jit(solution)/shard_map/pallas_call | solution.py:134
  114.4 7.7 %all-to-all-done.4.recv = f32[16,16,128]{2,1,0:T(8,128)S(1)} async-done(((f32[16,16,128]{2,1,0:T(8,128)}), f32[16,16,128]{2,1,0:T(8,128)S(1)}, u32[]{:S(2)}, u32[]{:S(2)}) %all-to-all-start.4) | async-done | bytes 131104 | tf_op jit(solution)/shard_map/all_to_all | solution.py:548
  122.1 2.8 %shard_map.208 = (f32[128,256]{1,0:T(8,128)S(1)}, f32[16,1,384]{2,1,0:T(1,128)S(1)}) custom-call(f32[16,16,128]{2,1,0:T(8,128)S(1)} %all-to-all-done.4.recv, bf16[2,256,256]{2,1,0:T(8,128)(2,1)S(1)} %copy-done.3, s32[2]{0:T(128)S(1)} %pad_add_fusion.where, f32[2]{0:T(128)S(1)} %pad_maximum_fusion.scalars, f32[128,256]{1,0:T(8,128)S(1)} %bitcast.22, ...), custom_call_target="tpu_custom_call" | custom-call | tf_op jit(solution)/shard_map/pallas_call | solution.py:134
  124.9 17.6 %all_to_all.35.recv = f32[16,1,384]{2,1,0:T(1,128)S(1)} all-to-all(f32[16,1,384]{2,1,0:T(1,128)S(1)} %get-tuple-element.35), channel_id=1, replica_groups=mesh['band'=32,'slab'=16] {'slab'}, dimensions={0} | all-to-all | bytes 49152 | tf_op jit(solution)/shard_map/all_to_all | solution.py:548
  142.5 1.0 shard_map.209
  143.5 5.9 %all-to-all-start.6 = ((f32[32,1,256]{2,1,0:T(1,128)}), f32[32,1,256]{2,1,0:T(1,128)S(1)}, u32[]{:S(2)}, u32[]{:S(2)}) async-start(f32[32,1,256]{2,1,0:T(1,128)} %get-tuple-element.36), calls=%async_computation.6 | async-start | bytes 65536 | tf_op jit(solution)/shard_map/all_to_all | solution.py:548
  150.0 2.2 %shard_map.210.rest = f32[128,256]{1,0:T(8,128)S(1)} custom-call(f32[1,128]{1,0:T(1,128)S(1)} %get-tuple-element.37.margin, s32[2]{0:T(128)S(1)} %pad_add_fusion.where, f32[2]{0:T(128)S(1)} %pad_maximum_fusion.scalars, f32[128,256]{1,0:T(8,128)S(1)} %bitcast.23, f32[128,256]{1,0:T(8,128)S(1)} %bitcast.27, f32[128,256]{1,0:T(8,128)S(1)} %get-tuple-element.38.applied, ...), custom_call_target="tpu_custom_call" | custom-call | tf_op jit(solution)/shard_map/pallas_call | solution.py:134
  152.3 4.3 %all-to-all-done.6.recv = f32[32,1,256]{2,1,0:T(1,128)S(1)} async-done(((f32[32,1,256]{2,1,0:T(1,128)}), f32[32,1,256]{2,1,0:T(1,128)S(1)}, u32[]{:S(2)}, u32[]{:S(2)}) %all-to-all-start.6) | async-done | bytes 32800 | tf_op jit(solution)/shard_map/all_to_all | solution.py:548
  156.6 1.3 shard_map.211
  (50 shorter events, 1.9 us)
Async XLA Ops:
  0.6 24.5 %copy-start.12 = (bf16[1,2,8,16384]{3,2,1,0:T(8,128)(2,1)S(1)}, bf16[1,2,8,16384]{3,2,1,0:T(8,128)(2,1)}, u32[]{:S(2)}) copy-start(bf16[1,2,8,16384]{3,2,1,0:T(8,128)(2,1)} %param.24) | copy-start | bytes 1572868
  2.8 15.9 %copy-start.14 = (s32[2048]{0:T(1024)S(1)}, s32[2048]{0:T(1024)}, u32[]{:S(2)}) copy-start(s32[2048]{0:T(1024)} %param.26) | copy-start | bytes 24580
  2.8 16.0 %copy-start.6 = (bf16[1,128,256]{2,1,0:T(8,128)(2,1)S(1)}, bf16[1,128,256]{2,1,0:T(8,128)(2,1)}, u32[]{:S(2)}) copy-start(bf16[1,128,256]{2,1,0:T(8,128)(2,1)} %param.23) | copy-start | bytes 196612
  2.8 27.9 %all-to-all-start = ((f32[16,16,128]{2,1,0:T(8,128)}), f32[16,16,128]{2,1,0:T(8,128)S(1)}, u32[]{:S(2)}, u32[]{:S(2)}) async-start(f32[16,16,128]{2,1,0:T(8,128)} %shard_map.202), calls=%async_computation | async-start | bytes 262144 | tf_op jit(solution)/shard_map/all_to_all | solution.py:548
  18.7 12.0 %copy-start.9 = (s32[2048]{0:T(1024)}, s32[2048]{0:T(1024)S(1)}, u32[]{:S(2)}) copy-start(s32[2048]{0:T(1024)S(1)} %fusion.4) | copy-start | bytes 24580
  18.8 16.8 %collective-permute-start.1 = (bf16[1,128,256]{2,1,0:T(8,128)(2,1)S(1)}, bf16[1,128,256]{2,1,0:T(8,128)(2,1)S(1)}, u32[]{:S(2)}, u32[]{:S(2)}) collective-permute-start(bf16[1,128,256]{2,1,0:T(8,128)(2,1)S(1)} %copy-done.6), channel_id=1, source_target_pairs={{0,96},{16,112},{32,64},{48,80},{64,32},{80,48},{96,0},{112,16},{1... | collective-permute-start | bytes 196616 | tf_op jit(solution)/shard_map/ppermute | solution.py:552
  23.2 12.4 %collective-permute-start = (bf16[1,128,256]{2,1,0:T(8,128)(2,1)S(1)}, bf16[1,128,256]{2,1,0:T(8,128)(2,1)S(1)}, u32[]{:S(2)}, u32[]{:S(2)}) collective-permute-start(bf16[1,128,256]{2,1,0:T(8,128)(2,1)S(1)} %copy-done.6), channel_id=1, source_target_pairs={{0,32},{16,48},{32,0},{48,16},{64,96},{80,112},{96,64},{112,80},{1... | collective-permute-start | bytes 196616 | tf_op jit(solution)/shard_map/ppermute | solution.py:552
  25.1 5.6 %copy-start.4 = (bf16[256,256]{1,0:T(8,128)(2,1)S(1)}, bf16[256,256]{1,0:T(8,128)(2,1)}, u32[]{:S(2)}) copy-start(bf16[256,256]{1,0:T(8,128)(2,1)} %constant.92.clone.modes_hbm.modes) | copy-start | bytes 393220
  25.1 5.6 %copy-start.5 = (bf16[512,256]{1,0:T(8,128)(2,1)S(1)}, bf16[512,256]{1,0:T(8,128)(2,1)}, u32[]{:S(2)}) copy-start(bf16[512,256]{1,0:T(8,128)(2,1)} %constant.90.clone.x_hbm) | copy-start | bytes 786436
  25.1 5.6 %copy-start.7 = (bf16[256,256]{1,0:T(8,128)(2,1)S(1)}, bf16[256,256]{1,0:T(8,128)(2,1)}, u32[]{:S(2)}) copy-start(bf16[256,256]{1,0:T(8,128)(2,1)} %constant.95.clone.modes_t_hbm) | copy-start | bytes 393220
  25.1 5.6 %copy-start.8 = (bf16[256,256]{1,0:T(8,128)(2,1)S(1)}, bf16[256,256]{1,0:T(8,128)(2,1)}, u32[]{:S(2)}) copy-start(bf16[256,256]{1,0:T(8,128)(2,1)} %constant.88.clone.y_hbm) | copy-start | bytes 393220
  25.2 10.3 %copy-start = (bf16[2,8,128,128]{3,2,1,0:T(8,128)(2,1)}, bf16[2,8,128,128]{3,2,1,0:T(8,128)(2,1)S(1)}, u32[]{:S(2)}) copy-start(bf16[2,8,128,128]{3,2,1,0:T(8,128)(2,1)S(1)} %copy.28) | copy-start | bytes 1572868
  35.6 22.3 %all-to-all-start.1 = ((f32[32,32,128]{2,1,0:T(8,128)}), f32[32,32,128]{2,1,0:T(8,128)S(1)}, u32[]{:S(2)}, u32[]{:S(2)}) async-start(f32[32,32,128]{2,1,0:T(8,128)} %bitcast.4), calls=%async_computation.1 | async-start | bytes 1048576 | tf_op jit(solution)/shard_map/all_to_all | solution.py:548
  46.3 10.8 %collective-permute-start.2 = (bf16[1,128,256]{2,1,0:T(8,128)(2,1)S(1)}, bf16[1,128,256]{2,1,0:T(8,128)(2,1)S(1)}, u32[]{:S(2)}, u32[]{:S(2)}) collective-permute-start(bf16[1,128,256]{2,1,0:T(8,128)(2,1)S(1)} %copy-done.6), channel_id=1, source_target_pairs={{0,64},{16,80},{32,96},{48,112},{64,0},{80,16},{96,32},{112,48},{1... | collective-permute-start | bytes 196616 | tf_op jit(solution)/shard_map/ppermute | solution.py:552
  58.6 16.4 %all-to-all-start.2 = ((s16[16,40,128]{2,1,0:T(8,128)(2,1)}), s16[16,40,128]{2,1,0:T(8,128)(2,1)S(1)}, u32[]{:S(2)}, u32[]{:S(2)}) async-start(s16[16,40,128]{2,1,0:T(8,128)(2,1)} %get-tuple-element.26), calls=%async_computation.2 | async-start | bytes 327680 | tf_op jit(solution)/shard_map/all_to_all | solution.py:548
  62.6 12.4 %copy-start.10 = (f32[128,128]{1,0:T(8,128)S(1)}, f32[128,128]{1,0:T(8,128)}, u32[]{:S(2)}) copy-start(f32[128,128]{1,0:T(8,128)} %constant.96.clone.modes_t32) | copy-start | bytes 196612
  62.7 22.6 %collective-permute-start.5 = (bf16[4,128,256]{2,1,0:T(8,128)(2,1)S(1)}, bf16[4,128,256]{2,1,0:T(8,128)(2,1)S(1)}, u32[]{:S(2)}, u32[]{:S(2)}) collective-permute-start(bf16[4,128,256]{2,1,0:T(8,128)(2,1)S(1)} %constant_dynamic-update-slice_fusion), channel_id=1, source_target_pairs={{0,384},{16,400},{32,416},{48,432},{64,448},{80,464},{96,480},{112... | collective-permute-start | bytes 786440 | tf_op jit(solution)/shard_map/ppermute | solution.py:552
  66.3 19.0 %collective-permute-start.4 = (bf16[4,128,256]{2,1,0:T(8,128)(2,1)S(1)}, bf16[4,128,256]{2,1,0:T(8,128)(2,1)S(1)}, u32[]{:S(2)}, u32[]{:S(2)}) collective-permute-start(bf16[4,128,256]{2,1,0:T(8,128)(2,1)S(1)} %constant_dynamic-update-slice_fusion), channel_id=1, source_target_pairs={{0,256},{16,272},{32,288},{48,304},{64,320},{80,336},{96,352},{112... | collective-permute-start | bytes 786440 | tf_op jit(solution)/shard_map/ppermute | solution.py:552
  68.7 16.6 %collective-permute-start.3 = (bf16[4,128,256]{2,1,0:T(8,128)(2,1)S(1)}, bf16[4,128,256]{2,1,0:T(8,128)(2,1)S(1)}, u32[]{:S(2)}, u32[]{:S(2)}) collective-permute-start(bf16[4,128,256]{2,1,0:T(8,128)(2,1)S(1)} %constant_dynamic-update-slice_fusion), channel_id=1, source_target_pairs={{0,128},{16,144},{32,160},{48,176},{64,192},{80,208},{96,224},{112... | collective-permute-start | bytes 786440 | tf_op jit(solution)/shard_map/ppermute | solution.py:552
  76.9 20.7 %all-to-all-start.3 = ((s16[32,72,128]{2,1,0:T(8,128)(2,1)}), s16[32,72,128]{2,1,0:T(8,128)(2,1)S(1)}, u32[]{:S(2)}, u32[]{:S(2)}) async-start(s16[32,72,128]{2,1,0:T(8,128)(2,1)} %shard_map.205), calls=%async_computation.3 | async-start | bytes 1179648 | tf_op jit(solution)/shard_map/all_to_all | solution.py:548
  85.4 2.4 %copy-start.13 = (f32[8,16384]{1,0:T(8,128)S(1)}, f32[8,16384]{1,0:T(8,128)}, u32[]{:S(2)}) copy-start(f32[8,16384]{1,0:T(8,128)} %param.25) | copy-start | bytes 1572868
  85.4 26.0 %collective-permute-start.6 = (bf16[16,128,256]{2,1,0:T(8,128)(2,1)S(1)}, bf16[16,128,256]{2,1,0:T(8,128)(2,1)S(1)}, u32[]{:S(2)}, u32[]{:S(2)}) collective-permute-start(bf16[16,128,256]{2,1,0:T(8,128)(2,1)S(1)} %constant_dynamic-update-slice_fusion.4.low), channel_id=1, source_target_pairs={{0,16},{16,0},{32,48},{48,32},{64,80},{80,64},{96,112},{112,96},{1... | collective-permute-start | bytes 3145736 | tf_op jit(solution)/shard_map/ppermute | solution.py:552
  97.5 0.8 copy-start.11
  103.6 7.9 %copy-start.1 = (f32[1,128,256]{2,1,0:T(8,128)S(1)}, f32[1,128,256]{2,1,0:T(8,128)}, u32[]{:S(2)}) copy-start(f32[1,128,256]{2,1,0:T(8,128)} %param.19) | copy-start | bytes 393220
  103.6 7.8 %copy-start.2 = (f32[1,128,256]{2,1,0:T(8,128)S(1)}, f32[1,128,256]{2,1,0:T(8,128)}, u32[]{:S(2)}) copy-start(f32[1,128,256]{2,1,0:T(8,128)} %param.20) | copy-start | bytes 393220
  103.6 18.5 %all-to-all-start.4 = ((f32[16,16,128]{2,1,0:T(8,128)}), f32[16,16,128]{2,1,0:T(8,128)S(1)}, u32[]{:S(2)}, u32[]{:S(2)}) async-start(f32[16,16,128]{2,1,0:T(8,128)} %shard_map.206), calls=%async_computation.4 | async-start | bytes 262144 | tf_op jit(solution)/shard_map/all_to_all | solution.py:548
  111.5 10.6 %copy-start.3 = (bf16[2,256,256]{2,1,0:T(8,128)(2,1)S(1)}, bf16[2,256,256]{2,1,0:T(8,128)(2,1)}, u32[]{:S(2)}) copy-start(bf16[2,256,256]{2,1,0:T(8,128)(2,1)} %constant.87.clone.table_hbm.table) | copy-start | bytes 786436
  143.5 13.1 %all-to-all-start.6 = ((f32[32,1,256]{2,1,0:T(1,128)}), f32[32,1,256]{2,1,0:T(1,128)S(1)}, u32[]{:S(2)}, u32[]{:S(2)}) async-start(f32[32,1,256]{2,1,0:T(1,128)} %get-tuple-element.36), calls=%async_computation.6 | async-start | bytes 65536 | tf_op jit(solution)/shard_map/all_to_all | solution.py:548

commit v8 on v7

--- a/solution.py
+++ b/solution.py
@@ -587,8 +587,8 @@
         sum_bands,
         [shape(AX * PL, N), shape(SLABS, AX * PL + 8, N, dtype=jnp.int16)],
         partial,
-        late=(x2,),
-    )
+    )
+    x2, total = after(x2, total)
     row = jnp.concatenate([own, x1, x2, x3], axis=0)
     y1, y2, y3 = across(row, 8), across(row, 16), across(row, 24)
     columns = swap(total, "slab")

time: 159 us -> 158 us (level)
    ppermute x7, waiting for transfers between devices: 5.98 us -> 0.02 us  [across(): return lax.ppermute(blocks, 'band', [(i, i ^ bit) for i in range(BANDS)])]
    all_to_all x6, waiting for transfers between devices: 30.4 us -> 36.4 us  [swap(): return lax.all_to_all(value, axis, 0, 0, tiled=True)]
  transfers between devices with their start and end apart: 13 -> 13, of which waited for: 7 -> 6; matrix products, arithmetic and copies ran while one was open for 1% -> 1% of each run, Pallas kernels for 11% -> 11%
where the time goes in v8:
time: 158 us; the launch traced here: 157 us
  starting transfers between devices  72.9 us (46%)
  waiting for transfers between devices  36.4 us (23%)
  Pallas kernels  25 us (16%)
  blocking collectives  17.6 us (11%)
  local copies, waits for them, and re-layouts  2.65 us (2%)
  between operations  2.54 us (2%)
    all_to_all x6, starting transfers between devices, swap(): return lax.all_to_all(value, axis, 0, 0, tiled=True)  50.5 us
    all_to_all x6, waiting for transfers between devices, swap(): return lax.all_to_all(value, axis, 0, 0, tiled=True)  36.4 us
    pallas_call x10, Pallas kernels, call(): pl.pallas_call(inner, out_shape=out, in_specs=[*(pl.BlockSpec(memory_spac...  25 us
    ppermute x7, starting transfers between devices, across(): return lax.ppermute(blocks, 'band', [(i, i ^ bit) for i in range(BANDS)])  22.4 us
    all_to_all x1, blocking collectives, swap(): return lax.all_to_all(value, axis, 0, 0, tiled=True)  17.6 us
  transfers between devices with their start and end apart: 13, of which 6 were waited for; matrix products, arithmetic and copies ran while one was open for 1% of the time, Pallas kernels for 11%

profile of v8, /device:TPU:1, one launch (start us, length us, event | category | flops | bytes accessed | tf_op | source)
XLA Modules:
  0.0 157.3 jit_solution(6164546817864581913)
XLA Ops:
  0.6 2.1 %shard_map.202 = f32[16,16,128]{2,1,0:T(8,128)} custom-call(f32[128,256]{1,0:T(8,128)} %bitcast.20, bf16[2,256,256]{2,1,0:T(8,128)(2,1)} %constant.87.clone.table_hbm.table), custom_call_target="tpu_custom_call" | custom-call | tf_op jit(solution)/shard_map/pallas_call | solution.py:134
  2.8 15.9 %all-to-all-start = ((f32[16,16,128]{2,1,0:T(8,128)}), f32[16,16,128]{2,1,0:T(8,128)S(1)}, u32[]{:S(2)}, u32[]{:S(2)}) async-start(f32[16,16,128]{2,1,0:T(8,128)} %shard_map.202), calls=%async_computation | async-start | bytes 262144 | tf_op jit(solution)/shard_map/all_to_all | solution.py:548
  18.8 4.4 %collective-permute-start.2 = (bf16[1,128,256]{2,1,0:T(8,128)(2,1)S(1)}, bf16[1,128,256]{2,1,0:T(8,128)(2,1)S(1)}, u32[]{:S(2)}, u32[]{:S(2)}) collective-permute-start(bf16[1,128,256]{2,1,0:T(8,128)(2,1)S(1)} %copy-done.6), channel_id=1, source_target_pairs={{0,96},{16,112},{32,64},{48,80},{64,32},{80,48},{96,0},{112,16},{1... | collective-permute-start | bytes 196616 | tf_op jit(solution)/shard_map/ppermute | solution.py:552
  23.2 1.9 %collective-permute-start.1 = (bf16[1,128,256]{2,1,0:T(8,128)(2,1)S(1)}, bf16[1,128,256]{2,1,0:T(8,128)(2,1)S(1)}, u32[]{:S(2)}, u32[]{:S(2)}) collective-permute-start(bf16[1,128,256]{2,1,0:T(8,128)(2,1)S(1)} %copy-done.6), channel_id=1, source_target_pairs={{0,32},{16,48},{32,0},{48,16},{64,96},{80,112},{96,64},{112,80},{1... | collective-permute-start | bytes 196616 | tf_op jit(solution)/shard_map/ppermute | solution.py:552
  25.3 5.4 %all-to-all-done.recv = f32[16,16,128]{2,1,0:T(8,128)S(1)} async-done(((f32[16,16,128]{2,1,0:T(8,128)}), f32[16,16,128]{2,1,0:T(8,128)S(1)}, u32[]{:S(2)}, u32[]{:S(2)}) %all-to-all-start) | async-done | bytes 131104 | tf_op jit(solution)/shard_map/all_to_all | solution.py:548
  30.7 4.8 %shard_map.203 = f32[1024,128]{1,0:T(8,128)} custom-call(f32[16,16,128]{2,1,0:T(8,128)S(1)} %all-to-all-done.recv, s32[1,2048]{1,0:T(1,128)S(1)} %bitcast.29, bf16[256,256]{1,0:T(8,128)(2,1)S(1)} %copy-done.8, bf16[512,256]{1,0:T(8,128)(2,1)S(1)} %copy-done.5, bf16[2,8,128,128]{3,2,1,0:T(8,128)(2,1)S(1)} %copy.28, bf16[256,256]{1,0:T(8,128)(2,1)S(1)} %copy-done.4, ...), custom_call_target="tpu_custom_call" | custom-call | tf_op jit(solution)/shard_map/pallas_call | solution.py:134
  35.6 10.7 %all-to-all-start.1 = ((f32[32,32,128]{2,1,0:T(8,128)}), f32[32,32,128]{2,1,0:T(8,128)S(1)}, u32[]{:S(2)}, u32[]{:S(2)}) async-start(f32[32,32,128]{2,1,0:T(8,128)} %bitcast.4), calls=%async_computation.1 | async-start | bytes 1048576 | tf_op jit(solution)/shard_map/all_to_all | solution.py:548
  46.3 4.8 %collective-permute-start = (bf16[1,128,256]{2,1,0:T(8,128)(2,1)S(1)}, bf16[1,128,256]{2,1,0:T(8,128)(2,1)S(1)}, u32[]{:S(2)}, u32[]{:S(2)}) collective-permute-start(bf16[1,128,256]{2,1,0:T(8,128)(2,1)S(1)} %copy-done.6), channel_id=1, source_target_pairs={{0,64},{16,80},{32,96},{48,112},{64,0},{80,16},{96,32},{112,48},{1... | collective-permute-start | bytes 196616 | tf_op jit(solution)/shard_map/ppermute | solution.py:552
  51.1 6.7 %all-to-all-done.1.recv = f32[32,32,128]{2,1,0:T(8,128)S(1)} async-done(((f32[32,32,128]{2,1,0:T(8,128)}), f32[32,32,128]{2,1,0:T(8,128)S(1)}, u32[]{:S(2)}, u32[]{:S(2)}) %all-to-all-start.1) | async-done | bytes 524320 | tf_op jit(solution)/shard_map/all_to_all | solution.py:548
  57.9 0.7 shard_map.204
  58.6 4.0 %all-to-all-start.2 = ((s16[16,40,128]{2,1,0:T(8,128)(2,1)}), s16[16,40,128]{2,1,0:T(8,128)(2,1)S(1)}, u32[]{:S(2)}, u32[]{:S(2)}) async-start(s16[16,40,128]{2,1,0:T(8,128)(2,1)} %get-tuple-element.29), calls=%async_computation.2 | async-start | bytes 327680 | tf_op jit(solution)/shard_map/all_to_all | solution.py:548
  62.7 2.8 %collective-permute-start.5 = (bf16[4,128,256]{2,1,0:T(8,128)(2,1)S(1)}, bf16[4,128,256]{2,1,0:T(8,128)(2,1)S(1)}, u32[]{:S(2)}, u32[]{:S(2)}) collective-permute-start(bf16[4,128,256]{2,1,0:T(8,128)(2,1)S(1)} %constant_dynamic-update-slice_fusion), channel_id=1, source_target_pairs={{0,384},{16,400},{32,416},{48,432},{64,448},{80,464},{96,480},{112... | collective-permute-start | bytes 786440 | tf_op jit(solution)/shard_map/ppermute | solution.py:552
  65.5 3.0 %collective-permute-start.4 = (bf16[4,128,256]{2,1,0:T(8,128)(2,1)S(1)}, bf16[4,128,256]{2,1,0:T(8,128)(2,1)S(1)}, u32[]{:S(2)}, u32[]{:S(2)}) collective-permute-start(bf16[4,128,256]{2,1,0:T(8,128)(2,1)S(1)} %constant_dynamic-update-slice_fusion), channel_id=1, source_target_pairs={{0,256},{16,272},{32,288},{48,304},{64,320},{80,336},{96,352},{112... | collective-permute-start | bytes 786440 | tf_op jit(solution)/shard_map/ppermute | solution.py:552
  68.5 3.2 %collective-permute-start.3 = (bf16[4,128,256]{2,1,0:T(8,128)(2,1)S(1)}, bf16[4,128,256]{2,1,0:T(8,128)(2,1)S(1)}, u32[]{:S(2)}, u32[]{:S(2)}) collective-permute-start(bf16[4,128,256]{2,1,0:T(8,128)(2,1)S(1)} %constant_dynamic-update-slice_fusion), channel_id=1, source_target_pairs={{0,128},{16,144},{32,160},{48,176},{64,192},{80,208},{96,224},{112... | collective-permute-start | bytes 786440 | tf_op jit(solution)/shard_map/ppermute | solution.py:552
  71.8 3.3 %all-to-all-done.2.recv = s16[16,40,128]{2,1,0:T(8,128)(2,1)S(1)} async-done(((s16[16,40,128]{2,1,0:T(8,128)(2,1)}), s16[16,40,128]{2,1,0:T(8,128)(2,1)S(1)}, u32[]{:S(2)}, u32[]{:S(2)}) %all-to-all-start.2) | async-done | bytes 163872 | tf_op jit(solution)/shard_map/all_to_all | solution.py:548
  75.0 1.9 %shard_map.205 = s16[32,72,128]{2,1,0:T(8,128)(2,1)} custom-call(s32[2]{0:T(128)S(1)} %pad_add_fusion.where, s16[16,40,128]{2,1,0:T(8,128)(2,1)S(1)} %all-to-all-done.2.recv, f32[32,128]{1,0:T(8,128)S(1)} %get-tuple-element.30.density, bf16[256,256]{1,0:T(8,128)(2,1)S(1)} %copy-done.4, f32[128,128]{1,0:T(8,128)S(1)} %copy-done.10), custom_call_target="tpu_custom_call" | custom-call | tf_op jit(solution)/shard_map/pallas_call | solution.py:134
  76.9 7.6 %all-to-all-start.3 = ((s16[32,72,128]{2,1,0:T(8,128)(2,1)}), s16[32,72,128]{2,1,0:T(8,128)(2,1)S(1)}, u32[]{:S(2)}, u32[]{:S(2)}) async-start(s16[32,72,128]{2,1,0:T(8,128)(2,1)} %shard_map.205), calls=%async_computation.3 | async-start | bytes 1179648 | tf_op jit(solution)/shard_map/all_to_all | solution.py:548
  84.7 2.3 %collective-permute-start.6 = (bf16[16,128,256]{2,1,0:T(8,128)(2,1)S(1)}, bf16[16,128,256]{2,1,0:T(8,128)(2,1)S(1)}, u32[]{:S(2)}, u32[]{:S(2)}) collective-permute-start(bf16[16,128,256]{2,1,0:T(8,128)(2,1)S(1)} %constant_dynamic-update-slice_fusion.4.low), channel_id=1, source_target_pairs={{0,16},{16,0},{32,48},{48,32},{64,80},{80,64},{96,112},{112,96},{1... | collective-permute-start | bytes 3145736 | tf_op jit(solution)/shard_map/ppermute | solution.py:552
  87.0 0.9 copy.27
  87.9 8.9 %all-to-all-done.3.recv = s16[32,72,128]{2,1,0:T(8,128)(2,1)S(1)} async-done(((s16[32,72,128]{2,1,0:T(8,128)(2,1)}), s16[32,72,128]{2,1,0:T(8,128)(2,1)S(1)}, u32[]{:S(2)}, u32[]{:S(2)}) %all-to-all-start.3) | async-done | bytes 589856 | tf_op jit(solution)/shard_map/all_to_all | solution.py:548
  96.8 0.8 copy-done.11
  97.7 5.3 %shard_map.206 = f32[16,16,128]{2,1,0:T(8,128)} custom-call(s16[32,72,128]{2,1,0:T(8,128)(2,1)} %copy-done.11, s32[1,2048]{1,0:T(1,128)} %bitcast.30, bf16[256,256]{1,0:T(8,128)(2,1)} %constant.93.clone.modes_hbm, bf16[256,256]{1,0:T(8,128)(2,1)} %constant.94.clone.modes_t_hbm, f32[8,128,128]{2,1,0:T(8,128)} %bitcast.31, bf16[2,8,128,128]{3,2,1,0:T(8,128)(2,1)} %copy-done, ...), custom_call_target="tpu_custom_call" | custom-call | tf_op jit(solution)/shard_map/pallas_call | solution.py:134
  102.9 6.4 %all-to-all-start.4 = ((f32[16,16,128]{2,1,0:T(8,128)}), f32[16,16,128]{2,1,0:T(8,128)S(1)}, u32[]{:S(2)}, u32[]{:S(2)}) async-start(f32[16,16,128]{2,1,0:T(8,128)} %shard_map.206), calls=%async_computation.4 | async-start | bytes 262144 | tf_op jit(solution)/shard_map/all_to_all | solution.py:548
  110.7 2.9 %shard_map.207.fixed = f32[8,128]{1,0:T(8,128)S(1)} custom-call(s32[2]{0:T(128)S(1)} %pad_add_fusion.where, bf16[16,128,256]{2,1,0:T(8,128)(2,1)S(1)} %constant_dynamic-update-slice_fusion.4.low, bf16[16,128,256]{2,1,0:T(8,128)(2,1)S(1)} %collective-permute-done.6.high, f32[128,256]{1,0:T(8,128)S(1)} %bitcast.21, f32[128,256]{1,0:T(8,128)S(1)} %bitcast.25, ...), custom_call_target="tpu_custom_call" | custom-call | tf_op jit(solution)/shard_map/pallas_call | solution.py:134
  113.7 7.7 %all-to-all-done.4.recv = f32[16,16,128]{2,1,0:T(8,128)S(1)} async-done(((f32[16,16,128]{2,1,0:T(8,128)}), f32[16,16,128]{2,1,0:T(8,128)S(1)}, u32[]{:S(2)}, u32[]{:S(2)}) %all-to-all-start.4) | async-done | bytes 131104 | tf_op jit(solution)/shard_map/all_to_all | solution.py:548
  121.3 2.8 %shard_map.208 = (f32[128,256]{1,0:T(8,128)S(1)}, f32[16,1,384]{2,1,0:T(1,128)S(1)}) custom-call(f32[16,16,128]{2,1,0:T(8,128)S(1)} %all-to-all-done.4.recv, bf16[2,256,256]{2,1,0:T(8,128)(2,1)S(1)} %copy-done.3, s32[2]{0:T(128)S(1)} %pad_add_fusion.where, f32[2]{0:T(128)S(1)} %pad_maximum_fusion.scalars, f32[128,256]{1,0:T(8,128)S(1)} %bitcast.22, ...), custom_call_target="tpu_custom_call" | custom-call | tf_op jit(solution)/shard_map/pallas_call | solution.py:134
  124.1 17.6 %all_to_all.35.recv = f32[16,1,384]{2,1,0:T(1,128)S(1)} all-to-all(f32[16,1,384]{2,1,0:T(1,128)S(1)} %get-tuple-element.39), channel_id=1, replica_groups=mesh['band'=32,'slab'=16] {'slab'}, dimensions={0} | all-to-all | bytes 49152 | tf_op jit(solution)/shard_map/all_to_all | solution.py:548
  141.7 1.0 shard_map.209
  142.7 5.9 %all-to-all-start.6 = ((f32[32,1,256]{2,1,0:T(1,128)}), f32[32,1,256]{2,1,0:T(1,128)S(1)}, u32[]{:S(2)}, u32[]{:S(2)}) async-start(f32[32,1,256]{2,1,0:T(1,128)} %get-tuple-element.40), calls=%async_computation.6 | async-start | bytes 65536 | tf_op jit(solution)/shard_map/all_to_all | solution.py:548
  149.3 2.2 %shard_map.210.rest = f32[128,256]{1,0:T(8,128)S(1)} custom-call(f32[1,128]{1,0:T(1,128)S(1)} %get-tuple-element.41.margin, s32[2]{0:T(128)S(1)} %pad_add_fusion.where, f32[2]{0:T(128)S(1)} %pad_maximum_fusion.scalars, f32[128,256]{1,0:T(8,128)S(1)} %bitcast.23, f32[128,256]{1,0:T(8,128)S(1)} %bitcast.27, f32[128,256]{1,0:T(8,128)S(1)} %get-tuple-element.42.applied, ...), custom_call_target="tpu_custom_call" | custom-call | tf_op jit(solution)/shard_map/pallas_call | solution.py:134
  151.5 4.3 %all-to-all-done.6.recv = f32[32,1,256]{2,1,0:T(1,128)S(1)} async-done(((f32[32,1,256]{2,1,0:T(1,128)}), f32[32,1,256]{2,1,0:T(1,128)S(1)}, u32[]{:S(2)}, u32[]{:S(2)}) %all-to-all-start.6) | async-done | bytes 32800 | tf_op jit(solution)/shard_map/all_to_all | solution.py:548
  155.9 1.3 shard_map.211
  (50 shorter events, 1.1 us)
Async XLA Ops:
  0.6 24.5 %copy-start.12 = (bf16[1,2,8,16384]{3,2,1,0:T(8,128)(2,1)S(1)}, bf16[1,2,8,16384]{3,2,1,0:T(8,128)(2,1)}, u32[]{:S(2)}) copy-start(bf16[1,2,8,16384]{3,2,1,0:T(8,128)(2,1)} %param.24) | copy-start | bytes 1572868
  2.8 15.9 %copy-start.14 = (s32[2048]{0:T(1024)S(1)}, s32[2048]{0:T(1024)}, u32[]{:S(2)}) copy-start(s32[2048]{0:T(1024)} %param.26) | copy-start | bytes 24580
  2.8 16.0 %copy-start.6 = (bf16[1,128,256]{2,1,0:T(8,128)(2,1)S(1)}, bf16[1,128,256]{2,1,0:T(8,128)(2,1)}, u32[]{:S(2)}) copy-start(bf16[1,128,256]{2,1,0:T(8,128)(2,1)} %param.23) | copy-start | bytes 196612
  2.8 27.9 %all-to-all-start = ((f32[16,16,128]{2,1,0:T(8,128)}), f32[16,16,128]{2,1,0:T(8,128)S(1)}, u32[]{:S(2)}, u32[]{:S(2)}) async-start(f32[16,16,128]{2,1,0:T(8,128)} %shard_map.202), calls=%async_computation | async-start | bytes 262144 | tf_op jit(solution)/shard_map/all_to_all | solution.py:548
  18.7 12.0 %copy-start.9 = (s32[2048]{0:T(1024)}, s32[2048]{0:T(1024)S(1)}, u32[]{:S(2)}) copy-start(s32[2048]{0:T(1024)S(1)} %fusion.4) | copy-start | bytes 24580
  18.8 16.8 %collective-permute-start.2 = (bf16[1,128,256]{2,1,0:T(8,128)(2,1)S(1)}, bf16[1,128,256]{2,1,0:T(8,128)(2,1)S(1)}, u32[]{:S(2)}, u32[]{:S(2)}) collective-permute-start(bf16[1,128,256]{2,1,0:T(8,128)(2,1)S(1)} %copy-done.6), channel_id=1, source_target_pairs={{0,96},{16,112},{32,64},{48,80},{64,32},{80,48},{96,0},{112,16},{1... | collective-permute-start | bytes 196616 | tf_op jit(solution)/shard_map/ppermute | solution.py:552
  23.2 12.4 %collective-permute-start.1 = (bf16[1,128,256]{2,1,0:T(8,128)(2,1)S(1)}, bf16[1,128,256]{2,1,0:T(8,128)(2,1)S(1)}, u32[]{:S(2)}, u32[]{:S(2)}) collective-permute-start(bf16[1,128,256]{2,1,0:T(8,128)(2,1)S(1)} %copy-done.6), channel_id=1, source_target_pairs={{0,32},{16,48},{32,0},{48,16},{64,96},{80,112},{96,64},{112,80},{1... | collective-permute-start | bytes 196616 | tf_op jit(solution)/shard_map/ppermute | solution.py:552
  25.1 5.6 %copy-start.4 = (bf16[256,256]{1,0:T(8,128)(2,1)S(1)}, bf16[256,256]{1,0:T(8,128)(2,1)}, u32[]{:S(2)}) copy-start(bf16[256,256]{1,0:T(8,128)(2,1)} %constant.92.clone.modes_hbm.modes) | copy-start | bytes 393220
  25.1 5.6 %copy-start.5 = (bf16[512,256]{1,0:T(8,128)(2,1)S(1)}, bf16[512,256]{1,0:T(8,128)(2,1)}, u32[]{:S(2)}) copy-start(bf16[512,256]{1,0:T(8,128)(2,1)} %constant.90.clone.x_hbm) | copy-start | bytes 786436
  25.1 5.6 %copy-start.7 = (bf16[256,256]{1,0:T(8,128)(2,1)S(1)}, bf16[256,256]{1,0:T(8,128)(2,1)}, u32[]{:S(2)}) copy-start(bf16[256,256]{1,0:T(8,128)(2,1)} %constant.95.clone.modes_t_hbm) | copy-start | bytes 393220
  25.1 5.6 %copy-start.8 = (bf16[256,256]{1,0:T(8,128)(2,1)S(1)}, bf16[256,256]{1,0:T(8,128)(2,1)}, u32[]{:S(2)}) copy-start(bf16[256,256]{1,0:T(8,128)(2,1)} %constant.88.clone.y_hbm) | copy-start | bytes 393220
  25.2 10.3 %copy-start = (bf16[2,8,128,128]{3,2,1,0:T(8,128)(2,1)}, bf16[2,8,128,128]{3,2,1,0:T(8,128)(2,1)S(1)}, u32[]{:S(2)}) copy-start(bf16[2,8,128,128]{3,2,1,0:T(8,128)(2,1)S(1)} %copy.28) | copy-start | bytes 1572868
  35.6 22.3 %all-to-all-start.1 = ((f32[32,32,128]{2,1,0:T(8,128)}), f32[32,32,128]{2,1,0:T(8,128)S(1)}, u32[]{:S(2)}, u32[]{:S(2)}) async-start(f32[32,32,128]{2,1,0:T(8,128)} %bitcast.4), calls=%async_computation.1 | async-start | bytes 1048576 | tf_op jit(solution)/shard_map/all_to_all | solution.py:548
  46.3 12.3 %collective-permute-start = (bf16[1,128,256]{2,1,0:T(8,128)(2,1)S(1)}, bf16[1,128,256]{2,1,0:T(8,128)(2,1)S(1)}, u32[]{:S(2)}, u32[]{:S(2)}) collective-permute-start(bf16[1,128,256]{2,1,0:T(8,128)(2,1)S(1)} %copy-done.6), channel_id=1, source_target_pairs={{0,64},{16,80},{32,96},{48,112},{64,0},{80,16},{96,32},{112,48},{1... | collective-permute-start | bytes 196616 | tf_op jit(solution)/shard_map/ppermute | solution.py:552
  58.6 16.4 %all-to-all-start.2 = ((s16[16,40,128]{2,1,0:T(8,128)(2,1)}), s16[16,40,128]{2,1,0:T(8,128)(2,1)S(1)}, u32[]{:S(2)}, u32[]{:S(2)}) async-start(s16[16,40,128]{2,1,0:T(8,128)(2,1)} %get-tuple-element.29), calls=%async_computation.2 | async-start | bytes 327680 | tf_op jit(solution)/shard_map/all_to_all | solution.py:548
  62.6 12.4 %copy-start.10 = (f32[128,128]{1,0:T(8,128)S(1)}, f32[128,128]{1,0:T(8,128)}, u32[]{:S(2)}) copy-start(f32[128,128]{1,0:T(8,128)} %constant.96.clone.modes_t32) | copy-start | bytes 196612
  62.7 21.9 %collective-permute-start.5 = (bf16[4,128,256]{2,1,0:T(8,128)(2,1)S(1)}, bf16[4,128,256]{2,1,0:T(8,128)(2,1)S(1)}, u32[]{:S(2)}, u32[]{:S(2)}) collective-permute-start(bf16[4,128,256]{2,1,0:T(8,128)(2,1)S(1)} %constant_dynamic-update-slice_fusion), channel_id=1, source_target_pairs={{0,384},{16,400},{32,416},{48,432},{64,448},{80,464},{96,480},{112... | collective-permute-start | bytes 786440 | tf_op jit(solution)/shard_map/ppermute | solution.py:552
  65.5 19.0 %collective-permute-start.4 = (bf16[4,128,256]{2,1,0:T(8,128)(2,1)S(1)}, bf16[4,128,256]{2,1,0:T(8,128)(2,1)S(1)}, u32[]{:S(2)}, u32[]{:S(2)}) collective-permute-start(bf16[4,128,256]{2,1,0:T(8,128)(2,1)S(1)} %constant_dynamic-update-slice_fusion), channel_id=1, source_target_pairs={{0,256},{16,272},{32,288},{48,304},{64,320},{80,336},{96,352},{112... | collective-permute-start | bytes 786440 | tf_op jit(solution)/shard_map/ppermute | solution.py:552
  68.5 16.0 %collective-permute-start.3 = (bf16[4,128,256]{2,1,0:T(8,128)(2,1)S(1)}, bf16[4,128,256]{2,1,0:T(8,128)(2,1)S(1)}, u32[]{:S(2)}, u32[]{:S(2)}) collective-permute-start(bf16[4,128,256]{2,1,0:T(8,128)(2,1)S(1)} %constant_dynamic-update-slice_fusion), channel_id=1, source_target_pairs={{0,128},{16,144},{32,160},{48,176},{64,192},{80,208},{96,224},{112... | collective-permute-start | bytes 786440 | tf_op jit(solution)/shard_map/ppermute | solution.py:552
  76.9 20.0 %all-to-all-start.3 = ((s16[32,72,128]{2,1,0:T(8,128)(2,1)}), s16[32,72,128]{2,1,0:T(8,128)(2,1)S(1)}, u32[]{:S(2)}, u32[]{:S(2)}) async-start(s16[32,72,128]{2,1,0:T(8,128)(2,1)} %shard_map.205), calls=%async_computation.3 | async-start | bytes 1179648 | tf_op jit(solution)/shard_map/all_to_all | solution.py:548
  84.6 2.4 %copy-start.13 = (f32[8,16384]{1,0:T(8,128)S(1)}, f32[8,16384]{1,0:T(8,128)}, u32[]{:S(2)}) copy-start(f32[8,16384]{1,0:T(8,128)} %param.25) | copy-start | bytes 1572868
  84.7 26.0 %collective-permute-start.6 = (bf16[16,128,256]{2,1,0:T(8,128)(2,1)S(1)}, bf16[16,128,256]{2,1,0:T(8,128)(2,1)S(1)}, u32[]{:S(2)}, u32[]{:S(2)}) collective-permute-start(bf16[16,128,256]{2,1,0:T(8,128)(2,1)S(1)} %constant_dynamic-update-slice_fusion.4.low), channel_id=1, source_target_pairs={{0,16},{16,0},{32,48},{48,32},{64,80},{80,64},{96,112},{112,96},{1... | collective-permute-start | bytes 3145736 | tf_op jit(solution)/shard_map/ppermute | solution.py:552
  96.8 0.8 copy-start.11
  102.9 7.8 %copy-start.1 = (f32[1,128,256]{2,1,0:T(8,128)S(1)}, f32[1,128,256]{2,1,0:T(8,128)}, u32[]{:S(2)}) copy-start(f32[1,128,256]{2,1,0:T(8,128)} %param.19) | copy-start | bytes 393220
  102.9 7.8 %copy-start.2 = (f32[1,128,256]{2,1,0:T(8,128)S(1)}, f32[1,128,256]{2,1,0:T(8,128)}, u32[]{:S(2)}) copy-start(f32[1,128,256]{2,1,0:T(8,128)} %param.20) | copy-start | bytes 393220
  102.9 18.4 %all-to-all-start.4 = ((f32[16,16,128]{2,1,0:T(8,128)}), f32[16,16,128]{2,1,0:T(8,128)S(1)}, u32[]{:S(2)}, u32[]{:S(2)}) async-start(f32[16,16,128]{2,1,0:T(8,128)} %shard_map.206), calls=%async_computation.4 | async-start | bytes 262144 | tf_op jit(solution)/shard_map/all_to_all | solution.py:548
  110.7 10.6 %copy-start.3 = (bf16[2,256,256]{2,1,0:T(8,128)(2,1)S(1)}, bf16[2,256,256]{2,1,0:T(8,128)(2,1)}, u32[]{:S(2)}) copy-start(bf16[2,256,256]{2,1,0:T(8,128)(2,1)} %constant.87.clone.table_hbm.table) | copy-start | bytes 786436
  142.7 13.1 %all-to-all-start.6 = ((f32[32,1,256]{2,1,0:T(1,128)}), f32[32,1,256]{2,1,0:T(1,128)S(1)}, u32[]{:S(2)}, u32[]{:S(2)}) async-start(f32[32,1,256]{2,1,0:T(1,128)} %get-tuple-element.40), calls=%async_computation.6 | async-start | bytes 65536 | tf_op jit(solution)/shard_map/all_to_all | solution.py:548
